TPU v7x, 128 devices: a whole 4x4x4 slice. The times are simulated.
128 devices in a mesh: dp: 8 (over z, core), enc: 16 (over x, y).
Axes of the slice: x: 4, y: 4, z: 4, core: 2. Of those that a mesh axis runs over, the one named last changes fastest.
Arguments:
- queries_in: bfloat16 [4096, 4096], P('dp'), may hold values from -6 to 6
- w_query: bfloat16 [4096, 4096], P(None, 'enc'), may hold values from -0.09375 to 0.09375
- w_key: bfloat16 [896, 4096], P(None, 'enc'), may hold values from -0.1875 to 0.1875
- w_value: bfloat16 [896, 4096], P(None, 'enc'), may hold values from -0.1875 to 0.1875
- tiles: bfloat16 [512, 128, 896], P(('dp', 'enc')), may hold values from -6 to 6
- neighbour_owner: int32 [64, 2], P('dp'), may hold values from 0 to 15, all different within a row; in each aligned block of 8 rows (0 to 7, 8 to 15, ...) at most 2 rows name the same one
- neighbour_slot: int32 [64, 2], P('dp'), may hold values from 0 to 3
- key_length: int32 [64, 2], P('dp'), may hold values from 64 to 128
- grad_context: bfloat16 [4096, 4096], P('dp', 'enc'), may hold values from -6 to 6
Outputs:
- context: bfloat16 [4096, 4096], P('dp', 'enc')
- grad_wq: float32 [4096, 4096], P(None, 'enc')
- grad_wk: float32 [896, 4096], P(None, 'enc')
- grad_wv: float32 [896, 4096], P(None, 'enc')
- grad_tiles: float32 [512, 128, 896], P(('dp', 'enc'))
Inputs may be any that keep to these rules, and one draw needn't show every extreme that they name: `neighbour_owner`: within each block of 8 spans (one dp group), no owner is named by more than 2 neighbours, and the 2 owners of one span differ.
All inputs are finite; a program needn't handle non-finite values.
Results may differ from a plain program's by a relative error of at most 0.02.
Values may be sent and summed in bfloat16 or wider, within the bound.
No kernel may reach another device: no remote copies, remote signals or barrier semaphores. Data moves between devices by JAX's collectives and lax.ppermute only.
A program may use at most 128 MiB of HBM per device.

v0:
```python
import jax
import jax.numpy as jnp
from jax import lax
from jax.sharding import PartitionSpec as P

HD = 128
SPAN = 64


def body(
    queries_in,
    w_query,
    w_key,
    w_value,
    tiles,
    neighbour_owner,
    neighbour_slot,
    key_length,
    grad_context,
):
    owners_count = lax.axis_size("enc")
    own_index = lax.axis_index("enc")
    spans = neighbour_owner.shape[0]
    per_span = neighbour_owner.shape[1]
    tile_count = tiles.shape[0]
    tile_tokens = tiles.shape[1]
    enc_width = tiles.shape[2]
    head_columns = w_query.shape[1]
    head_count = head_columns // HD
    capacity = max(2, 2 * per_span * spans // owners_count)
    score_scale = 1.0 / HD**0.5
    owner_flat = neighbour_owner.reshape(-1)
    slot_flat = neighbour_slot.reshape(-1)
    owner_hit = (owner_flat[:, None] == jnp.arange(owners_count, dtype=jnp.int32)[None, :]).astype(
        jnp.int32
    )
    earlier = jnp.cumsum(owner_hit, axis=0) - owner_hit
    position_rank = jnp.sum(earlier * owner_hit, axis=1)
    buffer_place = owner_flat * capacity + position_rank
    is_mine = owner_flat == own_index
    matches = (
        is_mine[:, None]
        & (position_rank[:, None] == jnp.arange(capacity, dtype=jnp.int32)[None, :])
    ).astype(jnp.int32)
    own_slot = jnp.sum(matches * slot_flat[:, None], axis=0)
    query = jnp.dot(queries_in, w_query, preferred_element_type=jnp.float32).astype(jnp.bfloat16)
    all_owned = lax.all_gather(tiles, "enc", axis=0, tiled=True)
    neighbours = all_owned[owner_flat * tile_count + slot_flat]
    neighbours = neighbours.reshape(-1, enc_width)
    key_rows = jnp.dot(neighbours, w_key, preferred_element_type=jnp.float32).astype(jnp.bfloat16)
    value_rows = jnp.dot(neighbours, w_value, preferred_element_type=jnp.float32).astype(
        jnp.bfloat16
    )
    query_heads = query.reshape(spans, SPAN, head_count, HD)
    key_heads = key_rows.reshape(spans, per_span * tile_tokens, head_count, HD)
    value_heads = value_rows.reshape(spans, per_span * tile_tokens, head_count, HD)
    score = (
        jnp.einsum("ctha,cnha->chtn", query_heads, key_heads, preferred_element_type=jnp.float32)
        * score_scale
    )
    position = jnp.arange(per_span * tile_tokens, dtype=jnp.int32) % tile_tokens
    lengths = jnp.repeat(key_length, tile_tokens, axis=1)
    visible = (position[None, :] < lengths).astype(jnp.float32)
    weights = jnp.exp(score) * visible[:, None, None, :]
    attention = weights / jnp.sum(weights, axis=-1, keepdims=True)
    attention_b = attention.astype(jnp.bfloat16)
    context = jnp.einsum(
        "chtn,cnha->ctha", attention_b, value_heads, preferred_element_type=jnp.float32
    )
    context = context.reshape(spans * SPAN, head_columns).astype(jnp.bfloat16)
    upstream = grad_context.reshape(spans, SPAN, head_count, HD)
    dprobs = jnp.einsum(
        "ctha,cnha->chtn", upstream, value_heads, preferred_element_type=jnp.float32
    )
    dscore = (
        attention * (dprobs - jnp.sum(attention * dprobs, axis=-1, keepdims=True)) * score_scale
    ).astype(jnp.bfloat16)
    query_grad = jnp.einsum(
        "chtn,cnha->ctha", dscore, key_heads, preferred_element_type=jnp.float32
    )
    query_grad = query_grad.reshape(spans * SPAN, head_columns).astype(jnp.bfloat16)
    key_grad = jnp.einsum(
        "chtn,ctha->cnha", dscore, query_heads, preferred_element_type=jnp.float32
    )
    key_grad = key_grad.reshape(-1, head_columns).astype(jnp.bfloat16)
    value_grad = jnp.einsum(
        "chtn,ctha->cnha", attention_b, upstream, preferred_element_type=jnp.float32
    )
    value_grad = value_grad.reshape(-1, head_columns).astype(jnp.bfloat16)
    partial_value = jnp.dot(key_grad, w_key.T, preferred_element_type=jnp.float32)
    partial_value = partial_value + jnp.dot(
        value_grad, w_value.T, preferred_element_type=jnp.float32
    )
    outbound = (
        jnp.zeros((owners_count * capacity, tile_tokens, enc_width), jnp.float32)
        .at[buffer_place]
        .set(partial_value.reshape(-1, tile_tokens, enc_width))
    )
    received = lax.psum_scatter(
        outbound.astype(jnp.bfloat16), "enc", scatter_dimension=0, tiled=True
    ).astype(jnp.float32)
    grad_tiles = (
        jnp.zeros((tile_count, tile_tokens, enc_width), jnp.float32).at[own_slot].add(received)
    )
    local_wq = jnp.dot(queries_in.T, query_grad, preferred_element_type=jnp.float32)
    local_wk = jnp.dot(neighbours.T, key_grad, preferred_element_type=jnp.float32)
    local_wv = jnp.dot(neighbours.T, value_grad, preferred_element_type=jnp.float32)
    summed = (
        lax.psum(local_wq.astype(jnp.bfloat16), "dp").astype(jnp.float32),
        lax.psum(local_wk.astype(jnp.bfloat16), "dp").astype(jnp.float32),
        lax.psum(local_wv.astype(jnp.bfloat16), "dp").astype(jnp.float32),
    )
    return (context, summed[0], summed[1], summed[2], grad_tiles)


def solution(mesh):
    in_specs = (
        P("dp", None),
        P(None, "enc"),
        P(None, "enc"),
        P(None, "enc"),
        P(("dp", "enc"), None, None),
        P("dp", None),
        P("dp", None),
        P("dp", None),
        P("dp", "enc"),
    )
    out_specs = (
        P("dp", "enc"),
        P(None, "enc"),
        P(None, "enc"),
        P(None, "enc"),
        P(("dp", "enc"), None, None),
    )
    return jax.shard_map(body, mesh=mesh, in_specs=in_specs, out_specs=out_specs, check_vma=False)
```

profile of v0, /device:TPU:0, one launch (start us, length us, event | category | flops | bytes accessed | tf_op | source)
XLA Modules:
  0.0 322.9 jit_solution(5274519920163399892)
XLA Ops:
  9.7 1.0 reshape.159
  10.7 3.5 %convolution_convert_fusion.9 = bf16[512,256]{1,0:T(8,128)(2,1)S(1)} fusion(bf16[512,4096]{1,0:T(8,128)(2,1)} %param.9, bf16[4096,256]{1,0:T(8,128)(2,1)S(1)} %copy-done), kind=kOutput, calls=%fused_computation.25 | convolution fusion | flops 1073872896 | bytes 6553600 | tf_op jit(solution)/shard_map/dot_general | solution.py:46
  14.5 98.7 %all-gather.2.cloned.1.call-done = bf16[64,128,896]{2,1,0:T(8,128)(2,1)} async-done(((bf16[4,128,896]{2,1,0:T(8,128)(2,1)}), bf16[64,128,896]{2,1,0:T(8,128)(2,1)}) %all-gather.2.cloned.1.call-update) | async-done | bytes 14680080 | tf_op jit(solution)/shard_map/all_gather | solution.py:47
  113.2 8.0 %gather_fusion = bf16[16,128,896]{2,1,0:T(8,128)(2,1)} fusion(bf16[64,128,896]{2,1,0:T(8,128)(2,1)} %all-gather.2.cloned.1.call-done, s32[1024]{0:T(1024)S(1)} %pad_clamp_fusion), kind=kCustom, calls=%fused_computation | custom fusion | bytes 7340096 | tf_op jit(solution)/shard_map/gather | solution.py:48
  121.2 3.3 %convolution_convert_fusion.1 = bf16[2048,256]{1,0:T(8,128)(2,1)S(1)} fusion(bf16[2048,896]{1,0:T(8,128)(2,1)} %bitcast.76, bf16[896,256]{1,0:T(8,128)(2,1)S(1)} %copy-done.7), kind=kOutput, calls=%fused_computation.7 | convolution fusion | flops 940048384 | bytes 5177344 | tf_op jit(solution)/shard_map/dot_general | solution.py:50
  125.4 1.4 fusion.21
  126.8 1.6 fusion.3
  128.4 3.4 %convolution_convert_fusion.2 = bf16[2048,256]{1,0:T(8,128)(2,1)S(1)} fusion(bf16[2048,896]{1,0:T(8,128)(2,1)} %bitcast.77, bf16[896,256]{1,0:T(8,128)(2,1)} %param.12), kind=kOutput, calls=%fused_computation.8 | convolution fusion | flops 940048384 | bytes 5177344 | tf_op jit(solution)/shard_map/dot_general | solution.py:51
  132.1 1.4 convolution_bitcast_fusion
  133.6 1.0 copy-done.4
  134.5 2.8 fusion.11
  137.3 2.9 fusion.2
  140.2 2.7 copy.73
  142.9 1.5 copy.81
  144.4 4.0 %convolution_convert_fusion.5 = bf16[896,256]{1,0:T(8,128)(2,1)} fusion(bf16[2048,896]{1,0:T(8,128)(2,1)} %bitcast.78, bf16[2048,256]{0,1:T(8,128)(2,1)S(1)} %bitcast.72), kind=kOutput, calls=%fused_computation.21 | convolution fusion | flops 939753472 | bytes 5177344 | tf_op jit(solution)/shard_map/dot_general | solution.py:107
  149.3 1.1 copy-done.3
  150.4 2.0 convolution_convert_fusion.6
  152.9 2.6 fusion.1
  156.3 2.4 fusion.44
  158.7 4.3 %convolution_add_fusion = f32[2048,896]{1,0:T(8,128)} fusion(f32[2048,896]{1,0:T(8,128)S(1)} %fusion.44, bf16[2048,256]{0,1:T(8,128)(2,1)S(1)} %bitcast.73, bf16[896,256]{1,0:T(8,128)(2,1)S(1)} %copy-done.8), kind=kOutput, calls=%fused_computation.6 | convolution fusion | flops 941359104 | bytes 16187392 | tf_op jit(solution)/shard_map/dot_general | solution.py:91
  162.9 6.9 %broadcast_in_dim.8 = f32[32,128,896]{2,1,0:T(8,128)} broadcast(f32[]{:T(128)} %constant.39.clone.1), dimensions={} | broadcast | bytes 14680068 | tf_op jit(solution)/shard_map/broadcast_in_dim | solution.py:95
  169.9 14.5 %scatter_fusion = f32[32,128,896]{2,1,0:T(8,128)} fusion(f32[32,128,896]{2,1,0:T(8,128)} %broadcast_in_dim.8, s32[16]{0:T(128)S(1)} %fusion.37, f32[16,128,896]{2,1,0:T(8,128)} %bitcast.69), kind=kCustom, calls=%fused_computation.1 | custom fusion | bytes 22020160 | tf_op jit(solution)/shard_map/scatter | solution.py:97
  184.3 9.4 %convert_element_type.119 = bf16[32,128,896]{2,1,0:T(8,128)(2,1)} convert(f32[32,128,896]{2,1,0:T(8,128)} %scatter_fusion) | non-fusion elementwise | flops 3670016 | bytes 22020096 | tf_op jit(solution)/shard_map/convert_element_type | solution.py:100
  194.8 2.0 fusion.10
  197.7 26.8 %all-reduce.3.cloned.1.call-done = (bf16[4096,256]{0,1:T(8,128)(2,1)}, bf16[896,256]{1,0:T(8,128)(2,1)}, bf16[896,256]{1,0:T(8,128)(2,1)}) async-done(((bf16[4096,256]{0,1:T(8,128)(2,1)}, bf16[896,256]{1,0:T(8,128)(2,1)}, bf16[896,256]{1,0:T(8,128)(2,1)}), (bf16[4096,256]{0,1:T(8,128)(2,1)}, bf16[896,256]{1,0:T(8,128)(2,1)}, bf16[896,256]{1,0:T(8,128)(2,1)})) %all-reduce.3.cloned.1.call-update) | async-done | bytes 3014672 | tf_op jit(solution)/shard_map/psum | solution.py:109
  224.5 2.0 convert_element_type.112
  226.5 2.0 convert_element_type.117
  228.5 4.4 %copy.77 = f32[4096,256]{1,0:T(8,128)} copy(bf16[4096,256]{0,1:T(8,128)(2,1)} %get-tuple-element.25) | data formatting | bytes 6291456
  233.0 78.2 %reduce-scatter.2.cloned.1.call-done = bf16[2,128,896]{2,1,0:T(8,128)(2,1)} async-done(((bf16[32,128,896]{2,1,0:T(8,128)(2,1)}), bf16[2,128,896]{2,1,0:T(8,128)(2,1)}) %reduce-scatter.2.cloned.1.call-update) | async-done | bytes 458768 | tf_op jit(solution)/shard_map/reduce_scatter | solution.py:99
  311.1 1.1 convert_element_type.120
  312.2 1.4 broadcast_in_dim.7
  313.6 2.8 scatter_fusion.1
  (57 shorter events, 8.0 us)
Async XLA Ops:
  7.2 3.5 %copy-start = (bf16[4096,256]{1,0:T(8,128)(2,1)S(1)}, bf16[4096,256]{1,0:T(8,128)(2,1)}, u32[]{:S(2)}) copy-start(bf16[4096,256]{1,0:T(8,128)(2,1)} %param.10) | copy-start | bytes 6291460
  7.2 106.0 %all-gather.2.cloned.1.call-start = ((), (), s32[]{:S(2)}) async-start(), calls=%async_computation.1 | async-start | bytes 15597568 | tf_op jit(solution)/shard_map/all_gather | solution.py:47
  7.9 216.6 %all-reduce.3.cloned.1.call-start = ((), (), s32[]{:S(2)}) async-start(), calls=%async_computation.3 | async-start | bytes 6029312 | tf_op jit(solution)/shard_map/psum | solution.py:109
  10.7 116.1 %copy-start.5 = (bf16[8,64,2,128]{3,2,1,0:T(2,128)(2,1)}, bf16[8,64,2,128]{3,2,1,0:T(2,128)(2,1)S(1)}, u32[]{:S(2)}) copy-start(bf16[8,64,2,128]{3,2,1,0:T(2,128)(2,1)S(1)} %reshape.159) | copy-start | bytes 786436
  10.7 3.7 %copy-start.11 = (s32[8,2]{0,1:T(2,128)S(1)}, s32[8,2]{0,1:T(2,128)}, u32[]{:S(2)}) copy-start(s32[8,2]{0,1:T(2,128)} %param.16) | copy-start | bytes 196
  14.4 106.7 %copy-start.7 = (bf16[896,256]{1,0:T(8,128)(2,1)S(1)}, bf16[896,256]{1,0:T(8,128)(2,1)}, u32[]{:S(2)}) copy-start(bf16[896,256]{1,0:T(8,128)(2,1)} %param.11) | copy-start | bytes 1376260
  125.4 3.0 copy-start.6
  133.5 1.0 copy-start.4
  148.4 2.0 copy-start.3
  150.4 2.0 copy-start.9
  150.4 2.4 copy-start.2
  155.5 155.6 %reduce-scatter.2.cloned.1.call-start = ((), (), s32[]{:S(2)}) async-start(), calls=%async_computation.2 | async-start | bytes 7798784 | tf_op jit(solution)/shard_map/reduce_scatter | solution.py:99
  156.3 2.4 copy-start.8
  193.8 0.7 copy-start.10
  228.5 87.8 %copy-start.1 = (bf16[4096,256]{1,0:T(8,128)(2,1)S(1)}, bf16[4096,256]{1,0:T(8,128)(2,1)}, u32[]{:S(2)}) copy-start(bf16[4096,256]{1,0:T(8,128)(2,1)} %param.10) | copy-start | bytes 6291460
Sparse Core Ops, SparseCore 0:
  10.2 102.9 all-gather.1
  155.7 68.8 all-reduce.2
  228.4 82.7 reduce-scatter.1
where the time goes:
time: 324 us; the launch traced here: 323 us
  waiting for transfers between devices  204 us (63%)
  local copies, waits for them, and re-layouts  47.7 us (15%)
  matrix products  36.6 us (11%)
  other arithmetic  19.9 us (6%)
  between operations  14 us (4%)
    all_gather x1, waiting for transfers between devices, body(): all_owned = lax.all_gather(tiles, 'enc', axis=0, tiled=True)  98.7 us
    reduce_scatter x1, waiting for transfers between devices, body(): lax.psum_scatter(outbound.astype(jnp.bfloat16), 'enc', scatter_dimension=...  78.2 us
    psum x1, waiting for transfers between devices, body(): lax.psum(local_wq.astype(jnp.bfloat16), 'dp').astype(jnp.float32)  26.8 us
    scatter x1, local copies, waits for them, and re-layouts, body(): outbound = jnp.zeros((owners_count * capacity, tile_tokens, enc_width), j...  14.5 us
    unnamed x30, local copies, waits for them, and re-layouts  10.9 us
    convert_element_type x1, other arithmetic, body(): outbound.astype(jnp.bfloat16)  9.44 us
    gather x1, local copies, waits for them, and re-layouts, body(): neighbours = all_owned[owner_flat * tile_count + slot_flat]  7.97 us
    broadcast_in_dim x1, local copies, waits for them, and re-layouts, body(): jnp.zeros((owners_count * capacity, tile_tokens, enc_width), jnp.float32)  6.94 us
  transfers between devices with their start and end apart: 3, of which 3 were waited for; matrix products, arithmetic and copies ran while one was open for 17% of the time, Pallas kernels for 0%

commit v1 on v0

v1 whole, which is shorter than its diff:
```python
import jax
import jax.numpy as jnp
from jax import lax
from jax.experimental import pallas as pl
from jax.experimental.pallas import tpu as pltpu
from jax.sharding import PartitionSpec as P

HD = 128
SPAN = 64
SIDE = 4
SUB = 16
NT = 16
VMEM_LIMIT = 48 * 1024 * 1024
F32 = jnp.float32
BF16 = jnp.bfloat16


def along_x(value, step):
    pairs = [(i, ((i // SIDE + step) % SIDE) * SIDE + i % SIDE) for i in range(SIDE * SIDE)]
    return lax.ppermute(value, "enc", pairs)


def along_y(value, step):
    pairs = [(i, (i // SIDE) * SIDE + (i + step) % SIDE) for i in range(SIDE * SIDE)]
    return lax.ppermute(value, "enc", pairs)


def place():
    own = lax.axis_index("enc")
    return own, lax.div(own, SIDE), lax.rem(own, SIDE)


def apart(here, there):
    return lax.rem(here - there + SIDE, SIDE)


def my_slots(owner, slot, own):
    count = jnp.int32(0)
    first = jnp.int32(0)
    second = jnp.int32(0)
    for t in range(NT):
        hit = owner[t // 2, t % 2] == own
        tile = slot[t // 2, t % 2]
        first = jnp.where(hit & (count == 0), tile, first)
        second = jnp.where(hit & (count == 1), tile, second)
        count = count + hit.astype(jnp.int32)
    return first, second


def named(owner, x, y):
    found = []
    for t in range(NT):
        o = owner[t // 2, t % 2]
        rank = jnp.int32(0)
        for e in range(t):
            rank = rank + (owner[e // 2, e % 2] == o).astype(jnp.int32)
        found.append((apart(x, lax.div(o, SIDE)), apart(y, lax.rem(o, SIDE)), rank))
    return found


def sub_row(at, base):
    return pl.ds(pl.multiple_of(base + lax.rem(at, SIDE) * SUB, SUB), SUB)


def split_kernel(owner, slot, tiles, *outs):
    own, x, y = place()
    for r, tile in enumerate(my_slots(owner, slot, own)):
        for k in range(SIDE):
            outs[k][r] = tiles[tile, sub_row(x + k, 0), :]
            outs[SIDE + k][r] = tiles[tile, sub_row(y + k, SIDE * SUB), :]


def compact_kernel(owner, *refs):
    in_a, in_b = refs[:SIDE], refs[SIDE : 2 * SIDE]
    out_a, out_b = refs[2 * SIDE :]
    _, x, y = place()
    for t, (dx, dy, rank) in enumerate(named(owner, x, y)):
        for step in range(SIDE):

            @pl.when(dy == step)
            def _(t=t, step=step, at=dx * 2 + rank):
                out_a[t] = in_a[step][at]

            @pl.when(dx == step)
            def _(t=t, step=step, at=dy * 2 + rank):
                out_b[t] = in_b[step][at]


def expand_kernel(owner, *refs):
    in_a, in_b = refs[:SIDE], refs[SIDE : 2 * SIDE]
    out_a, out_b = refs[2 * SIDE : 3 * SIDE], refs[3 * SIDE :]
    _, x, y = place()
    for out in out_a + out_b:
        out[...] = jnp.zeros_like(out)
    for t, (dx, dy, rank) in enumerate(named(owner, x, y)):
        total_a = sum(ref[t].astype(F32) for ref in in_a).astype(BF16)
        total_b = sum(ref[t].astype(F32) for ref in in_b).astype(BF16)
        for step in range(SIDE):

            @pl.when(dy == step)
            def _(step=step, at=dx * 2 + rank, total=total_a):
                out_a[step][at] = total

            @pl.when(dx == step)
            def _(step=step, at=dy * 2 + rank, total=total_b):
                out_b[step][at] = total


def owners_sum_kernel(*refs):
    in_a, in_b = refs[:SIDE], refs[SIDE : 2 * SIDE]
    out_a, out_b = refs[2 * SIDE : 3 * SIDE], refs[3 * SIDE :]
    for ins, outs in ((in_a, out_a), (in_b, out_b)):
        for k in range(SIDE):
            for r in range(2):
                outs[k][r] = sum(ref[k * 2 + r].astype(F32) for ref in ins).astype(BF16)


def tiles_kernel(owner, slot, *refs):
    in_a, in_b, out = refs[:SIDE], refs[SIDE : 2 * SIDE], refs[2 * SIDE]
    own, x, y = place()
    out[...] = jnp.zeros_like(out)
    for r, tile in enumerate(my_slots(owner, slot, own)):
        for k in range(SIDE):
            out[tile, sub_row(x + k, 0), :] += in_a[k][r].astype(F32)
            out[tile, sub_row(y + k, SIDE * SUB), :] += in_b[k][r].astype(F32)


def dot(a, b, a_dim, b_dim):
    return lax.dot_general(a, b, (((a_dim,), (b_dim,)), ((), ())), preferred_element_type=F32)


def attention_kernel(length, *refs):
    in_a, in_b = refs[:SIDE], refs[SIDE : 2 * SIDE]
    q_ref, up_ref, wk_ref, wv_ref = refs[8:12]
    ctx_ref, qg_ref = refs[12:14]
    out_a, out_b = refs[14:18], refs[18:22]
    gwk_ref, gwv_ref = refs[22:24]
    acc_k, acc_v = refs[24:26]
    span = pl.program_id(0)
    _, x, y = place()
    rows = [ref[j] for j in range(2) for ref in in_a + in_b]
    near = jnp.concatenate(rows, axis=0)
    key = dot(near, wk_ref[...], 1, 0).astype(BF16)
    value = dot(near, wv_ref[...], 1, 0).astype(BF16)
    row = lax.broadcasted_iota(jnp.int32, (1, 2 * 2 * SIDE * SUB), 1)
    lower = (row // (SIDE * SUB)) % 2
    block = (jnp.where(lower == 0, x, y) - (row // SUB) % SIDE + SIDE) % SIDE
    position = lower * (SIDE * SUB) + block * SUB + row % SUB
    limit = jnp.where(row < 2 * SIDE * SUB, length[span, 0], length[span, 1])
    visible = position < limit
    scale = 1.0 / HD**0.5
    key_grads = []
    value_grads = []
    for h in range(q_ref.shape[1] // HD):
        cols = slice(h * HD, (h + 1) * HD)
        q = q_ref[:, cols]
        up = up_ref[:, cols]
        key_h = key[:, cols]
        value_h = value[:, cols]
        score = dot(q, key_h, 1, 1) * scale
        weights = jnp.where(visible, jnp.exp(score), 0.0)
        attention = weights / jnp.sum(weights, axis=-1, keepdims=True)
        attention_b = attention.astype(BF16)
        ctx_ref[:, cols] = dot(attention_b, value_h, 1, 0).astype(BF16)
        dprobs = dot(up, value_h, 1, 1)
        inner = jnp.sum(attention * dprobs, axis=-1, keepdims=True)
        dscore = (attention * (dprobs - inner) * scale).astype(BF16)
        qg_ref[:, cols] = dot(dscore, key_h, 1, 0).astype(BF16)
        key_grads.append(dot(dscore, q, 0, 0).astype(BF16))
        value_grads.append(dot(attention_b, up, 0, 0).astype(BF16))
    key_grad = jnp.concatenate(key_grads, axis=1)
    value_grad = jnp.concatenate(value_grads, axis=1)
    partial = dot(key_grad, wk_ref[...], 1, 1) + dot(value_grad, wv_ref[...], 1, 1)
    partial = partial.astype(BF16)
    for j in range(2):
        for k, out in enumerate(out_a + out_b):
            low = (j * 2 * SIDE + k) * SUB
            out[j] = partial[low : low + SUB]
    step_k = dot(near, key_grad, 0, 0)
    step_v = dot(near, value_grad, 0, 0)

    @pl.when(span == 0)
    def _():
        acc_k[...] = step_k
        acc_v[...] = step_v

    @pl.when(span > 0)
    def _():
        acc_k[...] += step_k
        acc_v[...] += step_v

    @pl.when(span == pl.num_programs(0) - 1)
    def _():
        gwk_ref[...] = acc_k[...].astype(BF16)
        gwv_ref[...] = acc_v[...].astype(BF16)


def call(kernel, scalars, ins, outs):
    vmem = pl.BlockSpec(memory_space=pltpu.VMEM)
    return pl.pallas_call(
        kernel,
        out_shape=[jax.ShapeDtypeStruct(shape, dtype) for shape, dtype in outs],
        in_specs=[pl.BlockSpec(memory_space=pltpu.SMEM)] * len(scalars) + [vmem] * len(ins),
        out_specs=[vmem] * len(outs),
        compiler_params=pltpu.CompilerParams(vmem_limit_bytes=VMEM_LIMIT),
    )(*scalars, *ins)


def attend(key_length, parts, query, upstream, w_key, w_value):
    spans = key_length.shape[0]
    width, columns = w_key.shape
    tile_block = pl.BlockSpec((2, SUB, width), lambda c, *_: (c, 0, 0))
    token_block = pl.BlockSpec((SPAN, columns), lambda c, *_: (c, 0))
    whole = pl.BlockSpec((width, columns), lambda c, *_: (0, 0))
    return pl.pallas_call(
        attention_kernel,
        grid_spec=pltpu.PrefetchScalarGridSpec(
            num_scalar_prefetch=1,
            grid=(spans,),
            in_specs=[tile_block] * 8 + [token_block] * 2 + [whole] * 2,
            out_specs=[token_block] * 2 + [tile_block] * 8 + [whole] * 2,
            scratch_shapes=[pltpu.VMEM((width, columns), F32)] * 2,
        ),
        out_shape=[jax.ShapeDtypeStruct((spans * SPAN, columns), BF16)] * 2
        + [jax.ShapeDtypeStruct((NT, SUB, width), BF16)] * 8
        + [jax.ShapeDtypeStruct((width, columns), BF16)] * 2,
        compiler_params=pltpu.CompilerParams(vmem_limit_bytes=VMEM_LIMIT),
    )(key_length, *parts, query, upstream, w_key, w_value)


def body(
    queries_in,
    w_query,
    w_key,
    w_value,
    tiles,
    neighbour_owner,
    neighbour_slot,
    key_length,
    grad_context,
):
    width = tiles.shape[2]
    steps = range(1, SIDE)
    pair = ((2, SUB, width), BF16)
    line = ((2 * SIDE, SUB, width), BF16)
    group = ((NT, SUB, width), BF16)
    with jax.named_scope("gather"):
        cut = call(split_kernel, (neighbour_owner, neighbour_slot), (tiles,), [pair] * 8)
        row_a = [cut[0]] + [along_x(cut[k], k) for k in steps]
        row_b = [cut[SIDE]] + [along_y(cut[SIDE + k], k) for k in steps]
        line_a = jnp.concatenate(row_a, axis=0)
        line_b = jnp.concatenate(row_b, axis=0)
        all_a = [line_a] + [along_y(line_a, k) for k in steps]
        all_b = [line_b] + [along_x(line_b, k) for k in steps]
        own_a, own_b = call(compact_kernel, (neighbour_owner,), all_a + all_b, [group] * 2)
        part_a = [own_a] + [along_x(own_a, k) for k in steps]
        part_b = [own_b] + [along_y(own_b, k) for k in steps]
    query = jnp.dot(queries_in, w_query, preferred_element_type=F32).astype(BF16)
    with jax.named_scope("attend"):
        done = attend(key_length, part_a + part_b, query, grad_context, w_key, w_value)
    context, query_grad = done[:2]
    send_a, send_b = done[2:6], done[6:10]
    grad_wk, grad_wv = done[10:12]
    local_wq = jnp.dot(queries_in.T, query_grad, preferred_element_type=F32).astype(BF16)
    with jax.named_scope("weights"):
        summed = [lax.psum(g, "dp").astype(F32) for g in (local_wq, grad_wk, grad_wv)]
    with jax.named_scope("scatter"):
        back_a = [send_a[0]] + [along_x(send_a[k], -k) for k in steps]
        back_b = [send_b[0]] + [along_y(send_b[k], -k) for k in steps]
        wide = call(expand_kernel, (neighbour_owner,), back_a + back_b, [line] * 8)
        home_a = [wide[0]] + [along_y(wide[k], -k) for k in steps]
        home_b = [wide[SIDE]] + [along_x(wide[SIDE + k], -k) for k in steps]
        mine = call(owners_sum_kernel, (), home_a + home_b, [pair] * 8)
        last_a = [mine[0]] + [along_x(mine[k], -k) for k in steps]
        last_b = [mine[SIDE]] + [along_y(mine[SIDE + k], -k) for k in steps]
        (grad_tiles,) = call(
            tiles_kernel,
            (neighbour_owner, neighbour_slot),
            last_a + last_b,
            [(tiles.shape, F32)],
        )
    return (context, summed[0], summed[1], summed[2], grad_tiles)


def solution(mesh):
    in_specs = (
        P("dp", None),
        P(None, "enc"),
        P(None, "enc"),
        P(None, "enc"),
        P(("dp", "enc"), None, None),
        P("dp", None),
        P("dp", None),
        P("dp", None),
        P("dp", "enc"),
    )
    out_specs = (
        P("dp", "enc"),
        P(None, "enc"),
        P(None, "enc"),
        P(None, "enc"),
        P(("dp", "enc"), None, None),
    )
    return jax.shard_map(body, mesh=mesh, in_specs=in_specs, out_specs=out_specs, check_vma=False)
```

time: 324 us -> 177 us (0.55)
  waiting for transfers between devices: 204 us -> 63.5 us
  starting transfers between devices: 0.34 us -> 52.1 us
  local copies, waits for them, and re-layouts: 47.7 us -> 11.3 us
  matrix products: 36.6 us -> 6.22 us
  Pallas kernels: 0 us -> 27.6 us
  other arithmetic: 19.9 us -> 1.98 us
    all_gather x1 -> x0, waiting for transfers between devices: 98.7 us -> none  [body(): all_owned = lax.all_gather(tiles, 'enc', axis=0, tiled=True)]
    reduce_scatter x1 -> x0, waiting for transfers between devices: 78.2 us -> none  [body(): lax.psum_scatter(outbound.astype(jnp.bfloat16), 'enc', scatter_dimension=...]
    ppermute x0 -> x36, waiting for transfers between devices: none -> 52.6 us  [the longest x18 29.3 us: along_x(): return lax.ppermute(value, 'enc', pairs)]
    ppermute x0 -> x36, starting transfers between devices: none -> 52.1 us  [the longest x18 27.3 us: along_y(): return lax.ppermute(value, 'enc', pairs)]
    dot_general x14 -> x2, matrix products: 36.6 us -> 6.22 us  [the longest x1 3.58 us: body(): jnp.dot(queries_in, w_query, preferred_element_type=F32).astype(BF16)]
    pallas_call x0 -> x6, Pallas kernels: none -> 27.6 us  [the longest x1 20.1 us: attend(): pl.pallas_call(attention_kernel, grid_spec=pltpu.PrefetchScalarGridSpec(n...]
    psum x1, waiting for transfers between devices: 26.8 us -> 10.9 us  [body(): lax.psum(g, 'dp').astype(F32)]
    scatter x1 -> x0, local copies, waits for them, and re-layouts: 14.5 us -> none  [body(): outbound = jnp.zeros((owners_count * capacity, tile_tokens, enc_width), j...]
  transfers between devices with their start and end apart: 3 -> 37, of which waited for: 3 -> 21; matrix products, arithmetic and copies ran while one was open for 17% -> 2% of each run, Pallas kernels for 0% -> 3%
where the time goes in v1:
time: 177 us
  waiting for transfers between devices  63.5 us (36%)
  starting transfers between devices  52.1 us (29%)
  Pallas kernels  27.6 us (16%)
  between operations  14.3 us (8%)
  local copies, waits for them, and re-layouts  11.3 us (6%)
  matrix products  6.22 us (4%)
  other arithmetic  1.98 us (1%)
    ppermute x18, waiting for transfers between devices, along_x(): return lax.ppermute(value, 'enc', pairs)  29.3 us
    ppermute x18, starting transfers between devices, along_y(): return lax.ppermute(value, 'enc', pairs)  27.3 us
    ppermute x18, starting transfers between devices, along_x(): return lax.ppermute(value, 'enc', pairs)  24.7 us
    ppermute x18, waiting for transfers between devices, along_y(): return lax.ppermute(value, 'enc', pairs)  23.3 us
    pallas_call x1, Pallas kernels, attend(): pl.pallas_call(attention_kernel, grid_spec=pltpu.PrefetchScalarGridSpec(n...  20.1 us
    unnamed x52, local copies, waits for them, and re-layouts  11.3 us
    psum x1, waiting for transfers between devices, body(): lax.psum(g, 'dp').astype(F32)  10.9 us
    pallas_call x5, Pallas kernels, call(): pl.pallas_call(kernel, out_shape=[jax.ShapeDtypeStruct(shape, dtype) for...  7.47 us
  transfers between devices with their start and end apart: 37, of which 21 were waited for; matrix products, arithmetic and copies ran while one was open for 2% of the time, Pallas kernels for 3%

profile of v1, /device:TPU:0, one launch (start us, length us, event | category | flops | bytes accessed | tf_op | source)
XLA Modules:
  0.0 177.0 jit_solution(15451622554134004570)
XLA Ops:
  10.8 1.7 collective-permute-start.6
  12.6 2.9 %collective-permute-start.7 = (bf16[2,16,896]{2,1,0:T(8,128)(2,1)S(1)}, bf16[2,16,896]{2,1,0:T(8,128)(2,1)S(1)}, u32[]{:S(2)}, u32[]{:S(2)}) collective-permute-start(bf16[2,16,896]{2,1,0:T(8,128)(2,1)S(1)} %get-tuple-element.49), channel_id=1, source_target_pairs={{0,2},{1,3},{2,0},{3,1},{4,6},{5,7},{6,4},{7,5},{8,10},{9,11},{10,... | collective-permute-start | bytes 172040 | tf_op jit(solution)/shard_map/gather/ppermute | solution.py:25
  18.3 2.7 %collective-permute-start.1 = (bf16[2,16,896]{2,1,0:T(8,128)(2,1)S(1)}, bf16[2,16,896]{2,1,0:T(8,128)(2,1)S(1)}, u32[]{:S(2)}, u32[]{:S(2)}) collective-permute-start(bf16[2,16,896]{2,1,0:T(8,128)(2,1)S(1)} %get-tuple-element.45), channel_id=1, source_target_pairs={{0,8},{1,9},{2,10},{3,11},{4,12},{5,13},{6,14},{7,15},{8,0},{9,1},... | collective-permute-start | bytes 172040 | tf_op jit(solution)/shard_map/gather/ppermute | solution.py:20
  23.2 2.8 %collective-permute-start.11 = (bf16[8,16,896]{2,1,0:T(8,128)(2,1)S(1)}, bf16[8,16,896]{2,1,0:T(8,128)(2,1)S(1)}, u32[]{:S(2)}, u32[]{:S(2)}) collective-permute-start(bf16[8,16,896]{2,1,0:T(8,128)(2,1)S(1)} %constant_dynamic-update-slice_fusion.4.refs_4_), channel_id=1, source_target_pairs={{0,12},{1,13},{2,14},{3,15},{4,0},{5,1},{6,2},{7,3},{8,4},{9,5},{1... | collective-permute-start | bytes 688136 | tf_op jit(solution)/shard_map/gather/ppermute | solution.py:20
  27.1 1.8 %collective-permute-start.4 = (bf16[8,16,896]{2,1,0:T(8,128)(2,1)S(1)}, bf16[8,16,896]{2,1,0:T(8,128)(2,1)S(1)}, u32[]{:S(2)}, u32[]{:S(2)}) collective-permute-start(bf16[8,16,896]{2,1,0:T(8,128)(2,1)S(1)} %constant_dynamic-update-slice_fusion.refs_0_), channel_id=1, source_target_pairs={{0,2},{1,3},{2,0},{3,1},{4,6},{5,7},{6,4},{7,5},{8,10},{9,11},{10,... | collective-permute-start | bytes 688136 | tf_op jit(solution)/shard_map/gather/ppermute | solution.py:25
  28.9 3.4 %collective-permute-done.10.refs_6_ = bf16[8,16,896]{2,1,0:T(8,128)(2,1)S(1)} collective-permute-done((bf16[8,16,896]{2,1,0:T(8,128)(2,1)S(1)}, bf16[8,16,896]{2,1,0:T(8,128)(2,1)S(1)}, u32[]{:S(2)}, u32[]{:S(2)}) %collective-permute-start.10) | collective-permute-done | bytes 229408 | tf_op jit(solution)/shard_map/gather/ppermute | solution.py:20
  34.8 2.6 %collective-permute-done.3.refs_1_ = bf16[8,16,896]{2,1,0:T(8,128)(2,1)S(1)} collective-permute-done((bf16[8,16,896]{2,1,0:T(8,128)(2,1)S(1)}, bf16[8,16,896]{2,1,0:T(8,128)(2,1)S(1)}, u32[]{:S(2)}, u32[]{:S(2)}) %collective-permute-start.3) | collective-permute-done | bytes 229408 | tf_op jit(solution)/shard_map/gather/ppermute | solution.py:25
  38.4 2.0 %gather.3 = (bf16[16,16,896]{2,1,0:T(8,128)(2,1)S(1)}, bf16[16,16,896]{2,1,0:T(8,128)(2,1)S(1)}) custom-call(s32[8,2]{1,0:T(8,128)S(1)} %copy.16.owner, bf16[8,16,896]{2,1,0:T(8,128)(2,1)S(1)} %constant_dynamic-update-slice_fusion.refs_0_, bf16[8,16,896]{2,1,0:T(8,128)(2,1)S(1)} %collective-permute-done.3.refs_1_, ...), custom_call_target="tpu_custom_call" | custom-call | tf_op jit(solution)/shard_map/gather/pallas_call | solution.py:200
  42.2 3.3 %collective-permute-start.13 = (bf16[16,16,896]{2,1,0:T(8,128)(2,1)S(1)}, bf16[16,16,896]{2,1,0:T(8,128)(2,1)S(1)}, u32[]{:S(2)}, u32[]{:S(2)}) collective-permute-start(bf16[16,16,896]{2,1,0:T(8,128)(2,1)S(1)} %get-tuple-element.51.refs_0_), channel_id=1, source_target_pairs={{0,8},{1,9},{2,10},{3,11},{4,12},{5,13},{6,14},{7,15},{8,0},{9,1},... | collective-permute-start | bytes 1376264 | tf_op jit(solution)/shard_map/gather/ppermute | solution.py:20
  45.8 3.8 %collective-permute-start.16 = (bf16[16,16,896]{2,1,0:T(8,128)(2,1)S(1)}, bf16[16,16,896]{2,1,0:T(8,128)(2,1)S(1)}, u32[]{:S(2)}, u32[]{:S(2)}) collective-permute-start(bf16[16,16,896]{2,1,0:T(8,128)(2,1)S(1)} %get-tuple-element.52.refs_4_), channel_id=1, source_target_pairs={{0,2},{1,3},{2,0},{3,1},{4,6},{5,7},{6,4},{7,5},{8,10},{9,11},{10,... | collective-permute-start | bytes 1376264 | tf_op jit(solution)/shard_map/gather/ppermute | solution.py:25
  49.6 5.3 %collective-permute-done.12.refs_1_ = bf16[16,16,896]{2,1,0:T(8,128)(2,1)S(1)} collective-permute-done((bf16[16,16,896]{2,1,0:T(8,128)(2,1)S(1)}, bf16[16,16,896]{2,1,0:T(8,128)(2,1)S(1)}, u32[]{:S(2)}, u32[]{:S(2)}) %collective-permute-start.12) | collective-permute-done | bytes 458784 | tf_op jit(solution)/shard_map/gather/ppermute | solution.py:20
  54.9 2.4 %collective-permute-start.17 = (bf16[16,16,896]{2,1,0:T(8,128)(2,1)S(1)}, bf16[16,16,896]{2,1,0:T(8,128)(2,1)S(1)}, u32[]{:S(2)}, u32[]{:S(2)}) collective-permute-start(bf16[16,16,896]{2,1,0:T(8,128)(2,1)S(1)} %get-tuple-element.52.refs_4_), channel_id=1, source_target_pairs={{0,3},{1,0},{2,1},{3,2},{4,7},{5,4},{6,5},{7,6},{8,11},{9,8},{10,9... | collective-permute-start | bytes 1376264 | tf_op jit(solution)/shard_map/gather/ppermute | solution.py:25
  57.3 3.6 %convolution_convert_fusion.1.refs_8_ = bf16[512,256]{1,0:T(8,128)(2,1)S(1)} fusion(bf16[512,4096]{1,0:T(8,128)(2,1)} %param.9, bf16[4096,256]{1,0:T(8,128)(2,1)S(1)} %copy-done), kind=kOutput, calls=%fused_computation.2 | convolution fusion | flops 1073872896 | bytes 6553600 | tf_op jit(solution)/shard_map/dot_general | solution.py:258
  61.0 4.0 %collective-permute-done.16.refs_6_ = bf16[16,16,896]{2,1,0:T(8,128)(2,1)S(1)} collective-permute-done((bf16[16,16,896]{2,1,0:T(8,128)(2,1)S(1)}, bf16[16,16,896]{2,1,0:T(8,128)(2,1)S(1)}, u32[]{:S(2)}, u32[]{:S(2)}) %collective-permute-start.16) | collective-permute-done | bytes 458784 | tf_op jit(solution)/shard_map/gather/ppermute | solution.py:25
  67.5 20.1 %attend.1 = (bf16[512,256]{1,0:T(8,128)(2,1)}, bf16[512,256]{1,0:T(8,128)(2,1)S(1)}, bf16[16,16,896]{2,1,0:T(8,128)(2,1)S(1)}, bf16[16,16,896]{2,1,0:T(8,128)(2,...) custom-call(s32[8,2]{1,0:T(8,128)S(1)} %copy.17.length, ...), custom_call_target="tpu_custom_call" | custom-call | tf_op jit(solution)/shard_map/attend/pallas_call | solution.py:215
  88.4 2.6 %fusion = bf16[4096,256]{0,1:T(8,128)(2,1)} fusion(bf16[512,256]{1,0:T(8,128)(2,1)S(1)} %get-tuple-element.54, bf16[512,4096]{1,0:T(8,128)(2,1)S(1)} %copy-done.12), kind=kOutput, calls=%fused_computation.1 | convolution fusion | flops 1074790400 | bytes 6553600 | tf_op jit(solution)/shard_map/dot_general | solution.py:264
  91.5 3.1 %collective-permute-start.19 = (bf16[16,16,896]{2,1,0:T(8,128)(2,1)}, bf16[16,16,896]{2,1,0:T(8,128)(2,1)S(1)}, u32[]{:S(2)}, u32[]{:S(2)}) collective-permute-start(bf16[16,16,896]{2,1,0:T(8,128)(2,1)} %copy-done.10), channel_id=1, source_target_pairs={{0,8},{1,9},{2,10},{3,11},{4,12},{5,13},{6,14},{7,15},{8,0},{9,1},... | collective-permute-start | bytes 1376264 | tf_op jit(solution)/shard_map/scatter/ppermute | solution.py:20
  95.9 3.7 %collective-permute-start.21 = (bf16[16,16,896]{2,1,0:T(8,128)(2,1)}, bf16[16,16,896]{2,1,0:T(8,128)(2,1)S(1)}, u32[]{:S(2)}, u32[]{:S(2)}) collective-permute-start(bf16[16,16,896]{2,1,0:T(8,128)(2,1)} %copy-done.8), channel_id=1, source_target_pairs={{0,3},{1,0},{2,1},{3,2},{4,7},{5,4},{6,5},{7,6},{8,11},{9,8},{10,9... | collective-permute-start | bytes 1376264 | tf_op jit(solution)/shard_map/scatter/ppermute | solution.py:25
  99.6 9.5 %collective-permute-done.18.refs_1_ = bf16[16,16,896]{2,1,0:T(8,128)(2,1)S(1)} collective-permute-done((bf16[16,16,896]{2,1,0:T(8,128)(2,1)}, bf16[16,16,896]{2,1,0:T(8,128)(2,1)S(1)}, u32[]{:S(2)}, u32[]{:S(2)}) %collective-permute-start.18) | collective-permute-done | bytes 458784 | tf_op jit(solution)/shard_map/scatter/ppermute | solution.py:20
  110.1 2.7 %collective-permute-done.20.refs_3_ = bf16[16,16,896]{2,1,0:T(8,128)(2,1)S(1)} collective-permute-done((bf16[16,16,896]{2,1,0:T(8,128)(2,1)}, bf16[16,16,896]{2,1,0:T(8,128)(2,1)S(1)}, u32[]{:S(2)}, u32[]{:S(2)}) %collective-permute-start.20) | collective-permute-done | bytes 458784 | tf_op jit(solution)/shard_map/scatter/ppermute | solution.py:20
  113.5 5.5 %collective-permute-done.23.refs_7_ = bf16[16,16,896]{2,1,0:T(8,128)(2,1)S(1)} collective-permute-done((bf16[16,16,896]{2,1,0:T(8,128)(2,1)}, bf16[16,16,896]{2,1,0:T(8,128)(2,1)S(1)}, u32[]{:S(2)}, u32[]{:S(2)}) %collective-permute-start.23) | collective-permute-done | bytes 458784 | tf_op jit(solution)/shard_map/scatter/ppermute | solution.py:25
  119.1 2.4 %scatter.3 = (bf16[8,16,896]{2,1,0:T(8,128)(2,1)S(1)}, bf16[8,16,896]{2,1,0:T(8,128)(2,1)S(1)}, bf16[8,16,896]{2,1,0:T(8,128)(2,1)S(1)}, bf16[8,16,896]{2,1,0:T(...) custom-call(s32[8,2]{1,0:T(8,128)S(1)} %copy.16.owner, ...), custom_call_target="tpu_custom_call" | custom-call | tf_op jit(solution)/shard_map/scatter/pallas_call | solution.py:200
  124.0 3.6 %collective-permute-start.27 = (bf16[8,16,896]{2,1,0:T(8,128)(2,1)S(1)}, bf16[8,16,896]{2,1,0:T(8,128)(2,1)S(1)}, u32[]{:S(2)}, u32[]{:S(2)}) collective-permute-start(bf16[8,16,896]{2,1,0:T(8,128)(2,1)S(1)} %get-tuple-element.70), channel_id=1, source_target_pairs={{0,12},{1,13},{2,14},{3,15},{4,0},{5,1},{6,2},{7,3},{8,4},{9,5},{1... | collective-permute-start | bytes 688136 | tf_op jit(solution)/shard_map/scatter/ppermute | solution.py:20
  128.4 2.3 %collective-permute-done.25.refs_2_ = bf16[8,16,896]{2,1,0:T(8,128)(2,1)S(1)} collective-permute-done((bf16[8,16,896]{2,1,0:T(8,128)(2,1)S(1)}, bf16[8,16,896]{2,1,0:T(8,128)(2,1)S(1)}, u32[]{:S(2)}, u32[]{:S(2)}) %collective-permute-start.25) | collective-permute-done | bytes 229408 | tf_op jit(solution)/shard_map/scatter/ppermute | solution.py:25
  130.7 2.3 %collective-permute-done.26.refs_3_ = bf16[8,16,896]{2,1,0:T(8,128)(2,1)S(1)} collective-permute-done((bf16[8,16,896]{2,1,0:T(8,128)(2,1)S(1)}, bf16[8,16,896]{2,1,0:T(8,128)(2,1)S(1)}, u32[]{:S(2)}, u32[]{:S(2)}) %collective-permute-start.26) | collective-permute-done | bytes 229408 | tf_op jit(solution)/shard_map/scatter/ppermute | solution.py:25
  133.0 1.8 %collective-permute-done.27.refs_5_ = bf16[8,16,896]{2,1,0:T(8,128)(2,1)S(1)} collective-permute-done((bf16[8,16,896]{2,1,0:T(8,128)(2,1)S(1)}, bf16[8,16,896]{2,1,0:T(8,128)(2,1)S(1)}, u32[]{:S(2)}, u32[]{:S(2)}) %collective-permute-start.27) | collective-permute-done | bytes 229408 | tf_op jit(solution)/shard_map/scatter/ppermute | solution.py:20
  135.8 3.0 %collective-permute-done.29.refs_7_ = bf16[8,16,896]{2,1,0:T(8,128)(2,1)S(1)} collective-permute-done((bf16[8,16,896]{2,1,0:T(8,128)(2,1)S(1)}, bf16[8,16,896]{2,1,0:T(8,128)(2,1)S(1)}, u32[]{:S(2)}, u32[]{:S(2)}) %collective-permute-start.29) | collective-permute-done | bytes 229408 | tf_op jit(solution)/shard_map/scatter/ppermute | solution.py:20
  141.1 3.1 %collective-permute-start.33 = (bf16[2,16,896]{2,1,0:T(8,128)(2,1)S(1)}, bf16[2,16,896]{2,1,0:T(8,128)(2,1)S(1)}, u32[]{:S(2)}, u32[]{:S(2)}) collective-permute-start(bf16[2,16,896]{2,1,0:T(8,128)(2,1)S(1)} %get-tuple-element.78), channel_id=1, source_target_pairs={{0,3},{1,0},{2,1},{3,2},{4,7},{5,4},{6,5},{7,6},{8,11},{9,8},{10,9... | collective-permute-start | bytes 172040 | tf_op jit(solution)/shard_map/scatter/ppermute | solution.py:25
  146.0 3.9 %collective-permute-done.34.refs_6_ = bf16[2,16,896]{2,1,0:T(8,128)(2,1)S(1)} collective-permute-done((bf16[2,16,896]{2,1,0:T(8,128)(2,1)S(1)}, bf16[2,16,896]{2,1,0:T(8,128)(2,1)S(1)}, u32[]{:S(2)}, u32[]{:S(2)}) %collective-permute-start.34) | collective-permute-done | bytes 57376 | tf_op jit(solution)/shard_map/scatter/ppermute | solution.py:25
  150.8 2.1 %scatter.5 = f32[4,128,896]{2,1,0:T(8,128)} custom-call(s32[8,2]{1,0:T(8,128)S(1)} %copy.16.owner, s32[8,2]{1,0:T(8,128)S(1)} %copy.15.slot, bf16[2,16,896]{2,1,0:T(8,128)(2,1)S(1)} %get-tuple-element.73.refs_0_, bf16[2,16,896]{2,1,0:T(8,128)(2,1)S(1)} %collective-permute-done.30.refs_1_, bf16[2,16,896]{2,1,0:T(8,128)(2,1)S(1)} %collective-permute-done.31.refs_2_, ...), custom_call_target="tpu_custom_call" | custom-call | tf_op jit(solution)/shard_map/scatter/pallas_call | solution.py:200
  152.9 10.9 %all-reduce.3.cloned.1.call-done = (bf16[4096,256]{0,1:T(8,128)(2,1)}, bf16[896,256]{1,0:T(8,128)(2,1)}, bf16[896,256]{1,0:T(8,128)(2,1)}) async-done(((bf16[4096,256]{0,1:T(8,128)(2,1)}, bf16[896,256]{1,0:T(8,128)(2,1)}, bf16[896,256]{1,0:T(8,128)(2,1)}), (bf16[4096,256]{0,1:T(8,128)(2,1)}, bf16[896,256]{1,0:T(8,128)(2,1)}, bf16[896,256]{1,0:T(8,128)(2,1)})) %all-reduce.3.cloned.1.call-update) | async-done | bytes 3014672 | tf_op jit(solution)/shard_map/weights/psum | solution.py:266
  163.8 4.4 %copy.21 = f32[4096,256]{1,0:T(8,128)} copy(bf16[4096,256]{0,1:T(8,128)(2,1)} %get-tuple-element.86) | data formatting | bytes 6291456
  (107 shorter events, 33.6 us)
Async XLA Ops:
  7.2 156.6 %all-reduce.3.cloned.1.call-start = ((), (), s32[]{:S(2)}) async-start(), calls=%async_computation | async-start | bytes 6029312 | tf_op jit(solution)/shard_map/weights/psum | solution.py:266
  10.8 10.2 %collective-permute-start.6 = (bf16[2,16,896]{2,1,0:T(8,128)(2,1)S(1)}, bf16[2,16,896]{2,1,0:T(8,128)(2,1)S(1)}, u32[]{:S(2)}, u32[]{:S(2)}) collective-permute-start(bf16[2,16,896]{2,1,0:T(8,128)(2,1)S(1)} %get-tuple-element.48), channel_id=1, source_target_pairs={{0,1},{1,2},{2,3},{3,0},{4,5},{5,6},{6,7},{7,4},{8,9},{9,10},{10,1... | collective-permute-start | bytes 172040 | tf_op jit(solution)/shard_map/gather/ppermute | solution.py:25
  12.6 10.0 %collective-permute-start.7 = (bf16[2,16,896]{2,1,0:T(8,128)(2,1)S(1)}, bf16[2,16,896]{2,1,0:T(8,128)(2,1)S(1)}, u32[]{:S(2)}, u32[]{:S(2)}) collective-permute-start(bf16[2,16,896]{2,1,0:T(8,128)(2,1)S(1)} %get-tuple-element.49), channel_id=1, source_target_pairs={{0,2},{1,3},{2,0},{3,1},{4,6},{5,7},{6,4},{7,5},{8,10},{9,11},{10,... | collective-permute-start | bytes 172040 | tf_op jit(solution)/shard_map/gather/ppermute | solution.py:25
  15.5 7.1 %collective-permute-start.8 = (bf16[2,16,896]{2,1,0:T(8,128)(2,1)S(1)}, bf16[2,16,896]{2,1,0:T(8,128)(2,1)S(1)}, u32[]{:S(2)}, u32[]{:S(2)}) collective-permute-start(bf16[2,16,896]{2,1,0:T(8,128)(2,1)S(1)} %get-tuple-element.50), channel_id=1, source_target_pairs={{0,3},{1,0},{2,1},{3,2},{4,7},{5,4},{6,5},{7,6},{8,11},{9,8},{10,9... | collective-permute-start | bytes 172040 | tf_op jit(solution)/shard_map/gather/ppermute | solution.py:25
  16.8 9.2 %collective-permute-start = (bf16[2,16,896]{2,1,0:T(8,128)(2,1)S(1)}, bf16[2,16,896]{2,1,0:T(8,128)(2,1)S(1)}, u32[]{:S(2)}, u32[]{:S(2)}) collective-permute-start(bf16[2,16,896]{2,1,0:T(8,128)(2,1)S(1)} %get-tuple-element.44), channel_id=1, source_target_pairs={{0,4},{1,5},{2,6},{3,7},{4,8},{5,9},{6,10},{7,11},{8,12},{9,13},{1... | collective-permute-start | bytes 172040 | tf_op jit(solution)/shard_map/gather/ppermute | solution.py:20
  18.3 7.7 %collective-permute-start.1 = (bf16[2,16,896]{2,1,0:T(8,128)(2,1)S(1)}, bf16[2,16,896]{2,1,0:T(8,128)(2,1)S(1)}, u32[]{:S(2)}, u32[]{:S(2)}) collective-permute-start(bf16[2,16,896]{2,1,0:T(8,128)(2,1)S(1)} %get-tuple-element.45), channel_id=1, source_target_pairs={{0,8},{1,9},{2,10},{3,11},{4,12},{5,13},{6,14},{7,15},{8,0},{9,1},... | collective-permute-start | bytes 172040 | tf_op jit(solution)/shard_map/gather/ppermute | solution.py:20
  22.6 9.7 %collective-permute-start.10 = (bf16[8,16,896]{2,1,0:T(8,128)(2,1)S(1)}, bf16[8,16,896]{2,1,0:T(8,128)(2,1)S(1)}, u32[]{:S(2)}, u32[]{:S(2)}) collective-permute-start(bf16[8,16,896]{2,1,0:T(8,128)(2,1)S(1)} %constant_dynamic-update-slice_fusion.4.refs_4_), channel_id=1, source_target_pairs={{0,8},{1,9},{2,10},{3,11},{4,12},{5,13},{6,14},{7,15},{8,0},{9,1},... | collective-permute-start | bytes 688136 | tf_op jit(solution)/shard_map/gather/ppermute | solution.py:20
  23.2 10.6 %collective-permute-start.11 = (bf16[8,16,896]{2,1,0:T(8,128)(2,1)S(1)}, bf16[8,16,896]{2,1,0:T(8,128)(2,1)S(1)}, u32[]{:S(2)}, u32[]{:S(2)}) collective-permute-start(bf16[8,16,896]{2,1,0:T(8,128)(2,1)S(1)} %constant_dynamic-update-slice_fusion.4.refs_4_), channel_id=1, source_target_pairs={{0,12},{1,13},{2,14},{3,15},{4,0},{5,1},{6,2},{7,3},{8,4},{9,5},{1... | collective-permute-start | bytes 688136 | tf_op jit(solution)/shard_map/gather/ppermute | solution.py:20
  26.0 8.8 %collective-permute-start.9 = (bf16[8,16,896]{2,1,0:T(8,128)(2,1)S(1)}, bf16[8,16,896]{2,1,0:T(8,128)(2,1)S(1)}, u32[]{:S(2)}, u32[]{:S(2)}) collective-permute-start(bf16[8,16,896]{2,1,0:T(8,128)(2,1)S(1)} %constant_dynamic-update-slice_fusion.4.refs_4_), channel_id=1, source_target_pairs={{0,4},{1,5},{2,6},{3,7},{4,8},{5,9},{6,10},{7,11},{8,12},{9,13},{1... | collective-permute-start | bytes 688136 | tf_op jit(solution)/shard_map/gather/ppermute | solution.py:20
  26.4 10.9 %collective-permute-start.3 = (bf16[8,16,896]{2,1,0:T(8,128)(2,1)S(1)}, bf16[8,16,896]{2,1,0:T(8,128)(2,1)S(1)}, u32[]{:S(2)}, u32[]{:S(2)}) collective-permute-start(bf16[8,16,896]{2,1,0:T(8,128)(2,1)S(1)} %constant_dynamic-update-slice_fusion.refs_0_), channel_id=1, source_target_pairs={{0,1},{1,2},{2,3},{3,0},{4,5},{5,6},{6,7},{7,4},{8,9},{9,10},{10,1... | collective-permute-start | bytes 688136 | tf_op jit(solution)/shard_map/gather/ppermute | solution.py:25
  27.1 10.2 %collective-permute-start.4 = (bf16[8,16,896]{2,1,0:T(8,128)(2,1)S(1)}, bf16[8,16,896]{2,1,0:T(8,128)(2,1)S(1)}, u32[]{:S(2)}, u32[]{:S(2)}) collective-permute-start(bf16[8,16,896]{2,1,0:T(8,128)(2,1)S(1)} %constant_dynamic-update-slice_fusion.refs_0_), channel_id=1, source_target_pairs={{0,2},{1,3},{2,0},{3,1},{4,6},{5,7},{6,4},{7,5},{8,10},{9,11},{10,... | collective-permute-start | bytes 688136 | tf_op jit(solution)/shard_map/gather/ppermute | solution.py:25
  32.4 6.0 %collective-permute-start.5 = (bf16[8,16,896]{2,1,0:T(8,128)(2,1)S(1)}, bf16[8,16,896]{2,1,0:T(8,128)(2,1)S(1)}, u32[]{:S(2)}, u32[]{:S(2)}) collective-permute-start(bf16[8,16,896]{2,1,0:T(8,128)(2,1)S(1)} %constant_dynamic-update-slice_fusion.refs_0_), channel_id=1, source_target_pairs={{0,3},{1,0},{2,1},{3,2},{4,7},{5,4},{6,5},{7,6},{8,11},{9,8},{10,9... | collective-permute-start | bytes 688136 | tf_op jit(solution)/shard_map/gather/ppermute | solution.py:25
  40.4 14.5 %collective-permute-start.12 = (bf16[16,16,896]{2,1,0:T(8,128)(2,1)S(1)}, bf16[16,16,896]{2,1,0:T(8,128)(2,1)S(1)}, u32[]{:S(2)}, u32[]{:S(2)}) collective-permute-start(bf16[16,16,896]{2,1,0:T(8,128)(2,1)S(1)} %get-tuple-element.51.refs_0_), channel_id=1, source_target_pairs={{0,4},{1,5},{2,6},{3,7},{4,8},{5,9},{6,10},{7,11},{8,12},{9,13},{1... | collective-permute-start | bytes 1376264 | tf_op jit(solution)/shard_map/gather/ppermute | solution.py:20
  42.2 18.7 %collective-permute-start.13 = (bf16[16,16,896]{2,1,0:T(8,128)(2,1)S(1)}, bf16[16,16,896]{2,1,0:T(8,128)(2,1)S(1)}, u32[]{:S(2)}, u32[]{:S(2)}) collective-permute-start(bf16[16,16,896]{2,1,0:T(8,128)(2,1)S(1)} %get-tuple-element.51.refs_0_), channel_id=1, source_target_pairs={{0,8},{1,9},{2,10},{3,11},{4,12},{5,13},{6,14},{7,15},{8,0},{9,1},... | collective-permute-start | bytes 1376264 | tf_op jit(solution)/shard_map/gather/ppermute | solution.py:20
  45.5 15.4 %collective-permute-start.14 = (bf16[16,16,896]{2,1,0:T(8,128)(2,1)S(1)}, bf16[16,16,896]{2,1,0:T(8,128)(2,1)S(1)}, u32[]{:S(2)}, u32[]{:S(2)}) collective-permute-start(bf16[16,16,896]{2,1,0:T(8,128)(2,1)S(1)} %get-tuple-element.51.refs_0_), channel_id=1, source_target_pairs={{0,12},{1,13},{2,14},{3,15},{4,0},{5,1},{6,2},{7,3},{8,4},{9,5},{1... | collective-permute-start | bytes 1376264 | tf_op jit(solution)/shard_map/gather/ppermute | solution.py:20
  45.5 15.5 %collective-permute-start.15 = (bf16[16,16,896]{2,1,0:T(8,128)(2,1)S(1)}, bf16[16,16,896]{2,1,0:T(8,128)(2,1)S(1)}, u32[]{:S(2)}, u32[]{:S(2)}) collective-permute-start(bf16[16,16,896]{2,1,0:T(8,128)(2,1)S(1)} %get-tuple-element.52.refs_4_), channel_id=1, source_target_pairs={{0,1},{1,2},{2,3},{3,0},{4,5},{5,6},{6,7},{7,4},{8,9},{9,10},{10,1... | collective-permute-start | bytes 1376264 | tf_op jit(solution)/shard_map/gather/ppermute | solution.py:25
  45.8 19.1 %collective-permute-start.16 = (bf16[16,16,896]{2,1,0:T(8,128)(2,1)S(1)}, bf16[16,16,896]{2,1,0:T(8,128)(2,1)S(1)}, u32[]{:S(2)}, u32[]{:S(2)}) collective-permute-start(bf16[16,16,896]{2,1,0:T(8,128)(2,1)S(1)} %get-tuple-element.52.refs_4_), channel_id=1, source_target_pairs={{0,2},{1,3},{2,0},{3,1},{4,6},{5,7},{6,4},{7,5},{8,10},{9,11},{10,... | collective-permute-start | bytes 1376264 | tf_op jit(solution)/shard_map/gather/ppermute | solution.py:25
  54.9 10.1 %collective-permute-start.17 = (bf16[16,16,896]{2,1,0:T(8,128)(2,1)S(1)}, bf16[16,16,896]{2,1,0:T(8,128)(2,1)S(1)}, u32[]{:S(2)}, u32[]{:S(2)}) collective-permute-start(bf16[16,16,896]{2,1,0:T(8,128)(2,1)S(1)} %get-tuple-element.52.refs_4_), channel_id=1, source_target_pairs={{0,3},{1,0},{2,1},{3,2},{4,7},{5,4},{6,5},{7,6},{8,11},{9,8},{10,9... | collective-permute-start | bytes 1376264 | tf_op jit(solution)/shard_map/gather/ppermute | solution.py:25
  91.1 18.0 %collective-permute-start.18 = (bf16[16,16,896]{2,1,0:T(8,128)(2,1)}, bf16[16,16,896]{2,1,0:T(8,128)(2,1)S(1)}, u32[]{:S(2)}, u32[]{:S(2)}) collective-permute-start(bf16[16,16,896]{2,1,0:T(8,128)(2,1)} %copy-done.11), channel_id=1, source_target_pairs={{0,12},{1,13},{2,14},{3,15},{4,0},{5,1},{6,2},{7,3},{8,4},{9,5},{1... | collective-permute-start | bytes 1376264 | tf_op jit(solution)/shard_map/scatter/ppermute | solution.py:20
  91.5 18.6 %collective-permute-start.19 = (bf16[16,16,896]{2,1,0:T(8,128)(2,1)}, bf16[16,16,896]{2,1,0:T(8,128)(2,1)S(1)}, u32[]{:S(2)}, u32[]{:S(2)}) collective-permute-start(bf16[16,16,896]{2,1,0:T(8,128)(2,1)} %copy-done.10), channel_id=1, source_target_pairs={{0,8},{1,9},{2,10},{3,11},{4,12},{5,13},{6,14},{7,15},{8,0},{9,1},... | collective-permute-start | bytes 1376264 | tf_op jit(solution)/shard_map/scatter/ppermute | solution.py:20
  94.6 18.2 %collective-permute-start.20 = (bf16[16,16,896]{2,1,0:T(8,128)(2,1)}, bf16[16,16,896]{2,1,0:T(8,128)(2,1)S(1)}, u32[]{:S(2)}, u32[]{:S(2)}) collective-permute-start(bf16[16,16,896]{2,1,0:T(8,128)(2,1)} %copy-done.9), channel_id=1, source_target_pairs={{0,4},{1,5},{2,6},{3,7},{4,8},{5,9},{6,10},{7,11},{8,12},{9,13},{1... | collective-permute-start | bytes 1376264 | tf_op jit(solution)/shard_map/scatter/ppermute | solution.py:20
  95.9 16.9 %collective-permute-start.21 = (bf16[16,16,896]{2,1,0:T(8,128)(2,1)}, bf16[16,16,896]{2,1,0:T(8,128)(2,1)S(1)}, u32[]{:S(2)}, u32[]{:S(2)}) collective-permute-start(bf16[16,16,896]{2,1,0:T(8,128)(2,1)} %copy-done.8), channel_id=1, source_target_pairs={{0,3},{1,0},{2,1},{3,2},{4,7},{5,4},{6,5},{7,6},{8,11},{9,8},{10,9... | collective-permute-start | bytes 1376264 | tf_op jit(solution)/shard_map/scatter/ppermute | solution.py:25
  99.6 13.9 %collective-permute-start.22 = (bf16[16,16,896]{2,1,0:T(8,128)(2,1)}, bf16[16,16,896]{2,1,0:T(8,128)(2,1)S(1)}, u32[]{:S(2)}, u32[]{:S(2)}) collective-permute-start(bf16[16,16,896]{2,1,0:T(8,128)(2,1)} %copy-done.7), channel_id=1, source_target_pairs={{0,2},{1,3},{2,0},{3,1},{4,6},{5,7},{6,4},{7,5},{8,10},{9,11},{10,... | collective-permute-start | bytes 1376264 | tf_op jit(solution)/shard_map/scatter/ppermute | solution.py:25
  109.2 9.9 %collective-permute-start.23 = (bf16[16,16,896]{2,1,0:T(8,128)(2,1)}, bf16[16,16,896]{2,1,0:T(8,128)(2,1)S(1)}, u32[]{:S(2)}, u32[]{:S(2)}) collective-permute-start(bf16[16,16,896]{2,1,0:T(8,128)(2,1)} %copy-done.6), channel_id=1, source_target_pairs={{0,1},{1,2},{2,3},{3,0},{4,5},{5,6},{6,7},{7,4},{8,9},{9,10},{10,1... | collective-permute-start | bytes 1376264 | tf_op jit(solution)/shard_map/scatter/ppermute | solution.py:25
  121.5 6.5 %collective-permute-start.24 = (bf16[8,16,896]{2,1,0:T(8,128)(2,1)S(1)}, bf16[8,16,896]{2,1,0:T(8,128)(2,1)S(1)}, u32[]{:S(2)}, u32[]{:S(2)}) collective-permute-start(bf16[8,16,896]{2,1,0:T(8,128)(2,1)S(1)} %get-tuple-element.66), channel_id=1, source_target_pairs={{0,3},{1,0},{2,1},{3,2},{4,7},{5,4},{6,5},{7,6},{8,11},{9,8},{10,9... | collective-permute-start | bytes 688136 | tf_op jit(solution)/shard_map/scatter/ppermute | solution.py:25
  123.0 7.6 %collective-permute-start.25 = (bf16[8,16,896]{2,1,0:T(8,128)(2,1)S(1)}, bf16[8,16,896]{2,1,0:T(8,128)(2,1)S(1)}, u32[]{:S(2)}, u32[]{:S(2)}) collective-permute-start(bf16[8,16,896]{2,1,0:T(8,128)(2,1)S(1)} %get-tuple-element.67), channel_id=1, source_target_pairs={{0,2},{1,3},{2,0},{3,1},{4,6},{5,7},{6,4},{7,5},{8,10},{9,11},{10,... | collective-permute-start | bytes 688136 | tf_op jit(solution)/shard_map/scatter/ppermute | solution.py:25
  123.3 9.7 %collective-permute-start.26 = (bf16[8,16,896]{2,1,0:T(8,128)(2,1)S(1)}, bf16[8,16,896]{2,1,0:T(8,128)(2,1)S(1)}, u32[]{:S(2)}, u32[]{:S(2)}) collective-permute-start(bf16[8,16,896]{2,1,0:T(8,128)(2,1)S(1)} %get-tuple-element.68), channel_id=1, source_target_pairs={{0,1},{1,2},{2,3},{3,0},{4,5},{5,6},{6,7},{7,4},{8,9},{9,10},{10,1... | collective-permute-start | bytes 688136 | tf_op jit(solution)/shard_map/scatter/ppermute | solution.py:25
  124.0 10.8 %collective-permute-start.27 = (bf16[8,16,896]{2,1,0:T(8,128)(2,1)S(1)}, bf16[8,16,896]{2,1,0:T(8,128)(2,1)S(1)}, u32[]{:S(2)}, u32[]{:S(2)}) collective-permute-start(bf16[8,16,896]{2,1,0:T(8,128)(2,1)S(1)} %get-tuple-element.70), channel_id=1, source_target_pairs={{0,12},{1,13},{2,14},{3,15},{4,0},{5,1},{6,2},{7,3},{8,4},{9,5},{1... | collective-permute-start | bytes 688136 | tf_op jit(solution)/shard_map/scatter/ppermute | solution.py:20
  127.5 8.2 %collective-permute-start.28 = (bf16[8,16,896]{2,1,0:T(8,128)(2,1)S(1)}, bf16[8,16,896]{2,1,0:T(8,128)(2,1)S(1)}, u32[]{:S(2)}, u32[]{:S(2)}) collective-permute-start(bf16[8,16,896]{2,1,0:T(8,128)(2,1)S(1)} %get-tuple-element.71), channel_id=1, source_target_pairs={{0,8},{1,9},{2,10},{3,11},{4,12},{5,13},{6,14},{7,15},{8,0},{9,1},... | collective-permute-start | bytes 688136 | tf_op jit(solution)/shard_map/scatter/ppermute | solution.py:20
  128.0 10.8 %collective-permute-start.29 = (bf16[8,16,896]{2,1,0:T(8,128)(2,1)S(1)}, bf16[8,16,896]{2,1,0:T(8,128)(2,1)S(1)}, u32[]{:S(2)}, u32[]{:S(2)}) collective-permute-start(bf16[8,16,896]{2,1,0:T(8,128)(2,1)S(1)} %get-tuple-element.72), channel_id=1, source_target_pairs={{0,4},{1,5},{2,6},{3,7},{4,8},{5,9},{6,10},{7,11},{8,12},{9,13},{1... | collective-permute-start | bytes 688136 | tf_op jit(solution)/shard_map/scatter/ppermute | solution.py:20
  139.0 6.4 %collective-permute-start.30 = (bf16[2,16,896]{2,1,0:T(8,128)(2,1)S(1)}, bf16[2,16,896]{2,1,0:T(8,128)(2,1)S(1)}, u32[]{:S(2)}, u32[]{:S(2)}) collective-permute-start(bf16[2,16,896]{2,1,0:T(8,128)(2,1)S(1)} %get-tuple-element.74), channel_id=1, source_target_pairs={{0,12},{1,13},{2,14},{3,15},{4,0},{5,1},{6,2},{7,3},{8,4},{9,5},{1... | collective-permute-start | bytes 172040 | tf_op jit(solution)/shard_map/scatter/ppermute | solution.py:20
  139.7 6.3 %collective-permute-start.31 = (bf16[2,16,896]{2,1,0:T(8,128)(2,1)S(1)}, bf16[2,16,896]{2,1,0:T(8,128)(2,1)S(1)}, u32[]{:S(2)}, u32[]{:S(2)}) collective-permute-start(bf16[2,16,896]{2,1,0:T(8,128)(2,1)S(1)} %get-tuple-element.75), channel_id=1, source_target_pairs={{0,8},{1,9},{2,10},{3,11},{4,12},{5,13},{6,14},{7,15},{8,0},{9,1},... | collective-permute-start | bytes 172040 | tf_op jit(solution)/shard_map/scatter/ppermute | solution.py:20
  (26 other events, 216.4 us)
Sparse Core Ops, SparseCore 0:
  91.2 72.4 all-reduce.2

commit v2 on v1

v2 whole, which is shorter than its diff:
```python
import jax
import jax.numpy as jnp
from jax import lax
from jax.experimental import pallas as pl
from jax.experimental.pallas import tpu as pltpu
from jax.sharding import PartitionSpec as P

HD = 128
SPAN = 64
SIDE = 4
SUB = 16
NT = 16
STEP = 4
VMEM_LIMIT = 20 * 1024 * 1024
ATTEND_LIMIT = 36 * 1024 * 1024
F32 = jnp.float32
BF16 = jnp.bfloat16


def along_x(value, step):
    pairs = [(i, ((i // SIDE + step) % SIDE) * SIDE + i % SIDE) for i in range(SIDE * SIDE)]
    return lax.ppermute(value, "enc", pairs)


def along_y(value, step):
    pairs = [(i, (i // SIDE) * SIDE + (i + step) % SIDE) for i in range(SIDE * SIDE)]
    return lax.ppermute(value, "enc", pairs)


def place():
    own = lax.axis_index("enc")
    return own, lax.div(own, SIDE), lax.rem(own, SIDE)


def apart(here, there):
    return lax.rem(here - there + SIDE, SIDE)


def my_slots(owner, slot, own):
    count = jnp.int32(0)
    first = jnp.int32(0)
    second = jnp.int32(0)
    for t in range(NT):
        hit = owner[t // 2, t % 2] == own
        tile = slot[t // 2, t % 2]
        first = jnp.where(hit & (count == 0), tile, first)
        second = jnp.where(hit & (count == 1), tile, second)
        count = count + hit.astype(jnp.int32)
    return first, second


def named(owner, x, y):
    found = []
    for t in range(NT):
        o = owner[t // 2, t % 2]
        rank = jnp.int32(0)
        for e in range(t):
            rank = rank + (owner[e // 2, e % 2] == o).astype(jnp.int32)
        found.append((apart(x, lax.div(o, SIDE)), apart(y, lax.rem(o, SIDE)), rank))
    return found


def sub_row(at, base):
    return pl.ds(pl.multiple_of(base + lax.rem(at, SIDE) * SUB, SUB), SUB)


def split_kernel(owner, slot, tiles, *outs):
    own, x, y = place()
    for r, tile in enumerate(my_slots(owner, slot, own)):
        for k in range(SIDE):
            outs[k][r] = tiles[tile, sub_row(x + k, 0), :]
            outs[SIDE + k][r] = tiles[tile, sub_row(y + k, SIDE * SUB), :]


def compact_kernel(owner, *refs):
    in_a, in_b = refs[:SIDE], refs[SIDE : 2 * SIDE]
    out_a, out_b = refs[2 * SIDE :]
    _, x, y = place()
    for t, (dx, dy, rank) in enumerate(named(owner, x, y)):
        for step in range(SIDE):

            @pl.when(dy == step)
            def _(t=t, step=step, at=dx * 2 + rank):
                out_a[t] = in_a[step][at]

            @pl.when(dx == step)
            def _(t=t, step=step, at=dy * 2 + rank):
                out_b[t] = in_b[step][at]


def expand_kernel(owner, *refs):
    ins, outs = refs[: 2 * SIDE], refs[2 * SIDE :]
    out_a, out_b = outs[:SIDE], outs[SIDE:]
    _, x, y = place()
    for out in outs:
        out[...] = jnp.zeros_like(out)
    for t, (dx, dy, rank) in enumerate(named(owner, x, y)):
        total_a = sum(ref[t].astype(F32) for ref in ins[:SIDE]).astype(BF16)
        total_b = sum(ref[t].astype(F32) for ref in ins[SIDE:]).astype(BF16)
        for step in range(SIDE):

            @pl.when(dy == step)
            def _(step=step, at=dx * 2 + rank, total=total_a):
                out_a[step][at] = total

            @pl.when(dx == step)
            def _(step=step, at=dy * 2 + rank, total=total_b):
                out_b[step][at] = total


def owners_sum_kernel(*refs):
    in_a, in_b = refs[:SIDE], refs[SIDE : 2 * SIDE]
    out_a, out_b = refs[2 * SIDE : 3 * SIDE], refs[3 * SIDE :]
    for ins, outs in ((in_a, out_a), (in_b, out_b)):
        for k in range(SIDE):
            for r in range(2):
                outs[k][r] = sum(ref[k * 2 + r].astype(F32) for ref in ins).astype(BF16)


def tiles_kernel(owner, slot, *refs):
    in_a, in_b, out = refs[:SIDE], refs[SIDE : 2 * SIDE], refs[2 * SIDE]
    own, x, y = place()
    out[...] = jnp.zeros_like(out)
    for r, tile in enumerate(my_slots(owner, slot, own)):
        for k in range(SIDE):
            out[tile, sub_row(x + k, 0), :] += in_a[k][r].astype(F32)
            out[tile, sub_row(y + k, SIDE * SUB), :] += in_b[k][r].astype(F32)


def dot(a, b, a_dim, b_dim):
    return lax.dot_general(a, b, (((a_dim,), (b_dim,)), ((), ())), preferred_element_type=F32)


def attention_kernel(length, *refs):
    ins, (q_ref, up_ref, w_ref) = refs[: 2 * SIDE], refs[2 * SIDE : 2 * SIDE + 3]
    ctx_ref, qg_ref = refs[11:13]
    outs, g_ref, acc = refs[13 : 13 + 2 * SIDE], refs[-2], refs[-1]
    step = pl.program_id(0)
    spans = q_ref.shape[0] // SPAN
    columns = q_ref.shape[1]
    heads = columns // HD
    keys = 2 * 2 * SIDE * SUB
    _, x, y = place()
    near = jnp.concatenate(
        [ref[s * 2 + j] for s in range(spans) for j in range(2) for ref in ins], axis=0
    )
    both = dot(near, w_ref[...], 1, 0).astype(BF16)

    def tokens(s):
        return slice(s * SPAN, (s + 1) * SPAN)

    def head(h):
        return slice(h * HD, (h + 1) * HD)

    def key(s, h):
        return both[s * keys : (s + 1) * keys, h * HD : (h + 1) * HD]

    def value(s, h):
        return both[s * keys : (s + 1) * keys, columns + h * HD : columns + (h + 1) * HD]

    units = [(s, h) for s in range(spans) for h in range(heads)]
    scale = 1.0 / HD**0.5
    score = [dot(q_ref[tokens(s), head(h)], key(s, h), 1, 1) for s, h in units]
    dprobs = [dot(up_ref[tokens(s), head(h)], value(s, h), 1, 1) for s, h in units]
    score = jnp.concatenate(score, axis=0) * scale
    dprobs = jnp.concatenate(dprobs, axis=0)
    row = lax.broadcasted_iota(jnp.int32, (1, keys), 1)
    lower = (row // (SIDE * SUB)) % 2
    block = (jnp.where(lower == 0, x, y) - (row // SUB) % SIDE + SIDE) % SIDE
    position = lower * (SIDE * SUB) + block * SUB + row % SUB
    visible = []
    for s in range(spans):
        span = step * spans + s
        limit = jnp.where(row < keys // 2, length[span, 0], length[span, 1])
        visible.append(jnp.broadcast_to(position < limit, (heads * SPAN, keys)))
    visible = jnp.concatenate(visible, axis=0)
    weights = jnp.where(visible, jnp.exp(score), 0.0)
    attention = weights / jnp.sum(weights, axis=-1, keepdims=True)
    attention_b = attention.astype(BF16)
    inner = jnp.sum(attention * dprobs, axis=-1, keepdims=True)
    dscore = (attention * (dprobs - inner) * scale).astype(BF16)
    grads = []
    for s in range(spans):
        key_grads, value_grads = [], []
        for h in range(heads):
            rows = tokens(s * heads + h)
            ctx_ref[tokens(s), head(h)] = dot(attention_b[rows], value(s, h), 1, 0).astype(BF16)
            qg_ref[tokens(s), head(h)] = dot(dscore[rows], key(s, h), 1, 0).astype(BF16)
            key_grads.append(dot(dscore[rows], q_ref[tokens(s), head(h)], 0, 0).astype(BF16))
            value_grads.append(dot(attention_b[rows], up_ref[tokens(s), head(h)], 0, 0).astype(BF16))
        grads.append(jnp.concatenate(key_grads + value_grads, axis=1))
    grads = jnp.concatenate(grads, axis=0)
    partial = dot(grads, w_ref[...], 1, 1).astype(BF16)
    for s in range(spans):
        for j in range(2):
            for k, out in enumerate(outs):
                low = s * keys + (j * 2 * SIDE + k) * SUB
                out[s * 2 + j] = partial[low : low + SUB]
    gain = dot(near, grads, 0, 0)

    @pl.when(step == 0)
    def _():
        acc[...] = gain

    @pl.when(step > 0)
    def _():
        acc[...] += gain

    @pl.when(step == pl.num_programs(0) - 1)
    def _():
        g_ref[0] = acc[:, :columns].astype(BF16)
        g_ref[1] = acc[:, columns:].astype(BF16)


def query_weight_kernel(rows_0, rows_1, grads, near_e, out):
    z = pl.program_id(0)
    cut = rows_0.shape[1]
    rest = near_e.shape[1] // SIDE
    at = pl.ds(pl.multiple_of(z * rest, 32), rest)
    for core, rows in enumerate((rows_0, rows_1)):
        out[0, core, :cut] = dot(rows[...], grads[...], 0, 0).astype(BF16)
        out[0, core, cut:] = near_e[core, at]


def query_weight(queries_in, query_grad, near_e):
    tokens, width = queries_in.shape
    columns = query_grad.shape[1]
    cut = width // (2 * SIDE)
    rest = near_e.shape[1] // SIDE
    return pl.pallas_call(
        query_weight_kernel,
        grid=(SIDE,),
        in_specs=[
            pl.BlockSpec((tokens, cut), lambda z: (0, z)),
            pl.BlockSpec((tokens, cut), lambda z: (0, SIDE + z)),
            pl.BlockSpec((tokens, columns), lambda z: (0, 0)),
            pl.BlockSpec(near_e.shape, lambda z: (0, 0, 0)),
        ],
        out_specs=pl.BlockSpec((1, 2, cut + rest, columns), lambda z: (z, 0, 0, 0)),
        out_shape=pltpu.HBM((SIDE, 2, cut + rest, columns), BF16),
        compiler_params=pltpu.CompilerParams(vmem_limit_bytes=VMEM_LIMIT),
    )(queries_in, queries_in, query_grad, near_e)


def weights_kernel(chunks, out_q, out_k, out_v, bring, hold, arrive, leave):
    cut = out_q.shape[0] // (2 * SIDE)
    rest = out_k.shape[0] // SIDE
    count = chunks.shape[0]
    arrivals = [
        pltpu.make_async_copy(chunks.at[slot], bring.at[slot], arrive.at[slot])
        for slot in range(count)
    ]
    for copy in arrivals:
        copy.start()
    copies = []
    for slot in range(count):
        z, core = slot // 2, slot % 2
        out_e = out_v if core else out_k
        arrivals[slot].wait()
        hold[slot] = bring[slot].astype(F32)
        copies += [
            pltpu.make_async_copy(
                hold.at[slot, pl.ds(0, cut)],
                out_q.at[pl.ds((core * SIDE + z) * cut, cut)],
                leave.at[slot, 0],
            ),
            pltpu.make_async_copy(
                hold.at[slot, pl.ds(cut, rest)], out_e.at[pl.ds(z * rest, rest)], leave.at[slot, 1]
            ),
        ]
        copies[-2].start()
        copies[-1].start()
    for copy in copies:
        copy.wait()


def weight_outputs(chunks, shapes):
    return pl.pallas_call(
        weights_kernel,
        out_shape=[jax.ShapeDtypeStruct(shape, F32) for shape in shapes],
        in_specs=[pl.BlockSpec(memory_space=pl.ANY)],
        out_specs=[pl.BlockSpec(memory_space=pl.ANY)] * 3,
        scratch_shapes=[
            pltpu.VMEM(chunks.shape, BF16),
            pltpu.VMEM(chunks.shape, F32),
            pltpu.SemaphoreType.DMA((2 * SIDE,)),
            pltpu.SemaphoreType.DMA((2 * SIDE, 2)),
        ],
        compiler_params=pltpu.CompilerParams(vmem_limit_bytes=VMEM_LIMIT),
    )(chunks)


def call(kernel, scalars, ins, outs, make=jax.ShapeDtypeStruct):
    vmem = pl.BlockSpec(memory_space=pltpu.VMEM)
    return pl.pallas_call(
        kernel,
        out_shape=[make(shape, dtype) for shape, dtype in outs],
        in_specs=[pl.BlockSpec(memory_space=pltpu.SMEM)] * len(scalars) + [vmem] * len(ins),
        out_specs=[vmem] * len(outs),
        compiler_params=pltpu.CompilerParams(vmem_limit_bytes=VMEM_LIMIT),
    )(*scalars, *ins)


def attend(key_length, parts, query, upstream, weight):
    spans = key_length.shape[0]
    width = weight.shape[0]
    columns = query.shape[1]
    tile_block = pl.BlockSpec((2 * STEP, SUB, width), lambda c, *_: (c, 0, 0))
    token_block = pl.BlockSpec((STEP * SPAN, columns), lambda c, *_: (c, 0))
    return pl.pallas_call(
        attention_kernel,
        grid_spec=pltpu.PrefetchScalarGridSpec(
            num_scalar_prefetch=1,
            grid=(spans // STEP,),
            in_specs=[tile_block] * (2 * SIDE)
            + [token_block] * 2
            + [pl.BlockSpec(weight.shape, lambda c, *_: (0, 0))],
            out_specs=[token_block] * 2
            + [tile_block] * (2 * SIDE)
            + [pl.BlockSpec((2, width, columns), lambda c, *_: (0, 0, 0))],
            scratch_shapes=[pltpu.VMEM(weight.shape, F32)],
        ),
        out_shape=[jax.ShapeDtypeStruct((spans * SPAN, columns), BF16)] * 2
        + [pltpu.HBM((NT, SUB, width), BF16)] * (2 * SIDE)
        + [jax.ShapeDtypeStruct((2, width, columns), BF16)],
        compiler_params=pltpu.CompilerParams(vmem_limit_bytes=ATTEND_LIMIT),
    )(key_length, *parts, query, upstream, weight)


def body(
    queries_in,
    w_query,
    w_key,
    w_value,
    tiles,
    neighbour_owner,
    neighbour_slot,
    key_length,
    grad_context,
):
    width = tiles.shape[2]
    steps = range(1, SIDE)
    pair = ((2, SUB, width), BF16)
    line = ((2 * SIDE, SUB, width), BF16)
    with jax.named_scope("gather"):
        cut = call(split_kernel, (neighbour_owner, neighbour_slot), (tiles,), [pair] * 8)
        row_a = [cut[0]] + [along_x(cut[k], k) for k in steps]
        row_b = [cut[SIDE]] + [along_y(cut[SIDE + k], k) for k in steps]
        line_a = jnp.concatenate(row_a, axis=0)
        line_b = jnp.concatenate(row_b, axis=0)
        all_a = [line_a] + [along_y(line_a, k) for k in steps]
        all_b = [line_b] + [along_x(line_b, k) for k in steps]
        group = ((NT, SUB, width), BF16)
        own_a, own_b = call(compact_kernel, (neighbour_owner,), all_a + all_b, [group] * 2)
        parts = [own_a] + [along_x(own_a, k) for k in steps]
        parts += [own_b] + [along_y(own_b, k) for k in steps]
    query = jnp.dot(queries_in, w_query, preferred_element_type=F32).astype(BF16)
    weight = jnp.concatenate([w_key, w_value], axis=1)
    with jax.named_scope("attend"):
        context, query_grad, *sends, near_e = attend(
            key_length, parts, query, grad_context, weight
        )
    with jax.named_scope("scatter"):
        back = [sends[0]] + [along_x(sends[k], -k) for k in steps]
        back += [sends[SIDE]] + [along_y(sends[SIDE + k], -k) for k in steps]
    with jax.named_scope("weights"):
        local = query_weight(queries_in, query_grad, near_e)
        local = local.reshape(-1, *local.shape[2:])
        share = lax.psum_scatter(local, "dp", scatter_dimension=0, tiled=True)
    with jax.named_scope("scatter"):
        wide = call(expand_kernel, (neighbour_owner,), back, [line] * 8, pltpu.HBM)
    with jax.named_scope("scatter"):
        home_a = [wide[0]] + [along_y(wide[k], -k) for k in steps]
        home_b = [wide[SIDE]] + [along_x(wide[SIDE + k], -k) for k in steps]
    share, home_a[1] = lax.optimization_barrier((share, home_a[1]))
    with jax.named_scope("weights"):
        chunks = lax.all_gather(share, "dp", tiled=True)
        chunks = pltpu.with_memory_space_constraint(chunks, pltpu.HBM)
        grads = weight_outputs(chunks, (w_query.shape, w_key.shape, w_value.shape))
    with jax.named_scope("scatter"):
        mine = call(owners_sum_kernel, (), home_a + home_b, [pair] * 8)
        last_a = [mine[0]] + [along_x(mine[k], -k) for k in steps]
        last_b = [mine[SIDE]] + [along_y(mine[SIDE + k], -k) for k in steps]
        (grad_tiles,) = call(
            tiles_kernel,
            (neighbour_owner, neighbour_slot),
            last_a + last_b,
            [(tiles.shape, F32)],
        )
    return (context, *grads, grad_tiles)


def solution(mesh):
    in_specs = (
        P("dp", None),
        P(None, "enc"),
        P(None, "enc"),
        P(None, "enc"),
        P(("dp", "enc"), None, None),
        P("dp", None),
        P("dp", None),
        P("dp", None),
        P("dp", "enc"),
    )
    out_specs = (
        P("dp", "enc"),
        P(None, "enc"),
        P(None, "enc"),
        P(None, "enc"),
        P(("dp", "enc"), None, None),
    )
    return jax.shard_map(body, mesh=mesh, in_specs=in_specs, out_specs=out_specs, check_vma=False)
```

time: 177 us -> 166 us (0.938)
  starting transfers between devices: 52.1 us -> 43 us
  waiting for transfers between devices: 63.5 us -> 71 us
  local copies, waits for them, and re-layouts: 11.3 us -> 4.9 us
  matrix products: 6.22 us -> 3.43 us
    psum x1 -> x0, waiting for transfers between devices: 10.9 us -> none  [body(): lax.psum(g, 'dp').astype(F32)]
    ppermute x18, starting transfers between devices: 27.3 us -> 17.8 us  [along_y(): return lax.ppermute(value, 'enc', pairs)]
    ppermute x18, waiting for transfers between devices: 23.3 us -> 32.7 us  [along_y(): return lax.ppermute(value, 'enc', pairs)]
    pallas_call x1, Pallas kernels: 20.1 us -> 11.3 us  [attend(): pl.pallas_call(attention_kernel, grid_spec=pltpu.PrefetchScalarGridSpec(n...]
    pallas_call x5 -> x7, Pallas kernels: 7.47 us -> 15.8 us  [the longest x5 8.52 us: call(): pl.pallas_call(kernel, out_shape=[make(shape, dtype) for shape, dtype in...]
    ppermute x18, waiting for transfers between devices: 29.3 us -> 36.9 us  [along_x(): return lax.ppermute(value, 'enc', pairs)]
    unnamed x52 -> x29, local copies, waits for them, and re-layouts: 11.3 us -> 4.87 us
    dot_general x1 -> x0, matrix products: 2.64 us -> none  [body(): jnp.dot(queries_in.T, query_grad, preferred_element_type=F32).astype(BF16)]
  transfers between devices with their start and end apart: 37 -> 38, of which waited for: 21 -> 27; matrix products, arithmetic and copies ran while one was open for 2% -> 3% of each run, Pallas kernels for 3% -> 4%
where the time goes in v2:
time: 166 us; the launch traced here: 165 us
  waiting for transfers between devices  71 us (43%)
  starting transfers between devices  43 us (26%)
  Pallas kernels  27.1 us (16%)
  between operations  14.2 us (9%)
  local copies, waits for them, and re-layouts  4.9 us (3%)
  matrix products  3.43 us (2%)
    ppermute x18, waiting for transfers between devices, along_x(): return lax.ppermute(value, 'enc', pairs)  36.9 us
    ppermute x18, waiting for transfers between devices, along_y(): return lax.ppermute(value, 'enc', pairs)  32.7 us
    ppermute x18, starting transfers between devices, along_x(): return lax.ppermute(value, 'enc', pairs)  25.1 us
    ppermute x18, starting transfers between devices, along_y(): return lax.ppermute(value, 'enc', pairs)  17.8 us
    pallas_call x1, Pallas kernels, attend(): pl.pallas_call(attention_kernel, grid_spec=pltpu.PrefetchScalarGridSpec(n...  11.3 us
    pallas_call x5, Pallas kernels, call(): pl.pallas_call(kernel, out_shape=[make(shape, dtype) for shape, dtype in...  8.52 us
    unnamed x29, local copies, waits for them, and re-layouts  4.87 us
    pallas_call x1, Pallas kernels, weight_outputs(): pl.pallas_call(weights_kernel, out_shape=[jax.ShapeDtypeStruct(shape, F32...  3.8 us
  transfers between devices with their start and end apart: 38, of which 27 were waited for; matrix products, arithmetic and copies ran while one was open for 3% of the time, Pallas kernels for 4%

profile of v2, /device:TPU:0, one launch (start us, length us, event | category | flops | bytes accessed | tf_op | source)
XLA Modules:
  0.0 164.9 jit_solution(6461318090588662039)
XLA Ops:
  10.8 1.6 collective-permute-start
  12.5 2.7 %collective-permute-start.1 = (bf16[2,16,896]{2,1,0:T(8,128)(2,1)S(1)}, bf16[2,16,896]{2,1,0:T(8,128)(2,1)S(1)}, u32[]{:S(2)}, u32[]{:S(2)}) collective-permute-start(bf16[2,16,896]{2,1,0:T(8,128)(2,1)S(1)} %get-tuple-element.49), channel_id=1, source_target_pairs={{0,8},{1,9},{2,10},{3,11},{4,12},{5,13},{6,14},{7,15},{8,0},{9,1},... | collective-permute-start | bytes 172040 | tf_op jit(solution)/shard_map/gather/ppermute | solution.py:22
  18.2 2.9 %collective-permute-start.7 = (bf16[2,16,896]{2,1,0:T(8,128)(2,1)S(1)}, bf16[2,16,896]{2,1,0:T(8,128)(2,1)S(1)}, u32[]{:S(2)}, u32[]{:S(2)}) collective-permute-start(bf16[2,16,896]{2,1,0:T(8,128)(2,1)S(1)} %get-tuple-element.53), channel_id=1, source_target_pairs={{0,2},{1,3},{2,0},{3,1},{4,6},{5,7},{6,4},{7,5},{8,10},{9,11},{10,... | collective-permute-start | bytes 172040 | tf_op jit(solution)/shard_map/gather/ppermute | solution.py:27
  23.9 2.8 %collective-permute-done.8 = bf16[2,16,896]{2,1,0:T(8,128)(2,1)S(1)} collective-permute-done((bf16[2,16,896]{2,1,0:T(8,128)(2,1)S(1)}, bf16[2,16,896]{2,1,0:T(8,128)(2,1)S(1)}, u32[]{:S(2)}, u32[]{:S(2)}) %collective-permute-start.8) | collective-permute-done | bytes 57376 | tf_op jit(solution)/shard_map/gather/ppermute | solution.py:27
  26.9 2.5 %collective-permute-start.10 = (bf16[8,16,896]{2,1,0:T(8,128)(2,1)S(1)}, bf16[8,16,896]{2,1,0:T(8,128)(2,1)S(1)}, u32[]{:S(2)}, u32[]{:S(2)}) collective-permute-start(bf16[8,16,896]{2,1,0:T(8,128)(2,1)S(1)} %constant_dynamic-update-slice_fusion.4.refs_4_), channel_id=1, source_target_pairs={{0,8},{1,9},{2,10},{3,11},{4,12},{5,13},{6,14},{7,15},{8,0},{9,1},... | collective-permute-start | bytes 688136 | tf_op jit(solution)/shard_map/gather/ppermute | solution.py:22
  29.5 2.6 %collective-permute-start.5 = (bf16[8,16,896]{2,1,0:T(8,128)(2,1)S(1)}, bf16[8,16,896]{2,1,0:T(8,128)(2,1)S(1)}, u32[]{:S(2)}, u32[]{:S(2)}) collective-permute-start(bf16[8,16,896]{2,1,0:T(8,128)(2,1)S(1)} %constant_dynamic-update-slice_fusion.refs_0_), channel_id=1, source_target_pairs={{0,3},{1,0},{2,1},{3,2},{4,7},{5,4},{6,5},{7,6},{8,11},{9,8},{10,9... | collective-permute-start | bytes 688136 | tf_op jit(solution)/shard_map/gather/ppermute | solution.py:27
  33.8 1.6 collective-permute-done.10.refs_6_
  35.4 2.4 %collective-permute-done.9.refs_5_ = bf16[8,16,896]{2,1,0:T(8,128)(2,1)S(1)} collective-permute-done((bf16[8,16,896]{2,1,0:T(8,128)(2,1)S(1)}, bf16[8,16,896]{2,1,0:T(8,128)(2,1)S(1)}, u32[]{:S(2)}, u32[]{:S(2)}) %collective-permute-start.9) | collective-permute-done | bytes 229408 | tf_op jit(solution)/shard_map/gather/ppermute | solution.py:22
  40.0 2.4 %collective-permute-done.3.refs_1_ = bf16[8,16,896]{2,1,0:T(8,128)(2,1)S(1)} collective-permute-done((bf16[8,16,896]{2,1,0:T(8,128)(2,1)S(1)}, bf16[8,16,896]{2,1,0:T(8,128)(2,1)S(1)}, u32[]{:S(2)}, u32[]{:S(2)}) %collective-permute-start.3) | collective-permute-done | bytes 229408 | tf_op jit(solution)/shard_map/gather/ppermute | solution.py:27
  42.3 2.0 %gather.3 = (bf16[16,16,896]{2,1,0:T(8,128)(2,1)S(1)}, bf16[16,16,896]{2,1,0:T(8,128)(2,1)S(1)}) custom-call(s32[8,2]{1,0:T(8,128)S(1)} %copy.23.owner, bf16[8,16,896]{2,1,0:T(8,128)(2,1)S(1)} %constant_dynamic-update-slice_fusion.refs_0_, bf16[8,16,896]{2,1,0:T(8,128)(2,1)S(1)} %collective-permute-done.3.refs_1_, ...), custom_call_target="tpu_custom_call" | custom-call | tf_op jit(solution)/shard_map/gather/pallas_call | solution.py:295
  44.3 3.1 %collective-permute-start.14 = (bf16[16,16,896]{2,1,0:T(8,128)(2,1)S(1)}, bf16[16,16,896]{2,1,0:T(8,128)(2,1)S(1)}, u32[]{:S(2)}, u32[]{:S(2)}) collective-permute-start(bf16[16,16,896]{2,1,0:T(8,128)(2,1)S(1)} %get-tuple-element.55.refs_0_), channel_id=1, source_target_pairs={{0,12},{1,13},{2,14},{3,15},{4,0},{5,1},{6,2},{7,3},{8,4},{9,5},{1... | collective-permute-start | bytes 1376264 | tf_op jit(solution)/shard_map/gather/ppermute | solution.py:22
  51.5 10.2 %collective-permute-done.14.refs_3_ = bf16[16,16,896]{2,1,0:T(8,128)(2,1)S(1)} collective-permute-done((bf16[16,16,896]{2,1,0:T(8,128)(2,1)S(1)}, bf16[16,16,896]{2,1,0:T(8,128)(2,1)S(1)}, u32[]{:S(2)}, u32[]{:S(2)}) %collective-permute-start.14) | collective-permute-done | bytes 458784 | tf_op jit(solution)/shard_map/gather/ppermute | solution.py:22
  61.7 3.4 %convolution_convert_fusion.refs_8_ = bf16[512,256]{1,0:T(8,128)(2,1)S(1)} fusion(bf16[512,4096]{1,0:T(8,128)(2,1)} %rows_1.1, bf16[4096,256]{1,0:T(8,128)(2,1)S(1)} %copy-done), kind=kOutput, calls=%fused_computation | convolution fusion | flops 1073872896 | bytes 6553600 | tf_op jit(solution)/shard_map/dot_general | solution.py:357
  65.1 1.6 collective-permute-done.12.refs_1_
  66.7 4.6 %collective-permute-done.15.refs_5_ = bf16[16,16,896]{2,1,0:T(8,128)(2,1)S(1)} collective-permute-done((bf16[16,16,896]{2,1,0:T(8,128)(2,1)S(1)}, bf16[16,16,896]{2,1,0:T(8,128)(2,1)S(1)}, u32[]{:S(2)}, u32[]{:S(2)}) %collective-permute-start.15) | collective-permute-done | bytes 458784 | tf_op jit(solution)/shard_map/gather/ppermute | solution.py:27
  71.4 11.3 %attend.1 = (bf16[512,256]{1,0:T(8,128)(2,1)}, bf16[512,256]{1,0:T(8,128)(2,1)S(1)}, bf16[16,16,896]{2,1,0:T(8,128)(2,1)}, bf16[16,16,896]{2,1,0:T(8,128)(2,1)},...) custom-call(s32[8,2]{1,0:T(8,128)S(1)} %copy.24.length, ...), custom_call_target="tpu_custom_call" | custom-call | tf_op jit(solution)/shard_map/attend/pallas_call | solution.py:310
  82.7 3.5 %weights.2 = bf16[4,2,736,256]{3,2,1,0:T(8,128)(2,1)} custom-call(bf16[512,4096]{1,0:T(8,128)(2,1)S(1)} %copy-done.1, bf16[512,4096]{1,0:T(8,128)(2,1)S(1)} %copy-done.1, bf16[512,256]{1,0:T(8,128)(2,1)S(1)} %get-tuple-element.58.grads, bf16[2,896,256]{2,1,0:T(8,128)(2,1)S(1)} %get-tuple-element.59.near_e), custom_call_target="tpu_custom_call" | custom-call | tf_op jit(solution)/shard_map/weights/pallas_call | solution.py:230
  86.3 3.7 %collective-permute-start.18 = (bf16[16,16,896]{2,1,0:T(8,128)(2,1)}, bf16[16,16,896]{2,1,0:T(8,128)(2,1)S(1)}, u32[]{:S(2)}, u32[]{:S(2)}) collective-permute-start(bf16[16,16,896]{2,1,0:T(8,128)(2,1)} %get-tuple-element.61), channel_id=1, source_target_pairs={{0,12},{1,13},{2,14},{3,15},{4,0},{5,1},{6,2},{7,3},{8,4},{9,5},{1... | collective-permute-start | bytes 1376264 | tf_op jit(solution)/shard_map/scatter/ppermute | solution.py:22
  91.8 10.3 %collective-permute-done.18.refs_1_ = bf16[16,16,896]{2,1,0:T(8,128)(2,1)S(1)} collective-permute-done((bf16[16,16,896]{2,1,0:T(8,128)(2,1)}, bf16[16,16,896]{2,1,0:T(8,128)(2,1)S(1)}, u32[]{:S(2)}, u32[]{:S(2)}) %collective-permute-start.18) | collective-permute-done | bytes 458784 | tf_op jit(solution)/shard_map/scatter/ppermute | solution.py:22
  102.3 2.6 %collective-permute-done.20.refs_3_ = bf16[16,16,896]{2,1,0:T(8,128)(2,1)S(1)} collective-permute-done((bf16[16,16,896]{2,1,0:T(8,128)(2,1)}, bf16[16,16,896]{2,1,0:T(8,128)(2,1)S(1)}, u32[]{:S(2)}, u32[]{:S(2)}) %collective-permute-start.20) | collective-permute-done | bytes 458784 | tf_op jit(solution)/shard_map/scatter/ppermute | solution.py:22
  105.3 6.5 %collective-permute-done.23.refs_7_ = bf16[16,16,896]{2,1,0:T(8,128)(2,1)S(1)} collective-permute-done((bf16[16,16,896]{2,1,0:T(8,128)(2,1)S(1)}, bf16[16,16,896]{2,1,0:T(8,128)(2,1)S(1)}, u32[]{:S(2)}, u32[]{:S(2)}) %collective-permute-start.23) | collective-permute-done | bytes 458784 | tf_op jit(solution)/shard_map/scatter/ppermute | solution.py:27
  111.8 3.4 %scatter.3 = (bf16[8,16,896]{2,1,0:T(8,128)(2,1)}, bf16[8,16,896]{2,1,0:T(8,128)(2,1)}, bf16[8,16,896]{2,1,0:T(8,128)(2,1)}, bf16[8,16,896]{2,1,0:T(8,128)(2,1)}...) custom-call(s32[8,2]{1,0:T(8,128)S(1)} %copy.23.owner, ...), custom_call_target="tpu_custom_call" | custom-call | tf_op jit(solution)/shard_map/scatter/pallas_call | solution.py:295
  115.9 5.6 %collective-permute-done.24.refs_1_ = bf16[8,16,896]{2,1,0:T(8,128)(2,1)S(1)} collective-permute-done((bf16[8,16,896]{2,1,0:T(8,128)(2,1)}, bf16[8,16,896]{2,1,0:T(8,128)(2,1)S(1)}, u32[]{:S(2)}, u32[]{:S(2)}) %collective-permute-start.24) | collective-permute-done | bytes 229408 | tf_op jit(solution)/shard_map/scatter/ppermute | solution.py:27
  122.9 2.9 %collective-permute-start.25 = (bf16[8,16,896]{2,1,0:T(8,128)(2,1)}, bf16[8,16,896]{2,1,0:T(8,128)(2,1)S(1)}, u32[]{:S(2)}, u32[]{:S(2)}) collective-permute-start(bf16[8,16,896]{2,1,0:T(8,128)(2,1)} %get-tuple-element.75), channel_id=1, source_target_pairs={{0,2},{1,3},{2,0},{3,1},{4,6},{5,7},{6,4},{7,5},{8,10},{9,11},{10,... | collective-permute-start | bytes 688136 | tf_op jit(solution)/shard_map/scatter/ppermute | solution.py:27
  126.4 2.7 %collective-permute-start.27 = (bf16[8,16,896]{2,1,0:T(8,128)(2,1)}, bf16[8,16,896]{2,1,0:T(8,128)(2,1)S(1)}, u32[]{:S(2)}, u32[]{:S(2)}) collective-permute-start(bf16[8,16,896]{2,1,0:T(8,128)(2,1)} %get-tuple-element.78), channel_id=1, source_target_pairs={{0,12},{1,13},{2,14},{3,15},{4,0},{5,1},{6,2},{7,3},{8,4},{9,5},{1... | collective-permute-start | bytes 688136 | tf_op jit(solution)/shard_map/scatter/ppermute | solution.py:22
  131.6 2.4 %collective-permute-done.26.refs_3_ = bf16[8,16,896]{2,1,0:T(8,128)(2,1)S(1)} collective-permute-done((bf16[8,16,896]{2,1,0:T(8,128)(2,1)}, bf16[8,16,896]{2,1,0:T(8,128)(2,1)S(1)}, u32[]{:S(2)}, u32[]{:S(2)}) %collective-permute-start.26) | collective-permute-done | bytes 229408 | tf_op jit(solution)/shard_map/scatter/ppermute | solution.py:27
  134.0 1.6 collective-permute-done.27.refs_5_
  136.9 2.4 %collective-permute-done.29.refs_7_ = bf16[8,16,896]{2,1,0:T(8,128)(2,1)S(1)} collective-permute-done((bf16[8,16,896]{2,1,0:T(8,128)(2,1)}, bf16[8,16,896]{2,1,0:T(8,128)(2,1)S(1)}, u32[]{:S(2)}, u32[]{:S(2)}) %collective-permute-start.29) | collective-permute-done | bytes 229408 | tf_op jit(solution)/shard_map/scatter/ppermute | solution.py:22
  143.9 2.2 %collective-permute-start.33 = (bf16[2,16,896]{2,1,0:T(8,128)(2,1)S(1)}, bf16[2,16,896]{2,1,0:T(8,128)(2,1)S(1)}, u32[]{:S(2)}, u32[]{:S(2)}) collective-permute-start(bf16[2,16,896]{2,1,0:T(8,128)(2,1)S(1)} %get-tuple-element.86), channel_id=1, source_target_pairs={{0,3},{1,0},{2,1},{3,2},{4,7},{5,4},{6,5},{7,6},{8,11},{9,8},{10,9... | collective-permute-start | bytes 172040 | tf_op jit(solution)/shard_map/scatter/ppermute | solution.py:27
  148.5 3.4 %collective-permute-done.34.refs_6_ = bf16[2,16,896]{2,1,0:T(8,128)(2,1)S(1)} collective-permute-done((bf16[2,16,896]{2,1,0:T(8,128)(2,1)S(1)}, bf16[2,16,896]{2,1,0:T(8,128)(2,1)S(1)}, u32[]{:S(2)}, u32[]{:S(2)}) %collective-permute-start.34) | collective-permute-done | bytes 57376 | tf_op jit(solution)/shard_map/scatter/ppermute | solution.py:27
  152.2 2.1 %scatter.5 = f32[4,128,896]{2,1,0:T(8,128)} custom-call(s32[8,2]{1,0:T(8,128)S(1)} %copy.23.owner, s32[8,2]{1,0:T(8,128)S(1)} %copy.22.slot, bf16[2,16,896]{2,1,0:T(8,128)(2,1)S(1)} %get-tuple-element.81.refs_0_, bf16[2,16,896]{2,1,0:T(8,128)(2,1)S(1)} %collective-permute-done.30.refs_1_, bf16[2,16,896]{2,1,0:T(8,128)(2,1)S(1)} %collective-permute-done.31.refs_2_, ...), custom_call_target="tpu_custom_call" | custom-call | tf_op jit(solution)/shard_map/scatter/pallas_call | solution.py:295
  154.3 3.8 %weights.3 = (f32[4096,256]{1,0:T(8,128)}, f32[896,256]{1,0:T(8,128)}, f32[896,256]{1,0:T(8,128)}) custom-call(bf16[8,736,256]{2,1,0:T(8,128)(2,1)} %all-gather.2.cloned.1.call-done.chunks), custom_call_target="tpu_custom_call" | custom-call | tf_op jit(solution)/shard_map/weights/pallas_call | solution.py:278
  (87 shorter events, 34.0 us)
Async XLA Ops:
  7.2 115.7 %reduce-scatter.2.cloned.1.call-start = ((), (), s32[]{:S(2)}) async-start(), calls=%async_computation.1 | async-start | bytes 3391488 | tf_op jit(solution)/shard_map/weights/reduce_scatter | solution.py:369
  10.8 18.6 %collective-permute-start = (bf16[2,16,896]{2,1,0:T(8,128)(2,1)S(1)}, bf16[2,16,896]{2,1,0:T(8,128)(2,1)S(1)}, u32[]{:S(2)}, u32[]{:S(2)}) collective-permute-start(bf16[2,16,896]{2,1,0:T(8,128)(2,1)S(1)} %get-tuple-element.48), channel_id=1, source_target_pairs={{0,4},{1,5},{2,6},{3,7},{4,8},{5,9},{6,10},{7,11},{8,12},{9,13},{1... | collective-permute-start | bytes 172040 | tf_op jit(solution)/shard_map/gather/ppermute | solution.py:22
  12.5 17.0 %collective-permute-start.1 = (bf16[2,16,896]{2,1,0:T(8,128)(2,1)S(1)}, bf16[2,16,896]{2,1,0:T(8,128)(2,1)S(1)}, u32[]{:S(2)}, u32[]{:S(2)}) collective-permute-start(bf16[2,16,896]{2,1,0:T(8,128)(2,1)S(1)} %get-tuple-element.49), channel_id=1, source_target_pairs={{0,8},{1,9},{2,10},{3,11},{4,12},{5,13},{6,14},{7,15},{8,0},{9,1},... | collective-permute-start | bytes 172040 | tf_op jit(solution)/shard_map/gather/ppermute | solution.py:22
  15.2 14.3 %collective-permute-start.2 = (bf16[2,16,896]{2,1,0:T(8,128)(2,1)S(1)}, bf16[2,16,896]{2,1,0:T(8,128)(2,1)S(1)}, u32[]{:S(2)}, u32[]{:S(2)}) collective-permute-start(bf16[2,16,896]{2,1,0:T(8,128)(2,1)S(1)} %get-tuple-element.50), channel_id=1, source_target_pairs={{0,12},{1,13},{2,14},{3,15},{4,0},{5,1},{6,2},{7,3},{8,4},{9,5},{1... | collective-permute-start | bytes 172040 | tf_op jit(solution)/shard_map/gather/ppermute | solution.py:22
  16.7 5.9 %collective-permute-start.6 = (bf16[2,16,896]{2,1,0:T(8,128)(2,1)S(1)}, bf16[2,16,896]{2,1,0:T(8,128)(2,1)S(1)}, u32[]{:S(2)}, u32[]{:S(2)}) collective-permute-start(bf16[2,16,896]{2,1,0:T(8,128)(2,1)S(1)} %get-tuple-element.52), channel_id=1, source_target_pairs={{0,1},{1,2},{2,3},{3,0},{4,5},{5,6},{6,7},{7,4},{8,9},{9,10},{10,1... | collective-permute-start | bytes 172040 | tf_op jit(solution)/shard_map/gather/ppermute | solution.py:27
  26.7 6.9 %collective-permute-start.11 = (bf16[8,16,896]{2,1,0:T(8,128)(2,1)S(1)}, bf16[8,16,896]{2,1,0:T(8,128)(2,1)S(1)}, u32[]{:S(2)}, u32[]{:S(2)}) collective-permute-start(bf16[8,16,896]{2,1,0:T(8,128)(2,1)S(1)} %constant_dynamic-update-slice_fusion.4.refs_4_), channel_id=1, source_target_pairs={{0,12},{1,13},{2,14},{3,15},{4,0},{5,1},{6,2},{7,3},{8,4},{9,5},{1... | collective-permute-start | bytes 688136 | tf_op jit(solution)/shard_map/gather/ppermute | solution.py:22
  26.9 8.5 %collective-permute-start.10 = (bf16[8,16,896]{2,1,0:T(8,128)(2,1)S(1)}, bf16[8,16,896]{2,1,0:T(8,128)(2,1)S(1)}, u32[]{:S(2)}, u32[]{:S(2)}) collective-permute-start(bf16[8,16,896]{2,1,0:T(8,128)(2,1)S(1)} %constant_dynamic-update-slice_fusion.4.refs_4_), channel_id=1, source_target_pairs={{0,8},{1,9},{2,10},{3,11},{4,12},{5,13},{6,14},{7,15},{8,0},{9,1},... | collective-permute-start | bytes 688136 | tf_op jit(solution)/shard_map/gather/ppermute | solution.py:22
  29.5 8.3 %collective-permute-start.9 = (bf16[8,16,896]{2,1,0:T(8,128)(2,1)S(1)}, bf16[8,16,896]{2,1,0:T(8,128)(2,1)S(1)}, u32[]{:S(2)}, u32[]{:S(2)}) collective-permute-start(bf16[8,16,896]{2,1,0:T(8,128)(2,1)S(1)} %constant_dynamic-update-slice_fusion.4.refs_4_), channel_id=1, source_target_pairs={{0,4},{1,5},{2,6},{3,7},{4,8},{5,9},{6,10},{7,11},{8,12},{9,13},{1... | collective-permute-start | bytes 688136 | tf_op jit(solution)/shard_map/gather/ppermute | solution.py:22
  29.5 9.1 %collective-permute-start.5 = (bf16[8,16,896]{2,1,0:T(8,128)(2,1)S(1)}, bf16[8,16,896]{2,1,0:T(8,128)(2,1)S(1)}, u32[]{:S(2)}, u32[]{:S(2)}) collective-permute-start(bf16[8,16,896]{2,1,0:T(8,128)(2,1)S(1)} %constant_dynamic-update-slice_fusion.refs_0_), channel_id=1, source_target_pairs={{0,3},{1,0},{2,1},{3,2},{4,7},{5,4},{6,5},{7,6},{8,11},{9,8},{10,9... | collective-permute-start | bytes 688136 | tf_op jit(solution)/shard_map/gather/ppermute | solution.py:27
  32.1 7.8 %collective-permute-start.4 = (bf16[8,16,896]{2,1,0:T(8,128)(2,1)S(1)}, bf16[8,16,896]{2,1,0:T(8,128)(2,1)S(1)}, u32[]{:S(2)}, u32[]{:S(2)}) collective-permute-start(bf16[8,16,896]{2,1,0:T(8,128)(2,1)S(1)} %constant_dynamic-update-slice_fusion.refs_0_), channel_id=1, source_target_pairs={{0,2},{1,3},{2,0},{3,1},{4,6},{5,7},{6,4},{7,5},{8,10},{9,11},{10,... | collective-permute-start | bytes 688136 | tf_op jit(solution)/shard_map/gather/ppermute | solution.py:27
  33.7 8.6 %collective-permute-start.3 = (bf16[8,16,896]{2,1,0:T(8,128)(2,1)S(1)}, bf16[8,16,896]{2,1,0:T(8,128)(2,1)S(1)}, u32[]{:S(2)}, u32[]{:S(2)}) collective-permute-start(bf16[8,16,896]{2,1,0:T(8,128)(2,1)S(1)} %constant_dynamic-update-slice_fusion.refs_0_), channel_id=1, source_target_pairs={{0,1},{1,2},{2,3},{3,0},{4,5},{5,6},{6,7},{7,4},{8,9},{9,10},{10,1... | collective-permute-start | bytes 688136 | tf_op jit(solution)/shard_map/gather/ppermute | solution.py:27
  44.3 17.4 %collective-permute-start.14 = (bf16[16,16,896]{2,1,0:T(8,128)(2,1)S(1)}, bf16[16,16,896]{2,1,0:T(8,128)(2,1)S(1)}, u32[]{:S(2)}, u32[]{:S(2)}) collective-permute-start(bf16[16,16,896]{2,1,0:T(8,128)(2,1)S(1)} %get-tuple-element.55.refs_0_), channel_id=1, source_target_pairs={{0,12},{1,13},{2,14},{3,15},{4,0},{5,1},{6,2},{7,3},{8,4},{9,5},{1... | collective-permute-start | bytes 1376264 | tf_op jit(solution)/shard_map/gather/ppermute | solution.py:22
  48.7 16.5 %collective-permute-start.13 = (bf16[16,16,896]{2,1,0:T(8,128)(2,1)S(1)}, bf16[16,16,896]{2,1,0:T(8,128)(2,1)S(1)}, u32[]{:S(2)}, u32[]{:S(2)}) collective-permute-start(bf16[16,16,896]{2,1,0:T(8,128)(2,1)S(1)} %get-tuple-element.55.refs_0_), channel_id=1, source_target_pairs={{0,8},{1,9},{2,10},{3,11},{4,12},{5,13},{6,14},{7,15},{8,0},{9,1},... | collective-permute-start | bytes 1376264 | tf_op jit(solution)/shard_map/gather/ppermute | solution.py:22
  50.0 16.7 %collective-permute-start.12 = (bf16[16,16,896]{2,1,0:T(8,128)(2,1)S(1)}, bf16[16,16,896]{2,1,0:T(8,128)(2,1)S(1)}, u32[]{:S(2)}, u32[]{:S(2)}) collective-permute-start(bf16[16,16,896]{2,1,0:T(8,128)(2,1)S(1)} %get-tuple-element.55.refs_0_), channel_id=1, source_target_pairs={{0,4},{1,5},{2,6},{3,7},{4,8},{5,9},{6,10},{7,11},{8,12},{9,13},{1... | collective-permute-start | bytes 1376264 | tf_op jit(solution)/shard_map/gather/ppermute | solution.py:22
  50.4 16.3 %collective-permute-start.17 = (bf16[16,16,896]{2,1,0:T(8,128)(2,1)S(1)}, bf16[16,16,896]{2,1,0:T(8,128)(2,1)S(1)}, u32[]{:S(2)}, u32[]{:S(2)}) collective-permute-start(bf16[16,16,896]{2,1,0:T(8,128)(2,1)S(1)} %get-tuple-element.56.refs_4_), channel_id=1, source_target_pairs={{0,3},{1,0},{2,1},{3,2},{4,7},{5,4},{6,5},{7,6},{8,11},{9,8},{10,9... | collective-permute-start | bytes 1376264 | tf_op jit(solution)/shard_map/gather/ppermute | solution.py:27
  51.5 15.2 %collective-permute-start.16 = (bf16[16,16,896]{2,1,0:T(8,128)(2,1)S(1)}, bf16[16,16,896]{2,1,0:T(8,128)(2,1)S(1)}, u32[]{:S(2)}, u32[]{:S(2)}) collective-permute-start(bf16[16,16,896]{2,1,0:T(8,128)(2,1)S(1)} %get-tuple-element.56.refs_4_), channel_id=1, source_target_pairs={{0,2},{1,3},{2,0},{3,1},{4,6},{5,7},{6,4},{7,5},{8,10},{9,11},{10,... | collective-permute-start | bytes 1376264 | tf_op jit(solution)/shard_map/gather/ppermute | solution.py:27
  61.7 9.7 %collective-permute-start.15 = (bf16[16,16,896]{2,1,0:T(8,128)(2,1)S(1)}, bf16[16,16,896]{2,1,0:T(8,128)(2,1)S(1)}, u32[]{:S(2)}, u32[]{:S(2)}) collective-permute-start(bf16[16,16,896]{2,1,0:T(8,128)(2,1)S(1)} %get-tuple-element.56.refs_4_), channel_id=1, source_target_pairs={{0,1},{1,2},{2,3},{3,0},{4,5},{5,6},{6,7},{7,4},{8,9},{9,10},{10,1... | collective-permute-start | bytes 1376264 | tf_op jit(solution)/shard_map/gather/ppermute | solution.py:27
  86.2 68.1 %all-gather.2.cloned.1.call-start = ((), (), s32[]{:S(2)}) async-start(), calls=%async_computation.2 | async-start | bytes 3391488 | tf_op jit(solution)/shard_map/weights/all_gather | solution.py:377
  86.3 15.8 %collective-permute-start.18 = (bf16[16,16,896]{2,1,0:T(8,128)(2,1)}, bf16[16,16,896]{2,1,0:T(8,128)(2,1)S(1)}, u32[]{:S(2)}, u32[]{:S(2)}) collective-permute-start(bf16[16,16,896]{2,1,0:T(8,128)(2,1)} %get-tuple-element.61), channel_id=1, source_target_pairs={{0,12},{1,13},{2,14},{3,15},{4,0},{5,1},{6,2},{7,3},{8,4},{9,5},{1... | collective-permute-start | bytes 1376264 | tf_op jit(solution)/shard_map/scatter/ppermute | solution.py:22
  90.0 12.3 %collective-permute-start.19 = (bf16[16,16,896]{2,1,0:T(8,128)(2,1)}, bf16[16,16,896]{2,1,0:T(8,128)(2,1)S(1)}, u32[]{:S(2)}, u32[]{:S(2)}) collective-permute-start(bf16[16,16,896]{2,1,0:T(8,128)(2,1)} %get-tuple-element.62), channel_id=1, source_target_pairs={{0,8},{1,9},{2,10},{3,11},{4,12},{5,13},{6,14},{7,15},{8,0},{9,1},... | collective-permute-start | bytes 1376264 | tf_op jit(solution)/shard_map/scatter/ppermute | solution.py:22
  90.0 14.8 %collective-permute-start.20 = (bf16[16,16,896]{2,1,0:T(8,128)(2,1)}, bf16[16,16,896]{2,1,0:T(8,128)(2,1)S(1)}, u32[]{:S(2)}, u32[]{:S(2)}) collective-permute-start(bf16[16,16,896]{2,1,0:T(8,128)(2,1)} %get-tuple-element.63), channel_id=1, source_target_pairs={{0,4},{1,5},{2,6},{3,7},{4,8},{5,9},{6,10},{7,11},{8,12},{9,13},{1... | collective-permute-start | bytes 1376264 | tf_op jit(solution)/shard_map/scatter/ppermute | solution.py:22
  91.0 13.9 %collective-permute-start.21 = (bf16[16,16,896]{2,1,0:T(8,128)(2,1)}, bf16[16,16,896]{2,1,0:T(8,128)(2,1)S(1)}, u32[]{:S(2)}, u32[]{:S(2)}) collective-permute-start(bf16[16,16,896]{2,1,0:T(8,128)(2,1)} %get-tuple-element.65), channel_id=1, source_target_pairs={{0,3},{1,0},{2,1},{3,2},{4,7},{5,4},{6,5},{7,6},{8,11},{9,8},{10,9... | collective-permute-start | bytes 1376264 | tf_op jit(solution)/shard_map/scatter/ppermute | solution.py:27
  91.0 14.3 %collective-permute-start.22 = (bf16[16,16,896]{2,1,0:T(8,128)(2,1)}, bf16[16,16,896]{2,1,0:T(8,128)(2,1)S(1)}, u32[]{:S(2)}, u32[]{:S(2)}) collective-permute-start(bf16[16,16,896]{2,1,0:T(8,128)(2,1)} %get-tuple-element.66), channel_id=1, source_target_pairs={{0,2},{1,3},{2,0},{3,1},{4,6},{5,7},{6,4},{7,5},{8,10},{9,11},{10,... | collective-permute-start | bytes 1376264 | tf_op jit(solution)/shard_map/scatter/ppermute | solution.py:27
  102.1 9.7 %collective-permute-start.23 = (bf16[16,16,896]{2,1,0:T(8,128)(2,1)S(1)}, bf16[16,16,896]{2,1,0:T(8,128)(2,1)S(1)}, u32[]{:S(2)}, u32[]{:S(2)}) collective-permute-start(bf16[16,16,896]{2,1,0:T(8,128)(2,1)S(1)} %copy-done.9), channel_id=1, source_target_pairs={{0,1},{1,2},{2,3},{3,0},{4,5},{5,6},{6,7},{7,4},{8,9},{9,10},{10,1... | collective-permute-start | bytes 1376264 | tf_op jit(solution)/shard_map/scatter/ppermute | solution.py:27
  115.2 6.2 %collective-permute-start.24 = (bf16[8,16,896]{2,1,0:T(8,128)(2,1)}, bf16[8,16,896]{2,1,0:T(8,128)(2,1)S(1)}, u32[]{:S(2)}, u32[]{:S(2)}) collective-permute-start(bf16[8,16,896]{2,1,0:T(8,128)(2,1)} %get-tuple-element.68), channel_id=1, source_target_pairs={{0,3},{1,0},{2,1},{3,2},{4,7},{5,4},{6,5},{7,6},{8,11},{9,8},{10,9... | collective-permute-start | bytes 688136 | tf_op jit(solution)/shard_map/scatter/ppermute | solution.py:27
  122.9 8.7 %collective-permute-start.25 = (bf16[8,16,896]{2,1,0:T(8,128)(2,1)}, bf16[8,16,896]{2,1,0:T(8,128)(2,1)S(1)}, u32[]{:S(2)}, u32[]{:S(2)}) collective-permute-start(bf16[8,16,896]{2,1,0:T(8,128)(2,1)} %get-tuple-element.75), channel_id=1, source_target_pairs={{0,2},{1,3},{2,0},{3,1},{4,6},{5,7},{6,4},{7,5},{8,10},{9,11},{10,... | collective-permute-start | bytes 688136 | tf_op jit(solution)/shard_map/scatter/ppermute | solution.py:27
  125.8 8.1 %collective-permute-start.26 = (bf16[8,16,896]{2,1,0:T(8,128)(2,1)}, bf16[8,16,896]{2,1,0:T(8,128)(2,1)S(1)}, u32[]{:S(2)}, u32[]{:S(2)}) collective-permute-start(bf16[8,16,896]{2,1,0:T(8,128)(2,1)} %get-tuple-element.76), channel_id=1, source_target_pairs={{0,1},{1,2},{2,3},{3,0},{4,5},{5,6},{6,7},{7,4},{8,9},{9,10},{10,1... | collective-permute-start | bytes 688136 | tf_op jit(solution)/shard_map/scatter/ppermute | solution.py:27
  126.4 9.1 %collective-permute-start.27 = (bf16[8,16,896]{2,1,0:T(8,128)(2,1)}, bf16[8,16,896]{2,1,0:T(8,128)(2,1)S(1)}, u32[]{:S(2)}, u32[]{:S(2)}) collective-permute-start(bf16[8,16,896]{2,1,0:T(8,128)(2,1)} %get-tuple-element.78), channel_id=1, source_target_pairs={{0,12},{1,13},{2,14},{3,15},{4,0},{5,1},{6,2},{7,3},{8,4},{9,5},{1... | collective-permute-start | bytes 688136 | tf_op jit(solution)/shard_map/scatter/ppermute | solution.py:22
  129.1 7.8 %collective-permute-start.28 = (bf16[8,16,896]{2,1,0:T(8,128)(2,1)}, bf16[8,16,896]{2,1,0:T(8,128)(2,1)S(1)}, u32[]{:S(2)}, u32[]{:S(2)}) collective-permute-start(bf16[8,16,896]{2,1,0:T(8,128)(2,1)} %get-tuple-element.79), channel_id=1, source_target_pairs={{0,8},{1,9},{2,10},{3,11},{4,12},{5,13},{6,14},{7,15},{8,0},{9,1},... | collective-permute-start | bytes 688136 | tf_op jit(solution)/shard_map/scatter/ppermute | solution.py:22
  130.1 9.2 %collective-permute-start.29 = (bf16[8,16,896]{2,1,0:T(8,128)(2,1)}, bf16[8,16,896]{2,1,0:T(8,128)(2,1)S(1)}, u32[]{:S(2)}, u32[]{:S(2)}) collective-permute-start(bf16[8,16,896]{2,1,0:T(8,128)(2,1)} %get-tuple-element.80), channel_id=1, source_target_pairs={{0,4},{1,5},{2,6},{3,7},{4,8},{5,9},{6,10},{7,11},{8,12},{9,13},{1... | collective-permute-start | bytes 688136 | tf_op jit(solution)/shard_map/scatter/ppermute | solution.py:22
  146.2 5.8 %collective-permute-start.34 = (bf16[2,16,896]{2,1,0:T(8,128)(2,1)S(1)}, bf16[2,16,896]{2,1,0:T(8,128)(2,1)S(1)}, u32[]{:S(2)}, u32[]{:S(2)}) collective-permute-start(bf16[2,16,896]{2,1,0:T(8,128)(2,1)S(1)} %get-tuple-element.87), channel_id=1, source_target_pairs={{0,2},{1,3},{2,0},{3,1},{4,6},{5,7},{6,4},{7,5},{8,10},{9,11},{10,... | collective-permute-start | bytes 172040 | tf_op jit(solution)/shard_map/scatter/ppermute | solution.py:27
  146.2 6.0 %collective-permute-start.35 = (bf16[2,16,896]{2,1,0:T(8,128)(2,1)S(1)}, bf16[2,16,896]{2,1,0:T(8,128)(2,1)S(1)}, u32[]{:S(2)}, u32[]{:S(2)}) collective-permute-start(bf16[2,16,896]{2,1,0:T(8,128)(2,1)S(1)} %get-tuple-element.88), channel_id=1, source_target_pairs={{0,1},{1,2},{2,3},{3,0},{4,5},{5,6},{6,7},{7,4},{8,9},{9,10},{10,1... | collective-permute-start | bytes 172040 | tf_op jit(solution)/shard_map/scatter/ppermute | solution.py:27
  (16 other events, 233.6 us)
Sparse Core Ops, SparseCore 0:
  86.3 36.4 reduce-scatter.1
  124.7 25.9 all-gather.1

commit v3 on v2

--- a/solution.py
+++ b/solution.py
@@ -12,7 +12,7 @@
 NT = 16
 STEP = 4
 VMEM_LIMIT = 20 * 1024 * 1024
-ATTEND_LIMIT = 36 * 1024 * 1024
+ATTEND_LIMIT = 46 * 1024 * 1024
 F32 = jnp.float32
 BF16 = jnp.bfloat16
 
@@ -64,12 +64,21 @@
     return pl.ds(pl.multiple_of(base + lax.rem(at, SIDE) * SUB, SUB), SUB)
 
 
-def split_kernel(owner, slot, tiles, *outs):
+def split_kernel(owner, slot, tiles, *refs):
+    outs, (held, sems) = refs[: 2 * SIDE], refs[2 * SIDE :]
     own, x, y = place()
-    for r, tile in enumerate(my_slots(owner, slot, own)):
+    copies = [
+        pltpu.make_async_copy(tiles.at[tile], held.at[r], sems.at[r])
+        for r, tile in enumerate(my_slots(owner, slot, own))
+    ]
+    for copy in copies:
+        copy.start()
+    for copy in copies:
+        copy.wait()
+    for r in range(2):
         for k in range(SIDE):
-            outs[k][r] = tiles[tile, sub_row(x + k, 0), :]
-            outs[SIDE + k][r] = tiles[tile, sub_row(y + k, SIDE * SUB), :]
+            outs[k][r] = held[r, sub_row(x + k, 0), :]
+            outs[SIDE + k][r] = held[r, sub_row(y + k, SIDE * SUB), :]
 
 
 def compact_kernel(owner, *refs):
@@ -132,10 +141,22 @@
 
 
 def attention_kernel(length, *refs):
-    ins, (q_ref, up_ref, w_ref) = refs[: 2 * SIDE], refs[2 * SIDE : 2 * SIDE + 3]
-    ctx_ref, qg_ref = refs[11:13]
-    outs, g_ref, acc = refs[13 : 13 + 2 * SIDE], refs[-2], refs[-1]
+    ins, (q_ref, up_ref, w_ref, in_ref) = refs[: 2 * SIDE], refs[2 * SIDE : 2 * SIDE + 4]
+    ctx_ref, outs = refs[12], refs[13 : 13 + 2 * SIDE]
+    g_ref, acc, held_q, rows_q, ready, arrive, leave = refs[-7:]
     step = pl.program_id(0)
+    tall = STEP * SPAN
+    count = rows_q.shape[0] // tall
+
+    def bring(part):
+        rows = pl.ds(part * tall, tall)
+        return pltpu.make_async_copy(in_ref.at[rows], rows_q.at[rows], arrive.at[part])
+
+    @pl.when(step == 0)
+    def _():
+        for part in range(count):
+            bring(part).start()
+
     spans = q_ref.shape[0] // SPAN
     columns = q_ref.shape[1]
     heads = columns // HD
@@ -180,15 +201,18 @@
     inner = jnp.sum(attention * dprobs, axis=-1, keepdims=True)
     dscore = (attention * (dprobs - inner) * scale).astype(BF16)
     grads = []
+    query_grads = []
     for s in range(spans):
-        key_grads, value_grads = [], []
+        key_grads, value_grads, own_grads = [], [], []
         for h in range(heads):
             rows = tokens(s * heads + h)
             ctx_ref[tokens(s), head(h)] = dot(attention_b[rows], value(s, h), 1, 0).astype(BF16)
-            qg_ref[tokens(s), head(h)] = dot(dscore[rows], key(s, h), 1, 0).astype(BF16)
+            own_grads.append(dot(dscore[rows], key(s, h), 1, 0).astype(BF16))
             key_grads.append(dot(dscore[rows], q_ref[tokens(s), head(h)], 0, 0).astype(BF16))
             value_grads.append(dot(attention_b[rows], up_ref[tokens(s), head(h)], 0, 0).astype(BF16))
         grads.append(jnp.concatenate(key_grads + value_grads, axis=1))
+        query_grads.append(jnp.concatenate(own_grads, axis=1))
+    query_grads = jnp.concatenate(query_grads, axis=0)
     grads = jnp.concatenate(grads, axis=0)
     partial = dot(grads, w_ref[...], 1, 1).astype(BF16)
     for s in range(spans):
@@ -197,49 +221,40 @@
                 low = s * keys + (j * 2 * SIDE + k) * SUB
                 out[s * 2 + j] = partial[low : low + SUB]
     gain = dot(near, grads, 0, 0)
+    width = in_ref.shape[1]
+    cut = width // (2 * SIDE)
+    rest = gain.shape[0] // SIDE
+
+    held_q[pl.ds(pl.multiple_of(step * tall, tall), tall)] = query_grads
 
     @pl.when(step == 0)
     def _():
         acc[...] = gain
 
-    @pl.when(step > 0)
+    @pl.when((step > 0) & (step < pl.num_programs(0) - 1))
     def _():
         acc[...] += gain
 
     @pl.when(step == pl.num_programs(0) - 1)
     def _():
-        g_ref[0] = acc[:, :columns].astype(BF16)
-        g_ref[1] = acc[:, columns:].astype(BF16)
-
-
-def query_weight_kernel(rows_0, rows_1, grads, near_e, out):
-    z = pl.program_id(0)
-    cut = rows_0.shape[1]
-    rest = near_e.shape[1] // SIDE
-    at = pl.ds(pl.multiple_of(z * rest, 32), rest)
-    for core, rows in enumerate((rows_0, rows_1)):
-        out[0, core, :cut] = dot(rows[...], grads[...], 0, 0).astype(BF16)
-        out[0, core, cut:] = near_e[core, at]
-
-
-def query_weight(queries_in, query_grad, near_e):
-    tokens, width = queries_in.shape
-    columns = query_grad.shape[1]
-    cut = width // (2 * SIDE)
-    rest = near_e.shape[1] // SIDE
-    return pl.pallas_call(
-        query_weight_kernel,
-        grid=(SIDE,),
-        in_specs=[
-            pl.BlockSpec((tokens, cut), lambda z: (0, z)),
-            pl.BlockSpec((tokens, cut), lambda z: (0, SIDE + z)),
-            pl.BlockSpec((tokens, columns), lambda z: (0, 0)),
-            pl.BlockSpec(near_e.shape, lambda z: (0, 0, 0)),
-        ],
-        out_specs=pl.BlockSpec((1, 2, cut + rest, columns), lambda z: (z, 0, 0, 0)),
-        out_shape=pltpu.HBM((SIDE, 2, cut + rest, columns), BF16),
-        compiler_params=pltpu.CompilerParams(vmem_limit_bytes=VMEM_LIMIT),
-    )(queries_in, queries_in, query_grad, near_e)
+        total = (acc[...] + gain).astype(BF16)
+        for part in range(count):
+            bring(part).wait()
+        copies = []
+        for core in range(2):
+            for z in range(SIDE):
+                i = core * SIDE + z
+                slot = 2 * z + core
+                part = total[z * rest : (z + 1) * rest, core * columns : (core + 1) * columns]
+                ready[slot, cut:] = part
+                part = dot(rows_q[:, i * cut : (i + 1) * cut], held_q[...], 0, 0)
+                ready[slot, :cut] = part.astype(BF16)
+                copies.append(
+                    pltpu.make_async_copy(ready.at[slot], g_ref.at[slot], leave.at[slot])
+                )
+                copies[-1].start()
+        for copy in copies:
+            copy.wait()
 
 
 def weights_kernel(chunks, out_q, out_k, out_v, bring, hold, arrive, leave):
@@ -290,21 +305,42 @@
     )(chunks)
 
 
-def call(kernel, scalars, ins, outs, make=jax.ShapeDtypeStruct):
+def cut_tiles(owner, slot, tiles):
+    width = tiles.shape[2]
+    return pl.pallas_call(
+        split_kernel,
+        out_shape=[jax.ShapeDtypeStruct((2, SUB, width), BF16)] * (2 * SIDE),
+        in_specs=[pl.BlockSpec(memory_space=pltpu.SMEM)] * 2
+        + [pl.BlockSpec(memory_space=pl.ANY)],
+        out_specs=[pl.BlockSpec(memory_space=pltpu.VMEM)] * (2 * SIDE),
+        scratch_shapes=[
+            pltpu.VMEM((2,) + tiles.shape[1:], BF16),
+            pltpu.SemaphoreType.DMA((2,)),
+        ],
+        compiler_params=pltpu.CompilerParams(vmem_limit_bytes=VMEM_LIMIT),
+    )(owner, slot, pltpu.with_memory_space_constraint(tiles, pltpu.HBM))
+
+
+def call(kernel, scalars, ins, outs, kept=None):
     vmem = pl.BlockSpec(memory_space=pltpu.VMEM)
     return pl.pallas_call(
         kernel,
-        out_shape=[make(shape, dtype) for shape, dtype in outs],
+        out_shape=[
+            jax.ShapeDtypeStruct(*out) if kept is None or i in kept else pltpu.HBM(*out)
+            for i, out in enumerate(outs)
+        ],
         in_specs=[pl.BlockSpec(memory_space=pltpu.SMEM)] * len(scalars) + [vmem] * len(ins),
         out_specs=[vmem] * len(outs),
         compiler_params=pltpu.CompilerParams(vmem_limit_bytes=VMEM_LIMIT),
     )(*scalars, *ins)
 
 
-def attend(key_length, parts, query, upstream, weight):
+def attend(key_length, parts, query, upstream, weight, queries_in):
     spans = key_length.shape[0]
     width = weight.shape[0]
     columns = query.shape[1]
+    depth = queries_in.shape[1]
+    chunks = (2 * SIDE, depth // (2 * SIDE) + width // SIDE, columns)
     tile_block = pl.BlockSpec((2 * STEP, SUB, width), lambda c, *_: (c, 0, 0))
     token_block = pl.BlockSpec((STEP * SPAN, columns), lambda c, *_: (c, 0))
     return pl.pallas_call(
@@ -314,17 +350,25 @@
             grid=(spans // STEP,),
             in_specs=[tile_block] * (2 * SIDE)
             + [token_block] * 2
-            + [pl.BlockSpec(weight.shape, lambda c, *_: (0, 0))],
-            out_specs=[token_block] * 2
+            + [pl.BlockSpec(weight.shape, lambda c, *_: (0, 0))]
+            + [pl.BlockSpec(memory_space=pl.ANY)],
+            out_specs=[token_block]
             + [tile_block] * (2 * SIDE)
-            + [pl.BlockSpec((2, width, columns), lambda c, *_: (0, 0, 0))],
-            scratch_shapes=[pltpu.VMEM(weight.shape, F32)],
+            + [pl.BlockSpec(memory_space=pl.ANY)],
+            scratch_shapes=[
+                pltpu.VMEM(weight.shape, F32),
+                pltpu.VMEM((spans * SPAN, columns), BF16),
+                pltpu.VMEM(queries_in.shape, BF16),
+                pltpu.VMEM(chunks, BF16),
+                pltpu.SemaphoreType.DMA((spans // STEP,)),
+                pltpu.SemaphoreType.DMA((2 * SIDE,)),
+            ],
         ),
-        out_shape=[jax.ShapeDtypeStruct((spans * SPAN, columns), BF16)] * 2
+        out_shape=[jax.ShapeDtypeStruct((spans * SPAN, columns), BF16)]
         + [pltpu.HBM((NT, SUB, width), BF16)] * (2 * SIDE)
-        + [jax.ShapeDtypeStruct((2, width, columns), BF16)],
+        + [pltpu.HBM(chunks, BF16)],
         compiler_params=pltpu.CompilerParams(vmem_limit_bytes=ATTEND_LIMIT),
-    )(key_length, *parts, query, upstream, weight)
+    )(key_length, *parts, query, upstream, weight, pltpu.with_memory_space_constraint(queries_in, pltpu.HBM))
 
 
 def body(
@@ -343,7 +387,7 @@
     pair = ((2, SUB, width), BF16)
     line = ((2 * SIDE, SUB, width), BF16)
     with jax.named_scope("gather"):
-        cut = call(split_kernel, (neighbour_owner, neighbour_slot), (tiles,), [pair] * 8)
+        cut = cut_tiles(neighbour_owner, neighbour_slot, tiles)
         row_a = [cut[0]] + [along_x(cut[k], k) for k in steps]
         row_b = [cut[SIDE]] + [along_y(cut[SIDE + k], k) for k in steps]
         line_a = jnp.concatenate(row_a, axis=0)
@@ -357,18 +401,16 @@
     query = jnp.dot(queries_in, w_query, preferred_element_type=F32).astype(BF16)
     weight = jnp.concatenate([w_key, w_value], axis=1)
     with jax.named_scope("attend"):
-        context, query_grad, *sends, near_e = attend(
-            key_length, parts, query, grad_context, weight
+        context, *sends, local = attend(
+            key_length, parts, query, grad_context, weight, queries_in
         )
     with jax.named_scope("scatter"):
         back = [sends[0]] + [along_x(sends[k], -k) for k in steps]
         back += [sends[SIDE]] + [along_y(sends[SIDE + k], -k) for k in steps]
     with jax.named_scope("weights"):
-        local = query_weight(queries_in, query_grad, near_e)
-        local = local.reshape(-1, *local.shape[2:])
         share = lax.psum_scatter(local, "dp", scatter_dimension=0, tiled=True)
     with jax.named_scope("scatter"):
-        wide = call(expand_kernel, (neighbour_owner,), back, [line] * 8, pltpu.HBM)
+        wide = call(expand_kernel, (neighbour_owner,), back, [line] * 8, (0, SIDE))
     with jax.named_scope("scatter"):
         home_a = [wide[0]] + [along_y(wide[k], -k) for k in steps]
         home_b = [wide[SIDE]] + [along_x(wide[SIDE + k], -k) for k in steps]

time: 166 us -> 163 us (0.982)
  local copies, waits for them, and re-layouts: 4.9 us -> 1.84 us
    unnamed x29 -> x21, local copies, waits for them, and re-layouts: 4.87 us -> 1.82 us
    pallas_call x6 -> x5, Pallas kernels: 12 us -> 9.5 us  [the longest x4 7.68 us: call(): pl.pallas_call(kernel, out_shape=[jax.ShapeDtypeStruct(*out) if kept is N...]
    pallas_call x1, Pallas kernels: 11.3 us -> 13.6 us  [attend(): pl.pallas_call(attention_kernel, grid_spec=pltpu.PrefetchScalarGridSpec(n...]
where the time goes in v3:
time: 163 us; the launch traced here: 162 us
  waiting for transfers between devices  70.9 us (43%)
  starting transfers between devices  43.6 us (27%)
  Pallas kernels  26.9 us (17%)
  between operations  14.2 us (9%)
  matrix products  3.43 us (2%)
  local copies, waits for them, and re-layouts  1.84 us (1%)
    ppermute x18, waiting for transfers between devices, along_x(): return lax.ppermute(value, 'enc', pairs)  36.9 us
    ppermute x18, waiting for transfers between devices, along_y(): return lax.ppermute(value, 'enc', pairs)  32.5 us
    ppermute x18, starting transfers between devices, along_x(): return lax.ppermute(value, 'enc', pairs)  25.6 us
    ppermute x18, starting transfers between devices, along_y(): return lax.ppermute(value, 'enc', pairs)  18 us
    pallas_call x1, Pallas kernels, attend(): pl.pallas_call(attention_kernel, grid_spec=pltpu.PrefetchScalarGridSpec(n...  13.6 us
    pallas_call x4, Pallas kernels, call(): pl.pallas_call(kernel, out_shape=[jax.ShapeDtypeStruct(*out) if kept is N...  7.68 us
    pallas_call x1, Pallas kernels, weight_outputs(): pl.pallas_call(weights_kernel, out_shape=[jax.ShapeDtypeStruct(shape, F32...  3.8 us
    dot_general x1, matrix products, body(): jnp.dot(queries_in, w_query, preferred_element_type=F32).astype(BF16)  3.43 us
  transfers between devices with their start and end apart: 38, of which 27 were waited for; matrix products, arithmetic and copies ran while one was open for 3% of the time, Pallas kernels for 4%

profile of v3, /device:TPU:0, one launch (start us, length us, event | category | flops | bytes accessed | tf_op | source)
XLA Modules:
  0.0 162.2 jit_solution(7891492538800186824)
XLA Ops:
  8.9 1.8 %gather.2 = (bf16[2,16,896]{2,1,0:T(8,128)(2,1)S(1)}, bf16[2,16,896]{2,1,0:T(8,128)(2,1)S(1)}, bf16[2,16,896]{2,1,0:T(8,128)(2,1)S(1)}, bf16[2,16,896]{2,1,0:T(8...) custom-call(s32[8,2]{1,0:T(8,128)S(1)} %copy.23.owner, ...), custom_call_target="tpu_custom_call" | custom-call | tf_op jit(solution)/shard_map/gather/pallas_call | solution.py:310
  10.7 1.6 %collective-permute-start = (bf16[2,16,896]{2,1,0:T(8,128)(2,1)S(1)}, bf16[2,16,896]{2,1,0:T(8,128)(2,1)S(1)}, u32[]{:S(2)}, u32[]{:S(2)}) collective-permute-start(bf16[2,16,896]{2,1,0:T(8,128)(2,1)S(1)} %get-tuple-element.47), channel_id=1, source_target_pairs={{0,4},{1,5},{2,6},{3,7},{4,8},{5,9},{6,10},{7,11},{8,12},{9,13},{1... | collective-permute-start | bytes 172040 | tf_op jit(solution)/shard_map/gather/ppermute | solution.py:22
  12.3 2.7 %collective-permute-start.1 = (bf16[2,16,896]{2,1,0:T(8,128)(2,1)S(1)}, bf16[2,16,896]{2,1,0:T(8,128)(2,1)S(1)}, u32[]{:S(2)}, u32[]{:S(2)}) collective-permute-start(bf16[2,16,896]{2,1,0:T(8,128)(2,1)S(1)} %get-tuple-element.48), channel_id=1, source_target_pairs={{0,8},{1,9},{2,10},{3,11},{4,12},{5,13},{6,14},{7,15},{8,0},{9,1},... | collective-permute-start | bytes 172040 | tf_op jit(solution)/shard_map/gather/ppermute | solution.py:22
  18.1 2.9 %collective-permute-start.7 = (bf16[2,16,896]{2,1,0:T(8,128)(2,1)S(1)}, bf16[2,16,896]{2,1,0:T(8,128)(2,1)S(1)}, u32[]{:S(2)}, u32[]{:S(2)}) collective-permute-start(bf16[2,16,896]{2,1,0:T(8,128)(2,1)S(1)} %get-tuple-element.52), channel_id=1, source_target_pairs={{0,2},{1,3},{2,0},{3,1},{4,6},{5,7},{6,4},{7,5},{8,10},{9,11},{10,... | collective-permute-start | bytes 172040 | tf_op jit(solution)/shard_map/gather/ppermute | solution.py:27
  23.8 2.8 %collective-permute-done.8 = bf16[2,16,896]{2,1,0:T(8,128)(2,1)S(1)} collective-permute-done((bf16[2,16,896]{2,1,0:T(8,128)(2,1)S(1)}, bf16[2,16,896]{2,1,0:T(8,128)(2,1)S(1)}, u32[]{:S(2)}, u32[]{:S(2)}) %collective-permute-start.8) | collective-permute-done | bytes 57376 | tf_op jit(solution)/shard_map/gather/ppermute | solution.py:27
  26.8 2.5 %collective-permute-start.10 = (bf16[8,16,896]{2,1,0:T(8,128)(2,1)S(1)}, bf16[8,16,896]{2,1,0:T(8,128)(2,1)S(1)}, u32[]{:S(2)}, u32[]{:S(2)}) collective-permute-start(bf16[8,16,896]{2,1,0:T(8,128)(2,1)S(1)} %constant_dynamic-update-slice_fusion.4.refs_4_), channel_id=1, source_target_pairs={{0,8},{1,9},{2,10},{3,11},{4,12},{5,13},{6,14},{7,15},{8,0},{9,1},... | collective-permute-start | bytes 688136 | tf_op jit(solution)/shard_map/gather/ppermute | solution.py:22
  29.4 2.6 %collective-permute-start.5 = (bf16[8,16,896]{2,1,0:T(8,128)(2,1)S(1)}, bf16[8,16,896]{2,1,0:T(8,128)(2,1)S(1)}, u32[]{:S(2)}, u32[]{:S(2)}) collective-permute-start(bf16[8,16,896]{2,1,0:T(8,128)(2,1)S(1)} %constant_dynamic-update-slice_fusion.refs_0_), channel_id=1, source_target_pairs={{0,3},{1,0},{2,1},{3,2},{4,7},{5,4},{6,5},{7,6},{8,11},{9,8},{10,9... | collective-permute-start | bytes 688136 | tf_op jit(solution)/shard_map/gather/ppermute | solution.py:27
  33.6 1.6 collective-permute-done.10.refs_6_
  35.2 2.4 %collective-permute-done.9.refs_5_ = bf16[8,16,896]{2,1,0:T(8,128)(2,1)S(1)} collective-permute-done((bf16[8,16,896]{2,1,0:T(8,128)(2,1)S(1)}, bf16[8,16,896]{2,1,0:T(8,128)(2,1)S(1)}, u32[]{:S(2)}, u32[]{:S(2)}) %collective-permute-start.9) | collective-permute-done | bytes 229408 | tf_op jit(solution)/shard_map/gather/ppermute | solution.py:22
  39.8 2.4 %collective-permute-done.3.refs_1_ = bf16[8,16,896]{2,1,0:T(8,128)(2,1)S(1)} collective-permute-done((bf16[8,16,896]{2,1,0:T(8,128)(2,1)S(1)}, bf16[8,16,896]{2,1,0:T(8,128)(2,1)S(1)}, u32[]{:S(2)}, u32[]{:S(2)}) %collective-permute-start.3) | collective-permute-done | bytes 229408 | tf_op jit(solution)/shard_map/gather/ppermute | solution.py:27
  42.2 2.0 %gather.3 = (bf16[16,16,896]{2,1,0:T(8,128)(2,1)S(1)}, bf16[16,16,896]{2,1,0:T(8,128)(2,1)S(1)}) custom-call(s32[8,2]{1,0:T(8,128)S(1)} %copy.23.owner, bf16[8,16,896]{2,1,0:T(8,128)(2,1)S(1)} %constant_dynamic-update-slice_fusion.refs_0_, bf16[8,16,896]{2,1,0:T(8,128)(2,1)S(1)} %collective-permute-done.3.refs_1_, ...), custom_call_target="tpu_custom_call" | custom-call | tf_op jit(solution)/shard_map/gather/pallas_call | solution.py:326
  44.1 3.1 %collective-permute-start.14 = (bf16[16,16,896]{2,1,0:T(8,128)(2,1)S(1)}, bf16[16,16,896]{2,1,0:T(8,128)(2,1)S(1)}, u32[]{:S(2)}, u32[]{:S(2)}) collective-permute-start(bf16[16,16,896]{2,1,0:T(8,128)(2,1)S(1)} %get-tuple-element.54.refs_0_), channel_id=1, source_target_pairs={{0,12},{1,13},{2,14},{3,15},{4,0},{5,1},{6,2},{7,3},{8,4},{9,5},{1... | collective-permute-start | bytes 1376264 | tf_op jit(solution)/shard_map/gather/ppermute | solution.py:22
  51.4 10.2 %collective-permute-done.14.refs_3_ = bf16[16,16,896]{2,1,0:T(8,128)(2,1)S(1)} collective-permute-done((bf16[16,16,896]{2,1,0:T(8,128)(2,1)S(1)}, bf16[16,16,896]{2,1,0:T(8,128)(2,1)S(1)}, u32[]{:S(2)}, u32[]{:S(2)}) %collective-permute-start.14) | collective-permute-done | bytes 458784 | tf_op jit(solution)/shard_map/gather/ppermute | solution.py:22
  61.5 3.4 %convolution_convert_fusion.refs_8_ = bf16[512,256]{1,0:T(8,128)(2,1)S(1)} fusion(bf16[512,4096]{1,0:T(8,128)(2,1)} %refs_11_.1, bf16[4096,256]{1,0:T(8,128)(2,1)S(1)} %copy-done), kind=kOutput, calls=%fused_computation | convolution fusion | flops 1073872896 | bytes 6553600 | tf_op jit(solution)/shard_map/dot_general | solution.py:401
  65.0 1.6 collective-permute-done.12.refs_1_
  66.6 4.6 %collective-permute-done.15.refs_5_ = bf16[16,16,896]{2,1,0:T(8,128)(2,1)S(1)} collective-permute-done((bf16[16,16,896]{2,1,0:T(8,128)(2,1)S(1)}, bf16[16,16,896]{2,1,0:T(8,128)(2,1)S(1)}, u32[]{:S(2)}, u32[]{:S(2)}) %collective-permute-start.15) | collective-permute-done | bytes 458784 | tf_op jit(solution)/shard_map/gather/ppermute | solution.py:27
  71.2 13.6 %attend.1 = (bf16[512,256]{1,0:T(8,128)(2,1)}, bf16[16,16,896]{2,1,0:T(8,128)(2,1)}, bf16[16,16,896]{2,1,0:T(8,128)(2,1)}, bf16[16,16,896]{2,1,0:T(8,128)(2,1)},...) custom-call(s32[8,2]{1,0:T(8,128)S(1)} %copy.24.length, ...), custom_call_target="tpu_custom_call" | custom-call | tf_op jit(solution)/shard_map/attend/pallas_call | solution.py:346
  84.9 3.7 %collective-permute-start.18 = (bf16[16,16,896]{2,1,0:T(8,128)(2,1)}, bf16[16,16,896]{2,1,0:T(8,128)(2,1)S(1)}, u32[]{:S(2)}, u32[]{:S(2)}) collective-permute-start(bf16[16,16,896]{2,1,0:T(8,128)(2,1)} %get-tuple-element.59), channel_id=1, source_target_pairs={{0,12},{1,13},{2,14},{3,15},{4,0},{5,1},{6,2},{7,3},{8,4},{9,5},{1... | collective-permute-start | bytes 1376264 | tf_op jit(solution)/shard_map/scatter/ppermute | solution.py:22
  90.5 10.3 %collective-permute-done.18.refs_1_ = bf16[16,16,896]{2,1,0:T(8,128)(2,1)S(1)} collective-permute-done((bf16[16,16,896]{2,1,0:T(8,128)(2,1)}, bf16[16,16,896]{2,1,0:T(8,128)(2,1)S(1)}, u32[]{:S(2)}, u32[]{:S(2)}) %collective-permute-start.18) | collective-permute-done | bytes 458784 | tf_op jit(solution)/shard_map/scatter/ppermute | solution.py:22
  100.9 2.6 %collective-permute-done.20.refs_3_ = bf16[16,16,896]{2,1,0:T(8,128)(2,1)S(1)} collective-permute-done((bf16[16,16,896]{2,1,0:T(8,128)(2,1)}, bf16[16,16,896]{2,1,0:T(8,128)(2,1)S(1)}, u32[]{:S(2)}, u32[]{:S(2)}) %collective-permute-start.20) | collective-permute-done | bytes 458784 | tf_op jit(solution)/shard_map/scatter/ppermute | solution.py:22
  104.0 6.5 %collective-permute-done.23.refs_7_ = bf16[16,16,896]{2,1,0:T(8,128)(2,1)S(1)} collective-permute-done((bf16[16,16,896]{2,1,0:T(8,128)(2,1)S(1)}, bf16[16,16,896]{2,1,0:T(8,128)(2,1)S(1)}, u32[]{:S(2)}, u32[]{:S(2)}) %collective-permute-start.23) | collective-permute-done | bytes 458784 | tf_op jit(solution)/shard_map/scatter/ppermute | solution.py:27
  110.5 3.4 %scatter.3 = (bf16[8,16,896]{2,1,0:T(8,128)(2,1)S(1)}, bf16[8,16,896]{2,1,0:T(8,128)(2,1)}, bf16[8,16,896]{2,1,0:T(8,128)(2,1)}, bf16[8,16,896]{2,1,0:T(8,128)(2...) custom-call(s32[8,2]{1,0:T(8,128)S(1)} %copy.23.owner, ...), custom_call_target="tpu_custom_call" | custom-call | tf_op jit(solution)/shard_map/scatter/pallas_call | solution.py:326
  114.5 5.6 %collective-permute-done.24.refs_1_ = bf16[8,16,896]{2,1,0:T(8,128)(2,1)S(1)} collective-permute-done((bf16[8,16,896]{2,1,0:T(8,128)(2,1)}, bf16[8,16,896]{2,1,0:T(8,128)(2,1)S(1)}, u32[]{:S(2)}, u32[]{:S(2)}) %collective-permute-start.24) | collective-permute-done | bytes 229408 | tf_op jit(solution)/shard_map/scatter/ppermute | solution.py:27
  121.6 2.9 %collective-permute-start.25 = (bf16[8,16,896]{2,1,0:T(8,128)(2,1)}, bf16[8,16,896]{2,1,0:T(8,128)(2,1)S(1)}, u32[]{:S(2)}, u32[]{:S(2)}) collective-permute-start(bf16[8,16,896]{2,1,0:T(8,128)(2,1)} %get-tuple-element.73), channel_id=1, source_target_pairs={{0,2},{1,3},{2,0},{3,1},{4,6},{5,7},{6,4},{7,5},{8,10},{9,11},{10,... | collective-permute-start | bytes 688136 | tf_op jit(solution)/shard_map/scatter/ppermute | solution.py:27
  125.1 2.7 %collective-permute-start.27 = (bf16[8,16,896]{2,1,0:T(8,128)(2,1)}, bf16[8,16,896]{2,1,0:T(8,128)(2,1)S(1)}, u32[]{:S(2)}, u32[]{:S(2)}) collective-permute-start(bf16[8,16,896]{2,1,0:T(8,128)(2,1)} %get-tuple-element.76), channel_id=1, source_target_pairs={{0,12},{1,13},{2,14},{3,15},{4,0},{5,1},{6,2},{7,3},{8,4},{9,5},{1... | collective-permute-start | bytes 688136 | tf_op jit(solution)/shard_map/scatter/ppermute | solution.py:22
  130.1 2.4 %collective-permute-done.26.refs_3_ = bf16[8,16,896]{2,1,0:T(8,128)(2,1)S(1)} collective-permute-done((bf16[8,16,896]{2,1,0:T(8,128)(2,1)}, bf16[8,16,896]{2,1,0:T(8,128)(2,1)S(1)}, u32[]{:S(2)}, u32[]{:S(2)}) %collective-permute-start.26) | collective-permute-done | bytes 229408 | tf_op jit(solution)/shard_map/scatter/ppermute | solution.py:27
  132.5 1.9 %collective-permute-done.27.refs_5_ = bf16[8,16,896]{2,1,0:T(8,128)(2,1)S(1)} collective-permute-done((bf16[8,16,896]{2,1,0:T(8,128)(2,1)}, bf16[8,16,896]{2,1,0:T(8,128)(2,1)S(1)}, u32[]{:S(2)}, u32[]{:S(2)}) %collective-permute-start.27) | collective-permute-done | bytes 229408 | tf_op jit(solution)/shard_map/scatter/ppermute | solution.py:22
  135.6 2.4 %collective-permute-done.29.refs_7_ = bf16[8,16,896]{2,1,0:T(8,128)(2,1)S(1)} collective-permute-done((bf16[8,16,896]{2,1,0:T(8,128)(2,1)}, bf16[8,16,896]{2,1,0:T(8,128)(2,1)S(1)}, u32[]{:S(2)}, u32[]{:S(2)}) %collective-permute-start.29) | collective-permute-done | bytes 229408 | tf_op jit(solution)/shard_map/scatter/ppermute | solution.py:22
  141.2 2.2 %collective-permute-start.33 = (bf16[2,16,896]{2,1,0:T(8,128)(2,1)S(1)}, bf16[2,16,896]{2,1,0:T(8,128)(2,1)S(1)}, u32[]{:S(2)}, u32[]{:S(2)}) collective-permute-start(bf16[2,16,896]{2,1,0:T(8,128)(2,1)S(1)} %get-tuple-element.84), channel_id=1, source_target_pairs={{0,3},{1,0},{2,1},{3,2},{4,7},{5,4},{6,5},{7,6},{8,11},{9,8},{10,9... | collective-permute-start | bytes 172040 | tf_op jit(solution)/shard_map/scatter/ppermute | solution.py:27
  145.7 3.4 %collective-permute-done.34.refs_6_ = bf16[2,16,896]{2,1,0:T(8,128)(2,1)S(1)} collective-permute-done((bf16[2,16,896]{2,1,0:T(8,128)(2,1)S(1)}, bf16[2,16,896]{2,1,0:T(8,128)(2,1)S(1)}, u32[]{:S(2)}, u32[]{:S(2)}) %collective-permute-start.34) | collective-permute-done | bytes 57376 | tf_op jit(solution)/shard_map/scatter/ppermute | solution.py:27
  149.4 2.1 %scatter.5 = f32[4,128,896]{2,1,0:T(8,128)} custom-call(s32[8,2]{1,0:T(8,128)S(1)} %copy.23.owner, s32[8,2]{1,0:T(8,128)S(1)} %copy.22.slot, bf16[2,16,896]{2,1,0:T(8,128)(2,1)S(1)} %get-tuple-element.79.refs_0_, bf16[2,16,896]{2,1,0:T(8,128)(2,1)S(1)} %collective-permute-done.30.refs_1_, bf16[2,16,896]{2,1,0:T(8,128)(2,1)S(1)} %collective-permute-done.31.refs_2_, ...), custom_call_target="tpu_custom_call" | custom-call | tf_op jit(solution)/shard_map/scatter/pallas_call | solution.py:326
  151.5 3.8 %weights.1 = (f32[4096,256]{1,0:T(8,128)}, f32[896,256]{1,0:T(8,128)}, f32[896,256]{1,0:T(8,128)}) custom-call(bf16[8,736,256]{2,1,0:T(8,128)(2,1)} %all-gather.2.cloned.1.call-done.chunks), custom_call_target="tpu_custom_call" | custom-call | tf_op jit(solution)/shard_map/weights/pallas_call | solution.py:293
  (78 shorter events, 30.2 us)
Async XLA Ops:
  7.2 114.4 %reduce-scatter.2.cloned.1.call-start = ((), (), s32[]{:S(2)}) async-start(), calls=%async_computation.1 | async-start | bytes 3391488 | tf_op jit(solution)/shard_map/weights/reduce_scatter | solution.py:411
  10.7 18.6 %collective-permute-start = (bf16[2,16,896]{2,1,0:T(8,128)(2,1)S(1)}, bf16[2,16,896]{2,1,0:T(8,128)(2,1)S(1)}, u32[]{:S(2)}, u32[]{:S(2)}) collective-permute-start(bf16[2,16,896]{2,1,0:T(8,128)(2,1)S(1)} %get-tuple-element.47), channel_id=1, source_target_pairs={{0,4},{1,5},{2,6},{3,7},{4,8},{5,9},{6,10},{7,11},{8,12},{9,13},{1... | collective-permute-start | bytes 172040 | tf_op jit(solution)/shard_map/gather/ppermute | solution.py:22
  12.3 17.0 %collective-permute-start.1 = (bf16[2,16,896]{2,1,0:T(8,128)(2,1)S(1)}, bf16[2,16,896]{2,1,0:T(8,128)(2,1)S(1)}, u32[]{:S(2)}, u32[]{:S(2)}) collective-permute-start(bf16[2,16,896]{2,1,0:T(8,128)(2,1)S(1)} %get-tuple-element.48), channel_id=1, source_target_pairs={{0,8},{1,9},{2,10},{3,11},{4,12},{5,13},{6,14},{7,15},{8,0},{9,1},... | collective-permute-start | bytes 172040 | tf_op jit(solution)/shard_map/gather/ppermute | solution.py:22
  15.1 14.3 %collective-permute-start.2 = (bf16[2,16,896]{2,1,0:T(8,128)(2,1)S(1)}, bf16[2,16,896]{2,1,0:T(8,128)(2,1)S(1)}, u32[]{:S(2)}, u32[]{:S(2)}) collective-permute-start(bf16[2,16,896]{2,1,0:T(8,128)(2,1)S(1)} %get-tuple-element.49), channel_id=1, source_target_pairs={{0,12},{1,13},{2,14},{3,15},{4,0},{5,1},{6,2},{7,3},{8,4},{9,5},{1... | collective-permute-start | bytes 172040 | tf_op jit(solution)/shard_map/gather/ppermute | solution.py:22
  16.5 5.9 %collective-permute-start.6 = (bf16[2,16,896]{2,1,0:T(8,128)(2,1)S(1)}, bf16[2,16,896]{2,1,0:T(8,128)(2,1)S(1)}, u32[]{:S(2)}, u32[]{:S(2)}) collective-permute-start(bf16[2,16,896]{2,1,0:T(8,128)(2,1)S(1)} %get-tuple-element.51), channel_id=1, source_target_pairs={{0,1},{1,2},{2,3},{3,0},{4,5},{5,6},{6,7},{7,4},{8,9},{9,10},{10,1... | collective-permute-start | bytes 172040 | tf_op jit(solution)/shard_map/gather/ppermute | solution.py:27
  26.6 6.9 %collective-permute-start.11 = (bf16[8,16,896]{2,1,0:T(8,128)(2,1)S(1)}, bf16[8,16,896]{2,1,0:T(8,128)(2,1)S(1)}, u32[]{:S(2)}, u32[]{:S(2)}) collective-permute-start(bf16[8,16,896]{2,1,0:T(8,128)(2,1)S(1)} %constant_dynamic-update-slice_fusion.4.refs_4_), channel_id=1, source_target_pairs={{0,12},{1,13},{2,14},{3,15},{4,0},{5,1},{6,2},{7,3},{8,4},{9,5},{1... | collective-permute-start | bytes 688136 | tf_op jit(solution)/shard_map/gather/ppermute | solution.py:22
  26.8 8.5 %collective-permute-start.10 = (bf16[8,16,896]{2,1,0:T(8,128)(2,1)S(1)}, bf16[8,16,896]{2,1,0:T(8,128)(2,1)S(1)}, u32[]{:S(2)}, u32[]{:S(2)}) collective-permute-start(bf16[8,16,896]{2,1,0:T(8,128)(2,1)S(1)} %constant_dynamic-update-slice_fusion.4.refs_4_), channel_id=1, source_target_pairs={{0,8},{1,9},{2,10},{3,11},{4,12},{5,13},{6,14},{7,15},{8,0},{9,1},... | collective-permute-start | bytes 688136 | tf_op jit(solution)/shard_map/gather/ppermute | solution.py:22
  29.3 8.3 %collective-permute-start.9 = (bf16[8,16,896]{2,1,0:T(8,128)(2,1)S(1)}, bf16[8,16,896]{2,1,0:T(8,128)(2,1)S(1)}, u32[]{:S(2)}, u32[]{:S(2)}) collective-permute-start(bf16[8,16,896]{2,1,0:T(8,128)(2,1)S(1)} %constant_dynamic-update-slice_fusion.4.refs_4_), channel_id=1, source_target_pairs={{0,4},{1,5},{2,6},{3,7},{4,8},{5,9},{6,10},{7,11},{8,12},{9,13},{1... | collective-permute-start | bytes 688136 | tf_op jit(solution)/shard_map/gather/ppermute | solution.py:22
  29.4 9.1 %collective-permute-start.5 = (bf16[8,16,896]{2,1,0:T(8,128)(2,1)S(1)}, bf16[8,16,896]{2,1,0:T(8,128)(2,1)S(1)}, u32[]{:S(2)}, u32[]{:S(2)}) collective-permute-start(bf16[8,16,896]{2,1,0:T(8,128)(2,1)S(1)} %constant_dynamic-update-slice_fusion.refs_0_), channel_id=1, source_target_pairs={{0,3},{1,0},{2,1},{3,2},{4,7},{5,4},{6,5},{7,6},{8,11},{9,8},{10,9... | collective-permute-start | bytes 688136 | tf_op jit(solution)/shard_map/gather/ppermute | solution.py:27
  32.0 7.8 %collective-permute-start.4 = (bf16[8,16,896]{2,1,0:T(8,128)(2,1)S(1)}, bf16[8,16,896]{2,1,0:T(8,128)(2,1)S(1)}, u32[]{:S(2)}, u32[]{:S(2)}) collective-permute-start(bf16[8,16,896]{2,1,0:T(8,128)(2,1)S(1)} %constant_dynamic-update-slice_fusion.refs_0_), channel_id=1, source_target_pairs={{0,2},{1,3},{2,0},{3,1},{4,6},{5,7},{6,4},{7,5},{8,10},{9,11},{10,... | collective-permute-start | bytes 688136 | tf_op jit(solution)/shard_map/gather/ppermute | solution.py:27
  33.5 8.6 %collective-permute-start.3 = (bf16[8,16,896]{2,1,0:T(8,128)(2,1)S(1)}, bf16[8,16,896]{2,1,0:T(8,128)(2,1)S(1)}, u32[]{:S(2)}, u32[]{:S(2)}) collective-permute-start(bf16[8,16,896]{2,1,0:T(8,128)(2,1)S(1)} %constant_dynamic-update-slice_fusion.refs_0_), channel_id=1, source_target_pairs={{0,1},{1,2},{2,3},{3,0},{4,5},{5,6},{6,7},{7,4},{8,9},{9,10},{10,1... | collective-permute-start | bytes 688136 | tf_op jit(solution)/shard_map/gather/ppermute | solution.py:27
  44.1 17.4 %collective-permute-start.14 = (bf16[16,16,896]{2,1,0:T(8,128)(2,1)S(1)}, bf16[16,16,896]{2,1,0:T(8,128)(2,1)S(1)}, u32[]{:S(2)}, u32[]{:S(2)}) collective-permute-start(bf16[16,16,896]{2,1,0:T(8,128)(2,1)S(1)} %get-tuple-element.54.refs_0_), channel_id=1, source_target_pairs={{0,12},{1,13},{2,14},{3,15},{4,0},{5,1},{6,2},{7,3},{8,4},{9,5},{1... | collective-permute-start | bytes 1376264 | tf_op jit(solution)/shard_map/gather/ppermute | solution.py:22
  48.5 16.5 %collective-permute-start.13 = (bf16[16,16,896]{2,1,0:T(8,128)(2,1)S(1)}, bf16[16,16,896]{2,1,0:T(8,128)(2,1)S(1)}, u32[]{:S(2)}, u32[]{:S(2)}) collective-permute-start(bf16[16,16,896]{2,1,0:T(8,128)(2,1)S(1)} %get-tuple-element.54.refs_0_), channel_id=1, source_target_pairs={{0,8},{1,9},{2,10},{3,11},{4,12},{5,13},{6,14},{7,15},{8,0},{9,1},... | collective-permute-start | bytes 1376264 | tf_op jit(solution)/shard_map/gather/ppermute | solution.py:22
  49.9 16.7 %collective-permute-start.12 = (bf16[16,16,896]{2,1,0:T(8,128)(2,1)S(1)}, bf16[16,16,896]{2,1,0:T(8,128)(2,1)S(1)}, u32[]{:S(2)}, u32[]{:S(2)}) collective-permute-start(bf16[16,16,896]{2,1,0:T(8,128)(2,1)S(1)} %get-tuple-element.54.refs_0_), channel_id=1, source_target_pairs={{0,4},{1,5},{2,6},{3,7},{4,8},{5,9},{6,10},{7,11},{8,12},{9,13},{1... | collective-permute-start | bytes 1376264 | tf_op jit(solution)/shard_map/gather/ppermute | solution.py:22
  50.3 16.3 %collective-permute-start.17 = (bf16[16,16,896]{2,1,0:T(8,128)(2,1)S(1)}, bf16[16,16,896]{2,1,0:T(8,128)(2,1)S(1)}, u32[]{:S(2)}, u32[]{:S(2)}) collective-permute-start(bf16[16,16,896]{2,1,0:T(8,128)(2,1)S(1)} %get-tuple-element.55.refs_4_), channel_id=1, source_target_pairs={{0,3},{1,0},{2,1},{3,2},{4,7},{5,4},{6,5},{7,6},{8,11},{9,8},{10,9... | collective-permute-start | bytes 1376264 | tf_op jit(solution)/shard_map/gather/ppermute | solution.py:27
  51.4 15.2 %collective-permute-start.16 = (bf16[16,16,896]{2,1,0:T(8,128)(2,1)S(1)}, bf16[16,16,896]{2,1,0:T(8,128)(2,1)S(1)}, u32[]{:S(2)}, u32[]{:S(2)}) collective-permute-start(bf16[16,16,896]{2,1,0:T(8,128)(2,1)S(1)} %get-tuple-element.55.refs_4_), channel_id=1, source_target_pairs={{0,2},{1,3},{2,0},{3,1},{4,6},{5,7},{6,4},{7,5},{8,10},{9,11},{10,... | collective-permute-start | bytes 1376264 | tf_op jit(solution)/shard_map/gather/ppermute | solution.py:27
  61.5 9.7 %collective-permute-start.15 = (bf16[16,16,896]{2,1,0:T(8,128)(2,1)S(1)}, bf16[16,16,896]{2,1,0:T(8,128)(2,1)S(1)}, u32[]{:S(2)}, u32[]{:S(2)}) collective-permute-start(bf16[16,16,896]{2,1,0:T(8,128)(2,1)S(1)} %get-tuple-element.55.refs_4_), channel_id=1, source_target_pairs={{0,1},{1,2},{2,3},{3,0},{4,5},{5,6},{6,7},{7,4},{8,9},{9,10},{10,1... | collective-permute-start | bytes 1376264 | tf_op jit(solution)/shard_map/gather/ppermute | solution.py:27
  84.9 66.6 %all-gather.2.cloned.1.call-start = ((), (), s32[]{:S(2)}) async-start(), calls=%async_computation.2 | async-start | bytes 3391488 | tf_op jit(solution)/shard_map/weights/all_gather | solution.py:419
  84.9 15.8 %collective-permute-start.18 = (bf16[16,16,896]{2,1,0:T(8,128)(2,1)}, bf16[16,16,896]{2,1,0:T(8,128)(2,1)S(1)}, u32[]{:S(2)}, u32[]{:S(2)}) collective-permute-start(bf16[16,16,896]{2,1,0:T(8,128)(2,1)} %get-tuple-element.59), channel_id=1, source_target_pairs={{0,12},{1,13},{2,14},{3,15},{4,0},{5,1},{6,2},{7,3},{8,4},{9,5},{1... | collective-permute-start | bytes 1376264 | tf_op jit(solution)/shard_map/scatter/ppermute | solution.py:22
  88.7 12.3 %collective-permute-start.19 = (bf16[16,16,896]{2,1,0:T(8,128)(2,1)}, bf16[16,16,896]{2,1,0:T(8,128)(2,1)S(1)}, u32[]{:S(2)}, u32[]{:S(2)}) collective-permute-start(bf16[16,16,896]{2,1,0:T(8,128)(2,1)} %get-tuple-element.60), channel_id=1, source_target_pairs={{0,8},{1,9},{2,10},{3,11},{4,12},{5,13},{6,14},{7,15},{8,0},{9,1},... | collective-permute-start | bytes 1376264 | tf_op jit(solution)/shard_map/scatter/ppermute | solution.py:22
  88.7 14.8 %collective-permute-start.20 = (bf16[16,16,896]{2,1,0:T(8,128)(2,1)}, bf16[16,16,896]{2,1,0:T(8,128)(2,1)S(1)}, u32[]{:S(2)}, u32[]{:S(2)}) collective-permute-start(bf16[16,16,896]{2,1,0:T(8,128)(2,1)} %get-tuple-element.61), channel_id=1, source_target_pairs={{0,4},{1,5},{2,6},{3,7},{4,8},{5,9},{6,10},{7,11},{8,12},{9,13},{1... | collective-permute-start | bytes 1376264 | tf_op jit(solution)/shard_map/scatter/ppermute | solution.py:22
  89.6 13.9 %collective-permute-start.21 = (bf16[16,16,896]{2,1,0:T(8,128)(2,1)}, bf16[16,16,896]{2,1,0:T(8,128)(2,1)S(1)}, u32[]{:S(2)}, u32[]{:S(2)}) collective-permute-start(bf16[16,16,896]{2,1,0:T(8,128)(2,1)} %get-tuple-element.63), channel_id=1, source_target_pairs={{0,3},{1,0},{2,1},{3,2},{4,7},{5,4},{6,5},{7,6},{8,11},{9,8},{10,9... | collective-permute-start | bytes 1376264 | tf_op jit(solution)/shard_map/scatter/ppermute | solution.py:27
  89.6 14.3 %collective-permute-start.22 = (bf16[16,16,896]{2,1,0:T(8,128)(2,1)}, bf16[16,16,896]{2,1,0:T(8,128)(2,1)S(1)}, u32[]{:S(2)}, u32[]{:S(2)}) collective-permute-start(bf16[16,16,896]{2,1,0:T(8,128)(2,1)} %get-tuple-element.64), channel_id=1, source_target_pairs={{0,2},{1,3},{2,0},{3,1},{4,6},{5,7},{6,4},{7,5},{8,10},{9,11},{10,... | collective-permute-start | bytes 1376264 | tf_op jit(solution)/shard_map/scatter/ppermute | solution.py:27
  100.8 9.7 %collective-permute-start.23 = (bf16[16,16,896]{2,1,0:T(8,128)(2,1)S(1)}, bf16[16,16,896]{2,1,0:T(8,128)(2,1)S(1)}, u32[]{:S(2)}, u32[]{:S(2)}) collective-permute-start(bf16[16,16,896]{2,1,0:T(8,128)(2,1)S(1)} %copy-done.5), channel_id=1, source_target_pairs={{0,1},{1,2},{2,3},{3,0},{4,5},{5,6},{6,7},{7,4},{8,9},{9,10},{10,1... | collective-permute-start | bytes 1376264 | tf_op jit(solution)/shard_map/scatter/ppermute | solution.py:27
  113.9 6.2 %collective-permute-start.24 = (bf16[8,16,896]{2,1,0:T(8,128)(2,1)}, bf16[8,16,896]{2,1,0:T(8,128)(2,1)S(1)}, u32[]{:S(2)}, u32[]{:S(2)}) collective-permute-start(bf16[8,16,896]{2,1,0:T(8,128)(2,1)} %get-tuple-element.66), channel_id=1, source_target_pairs={{0,3},{1,0},{2,1},{3,2},{4,7},{5,4},{6,5},{7,6},{8,11},{9,8},{10,9... | collective-permute-start | bytes 688136 | tf_op jit(solution)/shard_map/scatter/ppermute | solution.py:27
  121.6 8.5 %collective-permute-start.25 = (bf16[8,16,896]{2,1,0:T(8,128)(2,1)}, bf16[8,16,896]{2,1,0:T(8,128)(2,1)S(1)}, u32[]{:S(2)}, u32[]{:S(2)}) collective-permute-start(bf16[8,16,896]{2,1,0:T(8,128)(2,1)} %get-tuple-element.73), channel_id=1, source_target_pairs={{0,2},{1,3},{2,0},{3,1},{4,6},{5,7},{6,4},{7,5},{8,10},{9,11},{10,... | collective-permute-start | bytes 688136 | tf_op jit(solution)/shard_map/scatter/ppermute | solution.py:27
  124.5 8.0 %collective-permute-start.26 = (bf16[8,16,896]{2,1,0:T(8,128)(2,1)}, bf16[8,16,896]{2,1,0:T(8,128)(2,1)S(1)}, u32[]{:S(2)}, u32[]{:S(2)}) collective-permute-start(bf16[8,16,896]{2,1,0:T(8,128)(2,1)} %get-tuple-element.74), channel_id=1, source_target_pairs={{0,1},{1,2},{2,3},{3,0},{4,5},{5,6},{6,7},{7,4},{8,9},{9,10},{10,1... | collective-permute-start | bytes 688136 | tf_op jit(solution)/shard_map/scatter/ppermute | solution.py:27
  125.1 9.3 %collective-permute-start.27 = (bf16[8,16,896]{2,1,0:T(8,128)(2,1)}, bf16[8,16,896]{2,1,0:T(8,128)(2,1)S(1)}, u32[]{:S(2)}, u32[]{:S(2)}) collective-permute-start(bf16[8,16,896]{2,1,0:T(8,128)(2,1)} %get-tuple-element.76), channel_id=1, source_target_pairs={{0,12},{1,13},{2,14},{3,15},{4,0},{5,1},{6,2},{7,3},{8,4},{9,5},{1... | collective-permute-start | bytes 688136 | tf_op jit(solution)/shard_map/scatter/ppermute | solution.py:22
  127.8 7.8 %collective-permute-start.28 = (bf16[8,16,896]{2,1,0:T(8,128)(2,1)}, bf16[8,16,896]{2,1,0:T(8,128)(2,1)S(1)}, u32[]{:S(2)}, u32[]{:S(2)}) collective-permute-start(bf16[8,16,896]{2,1,0:T(8,128)(2,1)} %get-tuple-element.77), channel_id=1, source_target_pairs={{0,8},{1,9},{2,10},{3,11},{4,12},{5,13},{6,14},{7,15},{8,0},{9,1},... | collective-permute-start | bytes 688136 | tf_op jit(solution)/shard_map/scatter/ppermute | solution.py:22
  128.8 9.3 %collective-permute-start.29 = (bf16[8,16,896]{2,1,0:T(8,128)(2,1)}, bf16[8,16,896]{2,1,0:T(8,128)(2,1)S(1)}, u32[]{:S(2)}, u32[]{:S(2)}) collective-permute-start(bf16[8,16,896]{2,1,0:T(8,128)(2,1)} %get-tuple-element.78), channel_id=1, source_target_pairs={{0,4},{1,5},{2,6},{3,7},{4,8},{5,9},{6,10},{7,11},{8,12},{9,13},{1... | collective-permute-start | bytes 688136 | tf_op jit(solution)/shard_map/scatter/ppermute | solution.py:22
  143.4 5.8 %collective-permute-start.34 = (bf16[2,16,896]{2,1,0:T(8,128)(2,1)S(1)}, bf16[2,16,896]{2,1,0:T(8,128)(2,1)S(1)}, u32[]{:S(2)}, u32[]{:S(2)}) collective-permute-start(bf16[2,16,896]{2,1,0:T(8,128)(2,1)S(1)} %get-tuple-element.85), channel_id=1, source_target_pairs={{0,2},{1,3},{2,0},{3,1},{4,6},{5,7},{6,4},{7,5},{8,10},{9,11},{10,... | collective-permute-start | bytes 172040 | tf_op jit(solution)/shard_map/scatter/ppermute | solution.py:27
  143.4 6.0 %collective-permute-start.35 = (bf16[2,16,896]{2,1,0:T(8,128)(2,1)S(1)}, bf16[2,16,896]{2,1,0:T(8,128)(2,1)S(1)}, u32[]{:S(2)}, u32[]{:S(2)}) collective-permute-start(bf16[2,16,896]{2,1,0:T(8,128)(2,1)S(1)} %get-tuple-element.86), channel_id=1, source_target_pairs={{0,1},{1,2},{2,3},{3,0},{4,5},{5,6},{6,7},{7,4},{8,9},{9,10},{10,1... | collective-permute-start | bytes 172040 | tf_op jit(solution)/shard_map/scatter/ppermute | solution.py:27
  (12 other events, 213.1 us)
Sparse Core Ops, SparseCore 0:
  85.0 36.5 reduce-scatter.1
  123.4 26.0 all-gather.1

commit v4 on v3

--- a/solution.py
+++ b/solution.py
@@ -41,8 +41,8 @@
     first = jnp.int32(0)
     second = jnp.int32(0)
     for t in range(NT):
-        hit = owner[t // 2, t % 2] == own
-        tile = slot[t // 2, t % 2]
+        hit = owner[t % 2, t // 2] == own
+        tile = slot[t % 2, t // 2]
         first = jnp.where(hit & (count == 0), tile, first)
         second = jnp.where(hit & (count == 1), tile, second)
         count = count + hit.astype(jnp.int32)
@@ -52,10 +52,10 @@
 def named(owner, x, y):
     found = []
     for t in range(NT):
-        o = owner[t // 2, t % 2]
+        o = owner[t % 2, t // 2]
         rank = jnp.int32(0)
         for e in range(t):
-            rank = rank + (owner[e // 2, e % 2] == o).astype(jnp.int32)
+            rank = rank + (owner[e % 2, e // 2] == o).astype(jnp.int32)
         found.append((apart(x, lax.div(o, SIDE)), apart(y, lax.rem(o, SIDE)), rank))
     return found
 
@@ -64,11 +64,19 @@
     return pl.ds(pl.multiple_of(base + lax.rem(at, SIDE) * SUB, SUB), SUB)
 
 
-def split_kernel(owner, slot, tiles, *refs):
-    outs, (held, sems) = refs[: 2 * SIDE], refs[2 * SIDE :]
+def split_kernel(owner_ref, slot_ref, tiles, *refs):
+    outs, (owner, slot, held, sems) = refs[: 2 * SIDE], refs[2 * SIDE :]
+    copies = [
+        pltpu.make_async_copy(owner_ref, owner, sems.at[0]),
+        pltpu.make_async_copy(slot_ref, slot, sems.at[1]),
+    ]
+    for copy in copies:
+        copy.start()
+    for copy in copies:
+        copy.wait()
     own, x, y = place()
     copies = [
-        pltpu.make_async_copy(tiles.at[tile], held.at[r], sems.at[r])
+        pltpu.make_async_copy(tiles.at[tile], held.at[r], sems.at[2 + r])
         for r, tile in enumerate(my_slots(owner, slot, own))
     ]
     for copy in copies:
@@ -124,16 +132,6 @@
         for k in range(SIDE):
             for r in range(2):
                 outs[k][r] = sum(ref[k * 2 + r].astype(F32) for ref in ins).astype(BF16)
-
-
-def tiles_kernel(owner, slot, *refs):
-    in_a, in_b, out = refs[:SIDE], refs[SIDE : 2 * SIDE], refs[2 * SIDE]
-    own, x, y = place()
-    out[...] = jnp.zeros_like(out)
-    for r, tile in enumerate(my_slots(owner, slot, own)):
-        for k in range(SIDE):
-            out[tile, sub_row(x + k, 0), :] += in_a[k][r].astype(F32)
-            out[tile, sub_row(y + k, SIDE * SUB), :] += in_b[k][r].astype(F32)
 
 
 def dot(a, b, a_dim, b_dim):
@@ -192,7 +190,7 @@
     visible = []
     for s in range(spans):
         span = step * spans + s
-        limit = jnp.where(row < keys // 2, length[span, 0], length[span, 1])
+        limit = jnp.where(row < keys // 2, length[0, span], length[1, span])
         visible.append(jnp.broadcast_to(position < limit, (heads * SPAN, keys)))
     visible = jnp.concatenate(visible, axis=0)
     weights = jnp.where(visible, jnp.exp(score), 0.0)
@@ -257,52 +255,66 @@
             copy.wait()
 
 
-def weights_kernel(chunks, out_q, out_k, out_v, bring, hold, arrive, leave):
+def last_kernel(owner, slot, *refs):
+    in_a, in_b, chunks = refs[:SIDE], refs[SIDE : 2 * SIDE], refs[2 * SIDE]
+    out_q, out_k, out_v, out_t = refs[2 * SIDE + 1 : 2 * SIDE + 5]
+    bring, hold, sums, arrive, leave, leave_t = refs[2 * SIDE + 5 :]
     cut = out_q.shape[0] // (2 * SIDE)
     rest = out_k.shape[0] // SIDE
     count = chunks.shape[0]
     arrivals = [
-        pltpu.make_async_copy(chunks.at[slot], bring.at[slot], arrive.at[slot])
-        for slot in range(count)
+        pltpu.make_async_copy(chunks.at[i], bring.at[i], arrive.at[i]) for i in range(count)
     ]
     for copy in arrivals:
         copy.start()
     copies = []
-    for slot in range(count):
-        z, core = slot // 2, slot % 2
+    for i in range(count):
+        z, core = i // 2, i % 2
         out_e = out_v if core else out_k
-        arrivals[slot].wait()
-        hold[slot] = bring[slot].astype(F32)
+        arrivals[i].wait()
+        hold[i] = bring[i].astype(F32)
         copies += [
             pltpu.make_async_copy(
-                hold.at[slot, pl.ds(0, cut)],
+                hold.at[i, pl.ds(0, cut)],
                 out_q.at[pl.ds((core * SIDE + z) * cut, cut)],
-                leave.at[slot, 0],
+                leave.at[i, 0],
             ),
             pltpu.make_async_copy(
-                hold.at[slot, pl.ds(cut, rest)], out_e.at[pl.ds(z * rest, rest)], leave.at[slot, 1]
+                hold.at[i, pl.ds(cut, rest)], out_e.at[pl.ds(z * rest, rest)], leave.at[i, 1]
             ),
         ]
         copies[-2].start()
         copies[-1].start()
+    own, x, y = place()
+    sums[...] = jnp.zeros_like(sums)
+    for r, tile in enumerate(my_slots(owner, slot, own)):
+        for k in range(SIDE):
+            sums[tile, sub_row(x + k, 0), :] += in_a[k][r].astype(F32)
+            sums[tile, sub_row(y + k, SIDE * SUB), :] += in_b[k][r].astype(F32)
+    copies.append(pltpu.make_async_copy(sums, out_t, leave_t))
+    copies[-1].start()
     for copy in copies:
         copy.wait()
 
 
-def weight_outputs(chunks, shapes):
+def last_outputs(owner, slot, lasts, chunks, shapes):
     return pl.pallas_call(
-        weights_kernel,
+        last_kernel,
         out_shape=[jax.ShapeDtypeStruct(shape, F32) for shape in shapes],
-        in_specs=[pl.BlockSpec(memory_space=pl.ANY)],
-        out_specs=[pl.BlockSpec(memory_space=pl.ANY)] * 3,
+        in_specs=[pl.BlockSpec(memory_space=pltpu.SMEM)] * 2
+        + [pl.BlockSpec(memory_space=pltpu.VMEM)] * len(lasts)
+        + [pl.BlockSpec(memory_space=pl.ANY)],
+        out_specs=[pl.BlockSpec(memory_space=pl.ANY)] * len(shapes),
         scratch_shapes=[
             pltpu.VMEM(chunks.shape, BF16),
             pltpu.VMEM(chunks.shape, F32),
+            pltpu.VMEM(shapes[-1], F32),
             pltpu.SemaphoreType.DMA((2 * SIDE,)),
             pltpu.SemaphoreType.DMA((2 * SIDE, 2)),
+            pltpu.SemaphoreType.DMA,
         ],
         compiler_params=pltpu.CompilerParams(vmem_limit_bytes=VMEM_LIMIT),
-    )(chunks)
+    )(owner, slot, *lasts, chunks)
 
 
 def cut_tiles(owner, slot, tiles):
@@ -310,15 +322,16 @@
     return pl.pallas_call(
         split_kernel,
         out_shape=[jax.ShapeDtypeStruct((2, SUB, width), BF16)] * (2 * SIDE),
-        in_specs=[pl.BlockSpec(memory_space=pltpu.SMEM)] * 2
-        + [pl.BlockSpec(memory_space=pl.ANY)],
+        in_specs=[pl.BlockSpec(memory_space=pl.ANY)] * 3,
         out_specs=[pl.BlockSpec(memory_space=pltpu.VMEM)] * (2 * SIDE),
         scratch_shapes=[
+            pltpu.SMEM(owner.shape, jnp.int32),
+            pltpu.SMEM(slot.shape, jnp.int32),
             pltpu.VMEM((2,) + tiles.shape[1:], BF16),
-            pltpu.SemaphoreType.DMA((2,)),
+            pltpu.SemaphoreType.DMA((4,)),
         ],
         compiler_params=pltpu.CompilerParams(vmem_limit_bytes=VMEM_LIMIT),
-    )(owner, slot, pltpu.with_memory_space_constraint(tiles, pltpu.HBM))
+    )(*(pltpu.with_memory_space_constraint(v, pltpu.HBM) for v in (owner, slot, tiles)))
 
 
 def call(kernel, scalars, ins, outs, kept=None):
@@ -336,7 +349,7 @@
 
 
 def attend(key_length, parts, query, upstream, weight, queries_in):
-    spans = key_length.shape[0]
+    spans = key_length.shape[1]
     width = weight.shape[0]
     columns = query.shape[1]
     depth = queries_in.shape[1]
@@ -384,6 +397,9 @@
 ):
     width = tiles.shape[2]
     steps = range(1, SIDE)
+    neighbour_owner, neighbour_slot, key_length = (
+        value.T for value in (neighbour_owner, neighbour_slot, key_length)
+    )
     pair = ((2, SUB, width), BF16)
     line = ((2 * SIDE, SUB, width), BF16)
     with jax.named_scope("gather"):
@@ -418,18 +434,18 @@
     with jax.named_scope("weights"):
         chunks = lax.all_gather(share, "dp", tiled=True)
         chunks = pltpu.with_memory_space_constraint(chunks, pltpu.HBM)
-        grads = weight_outputs(chunks, (w_query.shape, w_key.shape, w_value.shape))
     with jax.named_scope("scatter"):
         mine = call(owners_sum_kernel, (), home_a + home_b, [pair] * 8)
         last_a = [mine[0]] + [along_x(mine[k], -k) for k in steps]
         last_b = [mine[SIDE]] + [along_y(mine[SIDE + k], -k) for k in steps]
-        (grad_tiles,) = call(
-            tiles_kernel,
-            (neighbour_owner, neighbour_slot),
+        outs = last_outputs(
+            neighbour_owner,
+            neighbour_slot,
             last_a + last_b,
-            [(tiles.shape, F32)],
+            chunks,
+            (w_query.shape, w_key.shape, w_value.shape, tiles.shape),
         )
-    return (context, *grads, grad_tiles)
+    return (context, *outs)
 
 
 def solution(mesh):

time: 163 us -> 162 us (level)
  waiting for transfers between devices: 70.9 us -> 73.3 us
    pallas_call x4 -> x3, Pallas kernels: 7.68 us -> 5.48 us  [call(): pl.pallas_call(kernel, out_shape=[jax.ShapeDtypeStruct(*out) if kept is N...]
  transfers between devices with their start and end apart: 38 -> 38, of which waited for: 27 -> 27; matrix products, arithmetic and copies ran while one was open for 3% -> 2% of each run, Pallas kernels for 4% -> 2%
where the time goes in v4:
time: 162 us; the launch traced here: 161 us
  waiting for transfers between devices  73.3 us (45%)
  starting transfers between devices  42.7 us (26%)
  Pallas kernels  26 us (16%)
  between operations  14.2 us (9%)
  matrix products  3.43 us (2%)
    ppermute x18, waiting for transfers between devices, along_x(): return lax.ppermute(value, 'enc', pairs)  38.5 us
    ppermute x18, waiting for transfers between devices, along_y(): return lax.ppermute(value, 'enc', pairs)  33.5 us
    ppermute x18, starting transfers between devices, along_x(): return lax.ppermute(value, 'enc', pairs)  25.5 us
    ppermute x18, starting transfers between devices, along_y(): return lax.ppermute(value, 'enc', pairs)  17.1 us
    pallas_call x1, Pallas kernels, attend(): pl.pallas_call(attention_kernel, grid_spec=pltpu.PrefetchScalarGridSpec(n...  13.6 us
    pallas_call x3, Pallas kernels, call(): pl.pallas_call(kernel, out_shape=[jax.ShapeDtypeStruct(*out) if kept is N...  5.48 us
    pallas_call x1, Pallas kernels, last_outputs(): pl.pallas_call(last_kernel, out_shape=[jax.ShapeDtypeStruct(shape, F32) f...  4.98 us
    dot_general x1, matrix products, body(): jnp.dot(queries_in, w_query, preferred_element_type=F32).astype(BF16)  3.43 us
  transfers between devices with their start and end apart: 38, of which 27 were waited for; matrix products, arithmetic and copies ran while one was open for 2% of the time, Pallas kernels for 2%

profile of v4, /device:TPU:0, one launch (start us, length us, event | category | flops | bytes accessed | tf_op | source)
XLA Modules:
  0.0 160.6 jit_solution(4173568745411555379)
XLA Ops:
  7.2 2.0 %gather.2 = (bf16[2,16,896]{2,1,0:T(8,128)(2,1)S(1)}, bf16[2,16,896]{2,1,0:T(8,128)(2,1)S(1)}, bf16[2,16,896]{2,1,0:T(8,128)(2,1)S(1)}, bf16[2,16,896]{2,1,0:T(8...) custom-call(s32[2,8]{1,0:T(2,128)} %bitcast.5, ...), custom_call_target="tpu_custom_call" | custom-call | tf_op jit(solution)/shard_map/gather/pallas_call | solution.py:322
  9.3 1.6 %collective-permute-start = (bf16[2,16,896]{2,1,0:T(8,128)(2,1)S(1)}, bf16[2,16,896]{2,1,0:T(8,128)(2,1)S(1)}, u32[]{:S(2)}, u32[]{:S(2)}) collective-permute-start(bf16[2,16,896]{2,1,0:T(8,128)(2,1)S(1)} %get-tuple-element.48), channel_id=1, source_target_pairs={{0,4},{1,5},{2,6},{3,7},{4,8},{5,9},{6,10},{7,11},{8,12},{9,13},{1... | collective-permute-start | bytes 172040 | tf_op jit(solution)/shard_map/gather/ppermute | solution.py:22
  10.9 2.7 %collective-permute-start.1 = (bf16[2,16,896]{2,1,0:T(8,128)(2,1)S(1)}, bf16[2,16,896]{2,1,0:T(8,128)(2,1)S(1)}, u32[]{:S(2)}, u32[]{:S(2)}) collective-permute-start(bf16[2,16,896]{2,1,0:T(8,128)(2,1)S(1)} %get-tuple-element.49), channel_id=1, source_target_pairs={{0,8},{1,9},{2,10},{3,11},{4,12},{5,13},{6,14},{7,15},{8,0},{9,1},... | collective-permute-start | bytes 172040 | tf_op jit(solution)/shard_map/gather/ppermute | solution.py:22
  15.1 1.6 collective-permute-start.6
  16.7 2.9 %collective-permute-start.7 = (bf16[2,16,896]{2,1,0:T(8,128)(2,1)S(1)}, bf16[2,16,896]{2,1,0:T(8,128)(2,1)S(1)}, u32[]{:S(2)}, u32[]{:S(2)}) collective-permute-start(bf16[2,16,896]{2,1,0:T(8,128)(2,1)S(1)} %get-tuple-element.53), channel_id=1, source_target_pairs={{0,2},{1,3},{2,0},{3,1},{4,6},{5,7},{6,4},{7,5},{8,10},{9,11},{10,... | collective-permute-start | bytes 172040 | tf_op jit(solution)/shard_map/gather/ppermute | solution.py:27
  22.3 2.8 %collective-permute-done.8 = bf16[2,16,896]{2,1,0:T(8,128)(2,1)S(1)} collective-permute-done((bf16[2,16,896]{2,1,0:T(8,128)(2,1)S(1)}, bf16[2,16,896]{2,1,0:T(8,128)(2,1)S(1)}, u32[]{:S(2)}, u32[]{:S(2)}) %collective-permute-start.8) | collective-permute-done | bytes 57376 | tf_op jit(solution)/shard_map/gather/ppermute | solution.py:27
  25.3 2.5 %collective-permute-start.10 = (bf16[8,16,896]{2,1,0:T(8,128)(2,1)S(1)}, bf16[8,16,896]{2,1,0:T(8,128)(2,1)S(1)}, u32[]{:S(2)}, u32[]{:S(2)}) collective-permute-start(bf16[8,16,896]{2,1,0:T(8,128)(2,1)S(1)} %constant_dynamic-update-slice_fusion.4.refs_4_), channel_id=1, source_target_pairs={{0,8},{1,9},{2,10},{3,11},{4,12},{5,13},{6,14},{7,15},{8,0},{9,1},... | collective-permute-start | bytes 688136 | tf_op jit(solution)/shard_map/gather/ppermute | solution.py:22
  28.0 2.6 %collective-permute-start.5 = (bf16[8,16,896]{2,1,0:T(8,128)(2,1)S(1)}, bf16[8,16,896]{2,1,0:T(8,128)(2,1)S(1)}, u32[]{:S(2)}, u32[]{:S(2)}) collective-permute-start(bf16[8,16,896]{2,1,0:T(8,128)(2,1)S(1)} %constant_dynamic-update-slice_fusion.refs_0_), channel_id=1, source_target_pairs={{0,3},{1,0},{2,1},{3,2},{4,7},{5,4},{6,5},{7,6},{8,11},{9,8},{10,9... | collective-permute-start | bytes 688136 | tf_op jit(solution)/shard_map/gather/ppermute | solution.py:27
  30.5 1.6 collective-permute-done.11.refs_7_
  32.2 1.6 %collective-permute-done.10.refs_6_ = bf16[8,16,896]{2,1,0:T(8,128)(2,1)S(1)} collective-permute-done((bf16[8,16,896]{2,1,0:T(8,128)(2,1)S(1)}, bf16[8,16,896]{2,1,0:T(8,128)(2,1)S(1)}, u32[]{:S(2)}, u32[]{:S(2)}) %collective-permute-start.10) | collective-permute-done | bytes 229408 | tf_op jit(solution)/shard_map/gather/ppermute | solution.py:22
  33.8 2.4 %collective-permute-done.9.refs_5_ = bf16[8,16,896]{2,1,0:T(8,128)(2,1)S(1)} collective-permute-done((bf16[8,16,896]{2,1,0:T(8,128)(2,1)S(1)}, bf16[8,16,896]{2,1,0:T(8,128)(2,1)S(1)}, u32[]{:S(2)}, u32[]{:S(2)}) %collective-permute-start.9) | collective-permute-done | bytes 229408 | tf_op jit(solution)/shard_map/gather/ppermute | solution.py:22
  38.4 2.4 %collective-permute-done.3.refs_1_ = bf16[8,16,896]{2,1,0:T(8,128)(2,1)S(1)} collective-permute-done((bf16[8,16,896]{2,1,0:T(8,128)(2,1)S(1)}, bf16[8,16,896]{2,1,0:T(8,128)(2,1)S(1)}, u32[]{:S(2)}, u32[]{:S(2)}) %collective-permute-start.3) | collective-permute-done | bytes 229408 | tf_op jit(solution)/shard_map/gather/ppermute | solution.py:27
  41.4 1.9 %gather.3 = (bf16[16,16,896]{2,1,0:T(8,128)(2,1)S(1)}, bf16[16,16,896]{2,1,0:T(8,128)(2,1)S(1)}) custom-call(s32[2,8]{1,0:T(2,128)S(1)} %bitcast.6, bf16[8,16,896]{2,1,0:T(8,128)(2,1)S(1)} %constant_dynamic-update-slice_fusion.refs_0_, bf16[8,16,896]{2,1,0:T(8,128)(2,1)S(1)} %collective-permute-done.3.refs_1_, ...), custom_call_target="tpu_custom_call" | custom-call | tf_op jit(solution)/shard_map/gather/pallas_call | solution.py:339
  43.3 3.1 %collective-permute-start.14 = (bf16[16,16,896]{2,1,0:T(8,128)(2,1)S(1)}, bf16[16,16,896]{2,1,0:T(8,128)(2,1)S(1)}, u32[]{:S(2)}, u32[]{:S(2)}) collective-permute-start(bf16[16,16,896]{2,1,0:T(8,128)(2,1)S(1)} %get-tuple-element.55.refs_0_), channel_id=1, source_target_pairs={{0,12},{1,13},{2,14},{3,15},{4,0},{5,1},{6,2},{7,3},{8,4},{9,5},{1... | collective-permute-start | bytes 1376264 | tf_op jit(solution)/shard_map/gather/ppermute | solution.py:22
  49.3 11.4 %collective-permute-done.14.refs_3_ = bf16[16,16,896]{2,1,0:T(8,128)(2,1)S(1)} collective-permute-done((bf16[16,16,896]{2,1,0:T(8,128)(2,1)S(1)}, bf16[16,16,896]{2,1,0:T(8,128)(2,1)S(1)}, u32[]{:S(2)}, u32[]{:S(2)}) %collective-permute-start.14) | collective-permute-done | bytes 458784 | tf_op jit(solution)/shard_map/gather/ppermute | solution.py:22
  60.7 3.4 %convolution_convert_fusion.refs_8_ = bf16[512,256]{1,0:T(8,128)(2,1)S(1)} fusion(bf16[512,4096]{1,0:T(8,128)(2,1)} %refs_11_.1, bf16[4096,256]{1,0:T(8,128)(2,1)S(1)} %copy-done), kind=kOutput, calls=%fused_computation | convolution fusion | flops 1073872896 | bytes 6553600 | tf_op jit(solution)/shard_map/dot_general | solution.py:417
  64.6 5.9 %collective-permute-done.15.refs_5_ = bf16[16,16,896]{2,1,0:T(8,128)(2,1)S(1)} collective-permute-done((bf16[16,16,896]{2,1,0:T(8,128)(2,1)S(1)}, bf16[16,16,896]{2,1,0:T(8,128)(2,1)S(1)}, u32[]{:S(2)}, u32[]{:S(2)}) %collective-permute-start.15) | collective-permute-done | bytes 458784 | tf_op jit(solution)/shard_map/gather/ppermute | solution.py:27
  70.4 13.6 %attend.1 = (bf16[512,256]{1,0:T(8,128)(2,1)}, bf16[16,16,896]{2,1,0:T(8,128)(2,1)}, bf16[16,16,896]{2,1,0:T(8,128)(2,1)}, bf16[16,16,896]{2,1,0:T(8,128)(2,1)},...) custom-call(s32[2,8]{1,0:T(2,128)S(1)} %bitcast.11, ...), custom_call_target="tpu_custom_call" | custom-call | tf_op jit(solution)/shard_map/attend/pallas_call | solution.py:359
  84.1 3.7 %collective-permute-start.18 = (bf16[16,16,896]{2,1,0:T(8,128)(2,1)}, bf16[16,16,896]{2,1,0:T(8,128)(2,1)S(1)}, u32[]{:S(2)}, u32[]{:S(2)}) collective-permute-start(bf16[16,16,896]{2,1,0:T(8,128)(2,1)} %get-tuple-element.59), channel_id=1, source_target_pairs={{0,12},{1,13},{2,14},{3,15},{4,0},{5,1},{6,2},{7,3},{8,4},{9,5},{1... | collective-permute-start | bytes 1376264 | tf_op jit(solution)/shard_map/scatter/ppermute | solution.py:22
  89.7 10.8 %collective-permute-done.18.refs_1_ = bf16[16,16,896]{2,1,0:T(8,128)(2,1)S(1)} collective-permute-done((bf16[16,16,896]{2,1,0:T(8,128)(2,1)}, bf16[16,16,896]{2,1,0:T(8,128)(2,1)S(1)}, u32[]{:S(2)}, u32[]{:S(2)}) %collective-permute-start.18) | collective-permute-done | bytes 458784 | tf_op jit(solution)/shard_map/scatter/ppermute | solution.py:22
  100.5 3.3 %collective-permute-done.20.refs_3_ = bf16[16,16,896]{2,1,0:T(8,128)(2,1)S(1)} collective-permute-done((bf16[16,16,896]{2,1,0:T(8,128)(2,1)}, bf16[16,16,896]{2,1,0:T(8,128)(2,1)S(1)}, u32[]{:S(2)}, u32[]{:S(2)}) %collective-permute-start.20) | collective-permute-done | bytes 458784 | tf_op jit(solution)/shard_map/scatter/ppermute | solution.py:22
  103.8 6.4 %collective-permute-done.23.refs_7_ = bf16[16,16,896]{2,1,0:T(8,128)(2,1)S(1)} collective-permute-done((bf16[16,16,896]{2,1,0:T(8,128)(2,1)S(1)}, bf16[16,16,896]{2,1,0:T(8,128)(2,1)S(1)}, u32[]{:S(2)}, u32[]{:S(2)}) %collective-permute-start.23) | collective-permute-done | bytes 458784 | tf_op jit(solution)/shard_map/scatter/ppermute | solution.py:27
  110.2 3.3 %scatter.3 = (bf16[8,16,896]{2,1,0:T(8,128)(2,1)S(1)}, bf16[8,16,896]{2,1,0:T(8,128)(2,1)}, bf16[8,16,896]{2,1,0:T(8,128)(2,1)}, bf16[8,16,896]{2,1,0:T(8,128)(2...) custom-call(s32[2,8]{1,0:T(2,128)S(1)} %bitcast.7, ...), custom_call_target="tpu_custom_call" | custom-call | tf_op jit(solution)/shard_map/scatter/pallas_call | solution.py:339
  113.8 5.9 %collective-permute-done.24.refs_1_ = bf16[8,16,896]{2,1,0:T(8,128)(2,1)S(1)} collective-permute-done((bf16[8,16,896]{2,1,0:T(8,128)(2,1)}, bf16[8,16,896]{2,1,0:T(8,128)(2,1)S(1)}, u32[]{:S(2)}, u32[]{:S(2)}) %collective-permute-start.24) | collective-permute-done | bytes 229408 | tf_op jit(solution)/shard_map/scatter/ppermute | solution.py:27
  120.7 2.9 %collective-permute-start.25 = (bf16[8,16,896]{2,1,0:T(8,128)(2,1)}, bf16[8,16,896]{2,1,0:T(8,128)(2,1)S(1)}, u32[]{:S(2)}, u32[]{:S(2)}) collective-permute-start(bf16[8,16,896]{2,1,0:T(8,128)(2,1)} %get-tuple-element.70), channel_id=1, source_target_pairs={{0,2},{1,3},{2,0},{3,1},{4,6},{5,7},{6,4},{7,5},{8,10},{9,11},{10,... | collective-permute-start | bytes 688136 | tf_op jit(solution)/shard_map/scatter/ppermute | solution.py:27
  124.2 2.7 %collective-permute-start.27 = (bf16[8,16,896]{2,1,0:T(8,128)(2,1)}, bf16[8,16,896]{2,1,0:T(8,128)(2,1)S(1)}, u32[]{:S(2)}, u32[]{:S(2)}) collective-permute-start(bf16[8,16,896]{2,1,0:T(8,128)(2,1)} %get-tuple-element.73), channel_id=1, source_target_pairs={{0,12},{1,13},{2,14},{3,15},{4,0},{5,1},{6,2},{7,3},{8,4},{9,5},{1... | collective-permute-start | bytes 688136 | tf_op jit(solution)/shard_map/scatter/ppermute | solution.py:22
  129.5 2.4 %collective-permute-done.26.refs_3_ = bf16[8,16,896]{2,1,0:T(8,128)(2,1)S(1)} collective-permute-done((bf16[8,16,896]{2,1,0:T(8,128)(2,1)}, bf16[8,16,896]{2,1,0:T(8,128)(2,1)S(1)}, u32[]{:S(2)}, u32[]{:S(2)}) %collective-permute-start.26) | collective-permute-done | bytes 229408 | tf_op jit(solution)/shard_map/scatter/ppermute | solution.py:27
  131.9 1.5 collective-permute-done.27.refs_5_
  134.8 2.5 %collective-permute-done.29.refs_7_ = bf16[8,16,896]{2,1,0:T(8,128)(2,1)S(1)} collective-permute-done((bf16[8,16,896]{2,1,0:T(8,128)(2,1)}, bf16[8,16,896]{2,1,0:T(8,128)(2,1)S(1)}, u32[]{:S(2)}, u32[]{:S(2)}) %collective-permute-start.29) | collective-permute-done | bytes 229408 | tf_op jit(solution)/shard_map/scatter/ppermute | solution.py:22
  140.4 2.1 %collective-permute-start.33 = (bf16[2,16,896]{2,1,0:T(8,128)(2,1)S(1)}, bf16[2,16,896]{2,1,0:T(8,128)(2,1)S(1)}, u32[]{:S(2)}, u32[]{:S(2)}) collective-permute-start(bf16[2,16,896]{2,1,0:T(8,128)(2,1)S(1)} %get-tuple-element.81), channel_id=1, source_target_pairs={{0,3},{1,0},{2,1},{3,2},{4,7},{5,4},{6,5},{7,6},{8,11},{9,8},{10,9... | collective-permute-start | bytes 172040 | tf_op jit(solution)/shard_map/scatter/ppermute | solution.py:27
  144.9 3.3 %collective-permute-done.34.refs_6_ = bf16[2,16,896]{2,1,0:T(8,128)(2,1)S(1)} collective-permute-done((bf16[2,16,896]{2,1,0:T(8,128)(2,1)S(1)}, bf16[2,16,896]{2,1,0:T(8,128)(2,1)S(1)}, u32[]{:S(2)}, u32[]{:S(2)}) %collective-permute-start.34) | collective-permute-done | bytes 57376 | tf_op jit(solution)/shard_map/scatter/ppermute | solution.py:27
  148.8 5.0 %scatter.5 = (f32[4096,256]{1,0:T(8,128)}, f32[896,256]{1,0:T(8,128)}, f32[896,256]{1,0:T(8,128)}, f32[4,128,896]{2,1,0:T(8,128)}) custom-call(s32[2,8]{1,0:T(2,128)S(1)} %bitcast.8, s32[2,8]{1,0:T(2,128)S(1)} %bitcast.10, bf16[2,16,896]{2,1,0:T(8,128)(2,1)S(1)} %get-tuple-element.76.refs_0_, bf16[2,16,896]{2,1,0:T(8,128)(2,1)S(1)} %collective-permute-done.30.refs_1_, ...), custom_call_target="tpu_custom_call" | custom-call | tf_op jit(solution)/shard_map/scatter/pallas_call | solution.py:301
  (84 shorter events, 24.5 us)
Async XLA Ops:
  7.2 113.5 %reduce-scatter.2.cloned.1.call-start = ((), (), s32[]{:S(2)}) async-start(), calls=%async_computation.1 | async-start | bytes 3391488 | tf_op jit(solution)/shard_map/weights/reduce_scatter | solution.py:427
  9.3 18.6 %collective-permute-start = (bf16[2,16,896]{2,1,0:T(8,128)(2,1)S(1)}, bf16[2,16,896]{2,1,0:T(8,128)(2,1)S(1)}, u32[]{:S(2)}, u32[]{:S(2)}) collective-permute-start(bf16[2,16,896]{2,1,0:T(8,128)(2,1)S(1)} %get-tuple-element.48), channel_id=1, source_target_pairs={{0,4},{1,5},{2,6},{3,7},{4,8},{5,9},{6,10},{7,11},{8,12},{9,13},{1... | collective-permute-start | bytes 172040 | tf_op jit(solution)/shard_map/gather/ppermute | solution.py:22
  10.9 17.0 %collective-permute-start.1 = (bf16[2,16,896]{2,1,0:T(8,128)(2,1)S(1)}, bf16[2,16,896]{2,1,0:T(8,128)(2,1)S(1)}, u32[]{:S(2)}, u32[]{:S(2)}) collective-permute-start(bf16[2,16,896]{2,1,0:T(8,128)(2,1)S(1)} %get-tuple-element.49), channel_id=1, source_target_pairs={{0,8},{1,9},{2,10},{3,11},{4,12},{5,13},{6,14},{7,15},{8,0},{9,1},... | collective-permute-start | bytes 172040 | tf_op jit(solution)/shard_map/gather/ppermute | solution.py:22
  13.6 14.3 %collective-permute-start.2 = (bf16[2,16,896]{2,1,0:T(8,128)(2,1)S(1)}, bf16[2,16,896]{2,1,0:T(8,128)(2,1)S(1)}, u32[]{:S(2)}, u32[]{:S(2)}) collective-permute-start(bf16[2,16,896]{2,1,0:T(8,128)(2,1)S(1)} %get-tuple-element.50), channel_id=1, source_target_pairs={{0,12},{1,13},{2,14},{3,15},{4,0},{5,1},{6,2},{7,3},{8,4},{9,5},{1... | collective-permute-start | bytes 172040 | tf_op jit(solution)/shard_map/gather/ppermute | solution.py:22
  15.1 5.9 %collective-permute-start.6 = (bf16[2,16,896]{2,1,0:T(8,128)(2,1)S(1)}, bf16[2,16,896]{2,1,0:T(8,128)(2,1)S(1)}, u32[]{:S(2)}, u32[]{:S(2)}) collective-permute-start(bf16[2,16,896]{2,1,0:T(8,128)(2,1)S(1)} %get-tuple-element.52), channel_id=1, source_target_pairs={{0,1},{1,2},{2,3},{3,0},{4,5},{5,6},{6,7},{7,4},{8,9},{9,10},{10,1... | collective-permute-start | bytes 172040 | tf_op jit(solution)/shard_map/gather/ppermute | solution.py:27
  25.2 7.0 %collective-permute-start.11 = (bf16[8,16,896]{2,1,0:T(8,128)(2,1)S(1)}, bf16[8,16,896]{2,1,0:T(8,128)(2,1)S(1)}, u32[]{:S(2)}, u32[]{:S(2)}) collective-permute-start(bf16[8,16,896]{2,1,0:T(8,128)(2,1)S(1)} %constant_dynamic-update-slice_fusion.4.refs_4_), channel_id=1, source_target_pairs={{0,12},{1,13},{2,14},{3,15},{4,0},{5,1},{6,2},{7,3},{8,4},{9,5},{1... | collective-permute-start | bytes 688136 | tf_op jit(solution)/shard_map/gather/ppermute | solution.py:22
  25.3 8.5 %collective-permute-start.10 = (bf16[8,16,896]{2,1,0:T(8,128)(2,1)S(1)}, bf16[8,16,896]{2,1,0:T(8,128)(2,1)S(1)}, u32[]{:S(2)}, u32[]{:S(2)}) collective-permute-start(bf16[8,16,896]{2,1,0:T(8,128)(2,1)S(1)} %constant_dynamic-update-slice_fusion.4.refs_4_), channel_id=1, source_target_pairs={{0,8},{1,9},{2,10},{3,11},{4,12},{5,13},{6,14},{7,15},{8,0},{9,1},... | collective-permute-start | bytes 688136 | tf_op jit(solution)/shard_map/gather/ppermute | solution.py:22
  27.9 8.3 %collective-permute-start.9 = (bf16[8,16,896]{2,1,0:T(8,128)(2,1)S(1)}, bf16[8,16,896]{2,1,0:T(8,128)(2,1)S(1)}, u32[]{:S(2)}, u32[]{:S(2)}) collective-permute-start(bf16[8,16,896]{2,1,0:T(8,128)(2,1)S(1)} %constant_dynamic-update-slice_fusion.4.refs_4_), channel_id=1, source_target_pairs={{0,4},{1,5},{2,6},{3,7},{4,8},{5,9},{6,10},{7,11},{8,12},{9,13},{1... | collective-permute-start | bytes 688136 | tf_op jit(solution)/shard_map/gather/ppermute | solution.py:22
  28.0 9.1 %collective-permute-start.5 = (bf16[8,16,896]{2,1,0:T(8,128)(2,1)S(1)}, bf16[8,16,896]{2,1,0:T(8,128)(2,1)S(1)}, u32[]{:S(2)}, u32[]{:S(2)}) collective-permute-start(bf16[8,16,896]{2,1,0:T(8,128)(2,1)S(1)} %constant_dynamic-update-slice_fusion.refs_0_), channel_id=1, source_target_pairs={{0,3},{1,0},{2,1},{3,2},{4,7},{5,4},{6,5},{7,6},{8,11},{9,8},{10,9... | collective-permute-start | bytes 688136 | tf_op jit(solution)/shard_map/gather/ppermute | solution.py:27
  30.5 7.8 %collective-permute-start.4 = (bf16[8,16,896]{2,1,0:T(8,128)(2,1)S(1)}, bf16[8,16,896]{2,1,0:T(8,128)(2,1)S(1)}, u32[]{:S(2)}, u32[]{:S(2)}) collective-permute-start(bf16[8,16,896]{2,1,0:T(8,128)(2,1)S(1)} %constant_dynamic-update-slice_fusion.refs_0_), channel_id=1, source_target_pairs={{0,2},{1,3},{2,0},{3,1},{4,6},{5,7},{6,4},{7,5},{8,10},{9,11},{10,... | collective-permute-start | bytes 688136 | tf_op jit(solution)/shard_map/gather/ppermute | solution.py:27
  32.1 8.6 %collective-permute-start.3 = (bf16[8,16,896]{2,1,0:T(8,128)(2,1)S(1)}, bf16[8,16,896]{2,1,0:T(8,128)(2,1)S(1)}, u32[]{:S(2)}, u32[]{:S(2)}) collective-permute-start(bf16[8,16,896]{2,1,0:T(8,128)(2,1)S(1)} %constant_dynamic-update-slice_fusion.refs_0_), channel_id=1, source_target_pairs={{0,1},{1,2},{2,3},{3,0},{4,5},{5,6},{6,7},{7,4},{8,9},{9,10},{10,1... | collective-permute-start | bytes 688136 | tf_op jit(solution)/shard_map/gather/ppermute | solution.py:27
  43.3 17.4 %collective-permute-start.14 = (bf16[16,16,896]{2,1,0:T(8,128)(2,1)S(1)}, bf16[16,16,896]{2,1,0:T(8,128)(2,1)S(1)}, u32[]{:S(2)}, u32[]{:S(2)}) collective-permute-start(bf16[16,16,896]{2,1,0:T(8,128)(2,1)S(1)} %get-tuple-element.55.refs_0_), channel_id=1, source_target_pairs={{0,12},{1,13},{2,14},{3,15},{4,0},{5,1},{6,2},{7,3},{8,4},{9,5},{1... | collective-permute-start | bytes 1376264 | tf_op jit(solution)/shard_map/gather/ppermute | solution.py:22
  46.5 17.7 %collective-permute-start.13 = (bf16[16,16,896]{2,1,0:T(8,128)(2,1)S(1)}, bf16[16,16,896]{2,1,0:T(8,128)(2,1)S(1)}, u32[]{:S(2)}, u32[]{:S(2)}) collective-permute-start(bf16[16,16,896]{2,1,0:T(8,128)(2,1)S(1)} %get-tuple-element.55.refs_0_), channel_id=1, source_target_pairs={{0,8},{1,9},{2,10},{3,11},{4,12},{5,13},{6,14},{7,15},{8,0},{9,1},... | collective-permute-start | bytes 1376264 | tf_op jit(solution)/shard_map/gather/ppermute | solution.py:22
  47.8 16.7 %collective-permute-start.12 = (bf16[16,16,896]{2,1,0:T(8,128)(2,1)S(1)}, bf16[16,16,896]{2,1,0:T(8,128)(2,1)S(1)}, u32[]{:S(2)}, u32[]{:S(2)}) collective-permute-start(bf16[16,16,896]{2,1,0:T(8,128)(2,1)S(1)} %get-tuple-element.55.refs_0_), channel_id=1, source_target_pairs={{0,4},{1,5},{2,6},{3,7},{4,8},{5,9},{6,10},{7,11},{8,12},{9,13},{1... | collective-permute-start | bytes 1376264 | tf_op jit(solution)/shard_map/gather/ppermute | solution.py:22
  48.3 16.3 %collective-permute-start.17 = (bf16[16,16,896]{2,1,0:T(8,128)(2,1)S(1)}, bf16[16,16,896]{2,1,0:T(8,128)(2,1)S(1)}, u32[]{:S(2)}, u32[]{:S(2)}) collective-permute-start(bf16[16,16,896]{2,1,0:T(8,128)(2,1)S(1)} %get-tuple-element.56.refs_4_), channel_id=1, source_target_pairs={{0,3},{1,0},{2,1},{3,2},{4,7},{5,4},{6,5},{7,6},{8,11},{9,8},{10,9... | collective-permute-start | bytes 1376264 | tf_op jit(solution)/shard_map/gather/ppermute | solution.py:27
  49.3 15.2 %collective-permute-start.16 = (bf16[16,16,896]{2,1,0:T(8,128)(2,1)S(1)}, bf16[16,16,896]{2,1,0:T(8,128)(2,1)S(1)}, u32[]{:S(2)}, u32[]{:S(2)}) collective-permute-start(bf16[16,16,896]{2,1,0:T(8,128)(2,1)S(1)} %get-tuple-element.56.refs_4_), channel_id=1, source_target_pairs={{0,2},{1,3},{2,0},{3,1},{4,6},{5,7},{6,4},{7,5},{8,10},{9,11},{10,... | collective-permute-start | bytes 1376264 | tf_op jit(solution)/shard_map/gather/ppermute | solution.py:27
  60.7 9.7 %collective-permute-start.15 = (bf16[16,16,896]{2,1,0:T(8,128)(2,1)S(1)}, bf16[16,16,896]{2,1,0:T(8,128)(2,1)S(1)}, u32[]{:S(2)}, u32[]{:S(2)}) collective-permute-start(bf16[16,16,896]{2,1,0:T(8,128)(2,1)S(1)} %get-tuple-element.56.refs_4_), channel_id=1, source_target_pairs={{0,1},{1,2},{2,3},{3,0},{4,5},{5,6},{6,7},{7,4},{8,9},{9,10},{10,1... | collective-permute-start | bytes 1376264 | tf_op jit(solution)/shard_map/gather/ppermute | solution.py:27
  84.1 64.7 %all-gather.2.cloned.1.call-start = ((), (), s32[]{:S(2)}) async-start(), calls=%async_computation.2 | async-start | bytes 3391488 | tf_op jit(solution)/shard_map/weights/all_gather | solution.py:435
  84.1 16.4 %collective-permute-start.18 = (bf16[16,16,896]{2,1,0:T(8,128)(2,1)}, bf16[16,16,896]{2,1,0:T(8,128)(2,1)S(1)}, u32[]{:S(2)}, u32[]{:S(2)}) collective-permute-start(bf16[16,16,896]{2,1,0:T(8,128)(2,1)} %get-tuple-element.59), channel_id=1, source_target_pairs={{0,12},{1,13},{2,14},{3,15},{4,0},{5,1},{6,2},{7,3},{8,4},{9,5},{1... | collective-permute-start | bytes 1376264 | tf_op jit(solution)/shard_map/scatter/ppermute | solution.py:22
  87.8 12.7 %collective-permute-start.19 = (bf16[16,16,896]{2,1,0:T(8,128)(2,1)}, bf16[16,16,896]{2,1,0:T(8,128)(2,1)S(1)}, u32[]{:S(2)}, u32[]{:S(2)}) collective-permute-start(bf16[16,16,896]{2,1,0:T(8,128)(2,1)} %get-tuple-element.60), channel_id=1, source_target_pairs={{0,8},{1,9},{2,10},{3,11},{4,12},{5,13},{6,14},{7,15},{8,0},{9,1},... | collective-permute-start | bytes 1376264 | tf_op jit(solution)/shard_map/scatter/ppermute | solution.py:22
  87.8 15.9 %collective-permute-start.20 = (bf16[16,16,896]{2,1,0:T(8,128)(2,1)}, bf16[16,16,896]{2,1,0:T(8,128)(2,1)S(1)}, u32[]{:S(2)}, u32[]{:S(2)}) collective-permute-start(bf16[16,16,896]{2,1,0:T(8,128)(2,1)} %get-tuple-element.61), channel_id=1, source_target_pairs={{0,4},{1,5},{2,6},{3,7},{4,8},{5,9},{6,10},{7,11},{8,12},{9,13},{1... | collective-permute-start | bytes 1376264 | tf_op jit(solution)/shard_map/scatter/ppermute | solution.py:22
  88.8 15.0 %collective-permute-start.21 = (bf16[16,16,896]{2,1,0:T(8,128)(2,1)}, bf16[16,16,896]{2,1,0:T(8,128)(2,1)S(1)}, u32[]{:S(2)}, u32[]{:S(2)}) collective-permute-start(bf16[16,16,896]{2,1,0:T(8,128)(2,1)} %get-tuple-element.63), channel_id=1, source_target_pairs={{0,3},{1,0},{2,1},{3,2},{4,7},{5,4},{6,5},{7,6},{8,11},{9,8},{10,9... | collective-permute-start | bytes 1376264 | tf_op jit(solution)/shard_map/scatter/ppermute | solution.py:27
  88.8 15.0 %collective-permute-start.22 = (bf16[16,16,896]{2,1,0:T(8,128)(2,1)}, bf16[16,16,896]{2,1,0:T(8,128)(2,1)S(1)}, u32[]{:S(2)}, u32[]{:S(2)}) collective-permute-start(bf16[16,16,896]{2,1,0:T(8,128)(2,1)} %get-tuple-element.64), channel_id=1, source_target_pairs={{0,2},{1,3},{2,0},{3,1},{4,6},{5,7},{6,4},{7,5},{8,10},{9,11},{10,... | collective-permute-start | bytes 1376264 | tf_op jit(solution)/shard_map/scatter/ppermute | solution.py:27
  100.5 9.7 %collective-permute-start.23 = (bf16[16,16,896]{2,1,0:T(8,128)(2,1)S(1)}, bf16[16,16,896]{2,1,0:T(8,128)(2,1)S(1)}, u32[]{:S(2)}, u32[]{:S(2)}) collective-permute-start(bf16[16,16,896]{2,1,0:T(8,128)(2,1)S(1)} %copy-done.10), channel_id=1, source_target_pairs={{0,1},{1,2},{2,3},{3,0},{4,5},{5,6},{6,7},{7,4},{8,9},{9,10},{10,1... | collective-permute-start | bytes 1376264 | tf_op jit(solution)/shard_map/scatter/ppermute | solution.py:27
  113.5 6.2 %collective-permute-start.24 = (bf16[8,16,896]{2,1,0:T(8,128)(2,1)}, bf16[8,16,896]{2,1,0:T(8,128)(2,1)S(1)}, u32[]{:S(2)}, u32[]{:S(2)}) collective-permute-start(bf16[8,16,896]{2,1,0:T(8,128)(2,1)} %get-tuple-element.68), channel_id=1, source_target_pairs={{0,3},{1,0},{2,1},{3,2},{4,7},{5,4},{6,5},{7,6},{8,11},{9,8},{10,9... | collective-permute-start | bytes 688136 | tf_op jit(solution)/shard_map/scatter/ppermute | solution.py:27
  120.7 8.7 %collective-permute-start.25 = (bf16[8,16,896]{2,1,0:T(8,128)(2,1)}, bf16[8,16,896]{2,1,0:T(8,128)(2,1)S(1)}, u32[]{:S(2)}, u32[]{:S(2)}) collective-permute-start(bf16[8,16,896]{2,1,0:T(8,128)(2,1)} %get-tuple-element.70), channel_id=1, source_target_pairs={{0,2},{1,3},{2,0},{3,1},{4,6},{5,7},{6,4},{7,5},{8,10},{9,11},{10,... | collective-permute-start | bytes 688136 | tf_op jit(solution)/shard_map/scatter/ppermute | solution.py:27
  123.7 8.2 %collective-permute-start.26 = (bf16[8,16,896]{2,1,0:T(8,128)(2,1)}, bf16[8,16,896]{2,1,0:T(8,128)(2,1)S(1)}, u32[]{:S(2)}, u32[]{:S(2)}) collective-permute-start(bf16[8,16,896]{2,1,0:T(8,128)(2,1)} %get-tuple-element.71), channel_id=1, source_target_pairs={{0,1},{1,2},{2,3},{3,0},{4,5},{5,6},{6,7},{7,4},{8,9},{9,10},{10,1... | collective-permute-start | bytes 688136 | tf_op jit(solution)/shard_map/scatter/ppermute | solution.py:27
  124.2 9.2 %collective-permute-start.27 = (bf16[8,16,896]{2,1,0:T(8,128)(2,1)}, bf16[8,16,896]{2,1,0:T(8,128)(2,1)S(1)}, u32[]{:S(2)}, u32[]{:S(2)}) collective-permute-start(bf16[8,16,896]{2,1,0:T(8,128)(2,1)} %get-tuple-element.73), channel_id=1, source_target_pairs={{0,12},{1,13},{2,14},{3,15},{4,0},{5,1},{6,2},{7,3},{8,4},{9,5},{1... | collective-permute-start | bytes 688136 | tf_op jit(solution)/shard_map/scatter/ppermute | solution.py:22
  127.0 7.8 %collective-permute-start.28 = (bf16[8,16,896]{2,1,0:T(8,128)(2,1)}, bf16[8,16,896]{2,1,0:T(8,128)(2,1)S(1)}, u32[]{:S(2)}, u32[]{:S(2)}) collective-permute-start(bf16[8,16,896]{2,1,0:T(8,128)(2,1)} %get-tuple-element.74), channel_id=1, source_target_pairs={{0,8},{1,9},{2,10},{3,11},{4,12},{5,13},{6,14},{7,15},{8,0},{9,1},... | collective-permute-start | bytes 688136 | tf_op jit(solution)/shard_map/scatter/ppermute | solution.py:22
  128.0 9.3 %collective-permute-start.29 = (bf16[8,16,896]{2,1,0:T(8,128)(2,1)}, bf16[8,16,896]{2,1,0:T(8,128)(2,1)S(1)}, u32[]{:S(2)}, u32[]{:S(2)}) collective-permute-start(bf16[8,16,896]{2,1,0:T(8,128)(2,1)} %get-tuple-element.75), channel_id=1, source_target_pairs={{0,4},{1,5},{2,6},{3,7},{4,8},{5,9},{6,10},{7,11},{8,12},{9,13},{1... | collective-permute-start | bytes 688136 | tf_op jit(solution)/shard_map/scatter/ppermute | solution.py:22
  142.4 5.8 %collective-permute-start.34 = (bf16[2,16,896]{2,1,0:T(8,128)(2,1)S(1)}, bf16[2,16,896]{2,1,0:T(8,128)(2,1)S(1)}, u32[]{:S(2)}, u32[]{:S(2)}) collective-permute-start(bf16[2,16,896]{2,1,0:T(8,128)(2,1)S(1)} %get-tuple-element.82), channel_id=1, source_target_pairs={{0,2},{1,3},{2,0},{3,1},{4,6},{5,7},{6,4},{7,5},{8,10},{9,11},{10,... | collective-permute-start | bytes 172040 | tf_op jit(solution)/shard_map/scatter/ppermute | solution.py:27
  142.4 6.0 %collective-permute-start.35 = (bf16[2,16,896]{2,1,0:T(8,128)(2,1)S(1)}, bf16[2,16,896]{2,1,0:T(8,128)(2,1)S(1)}, u32[]{:S(2)}, u32[]{:S(2)}) collective-permute-start(bf16[2,16,896]{2,1,0:T(8,128)(2,1)S(1)} %get-tuple-element.83), channel_id=1, source_target_pairs={{0,1},{1,2},{2,3},{3,0},{4,5},{5,6},{6,7},{7,4},{8,9},{9,10},{10,1... | collective-permute-start | bytes 172040 | tf_op jit(solution)/shard_map/scatter/ppermute | solution.py:27
  (17 other events, 340.9 us)
Sparse Core Ops, SparseCore 0:
  84.2 36.4 reduce-scatter.1
  122.5 26.2 all-gather.1

commit v5 on v4

--- a/solution.py
+++ b/solution.py
@@ -268,6 +268,14 @@
     for copy in arrivals:
         copy.start()
     copies = []
+    own, x, y = place()
+    sums[...] = jnp.zeros_like(sums)
+    for r, tile in enumerate(my_slots(owner, slot, own)):
+        for k in range(SIDE):
+            sums[tile, sub_row(x + k, 0), :] += in_a[k][r].astype(F32)
+            sums[tile, sub_row(y + k, SIDE * SUB), :] += in_b[k][r].astype(F32)
+    copies.append(pltpu.make_async_copy(sums, out_t, leave_t))
+    copies[-1].start()
     for i in range(count):
         z, core = i // 2, i % 2
         out_e = out_v if core else out_k
@@ -285,14 +293,6 @@
         ]
         copies[-2].start()
         copies[-1].start()
-    own, x, y = place()
-    sums[...] = jnp.zeros_like(sums)
-    for r, tile in enumerate(my_slots(owner, slot, own)):
-        for k in range(SIDE):
-            sums[tile, sub_row(x + k, 0), :] += in_a[k][r].astype(F32)
-            sums[tile, sub_row(y + k, SIDE * SUB), :] += in_b[k][r].astype(F32)
-    copies.append(pltpu.make_async_copy(sums, out_t, leave_t))
-    copies[-1].start()
     for copy in copies:
         copy.wait()
 

time: 162 us -> 162 us (level)
  no operation moved by 1% of the time
where the time goes in v5:
time: 162 us; the launch traced here: 161 us
  waiting for transfers between devices  73.4 us (45%)
  starting transfers between devices  42.7 us (26%)
  Pallas kernels  26.2 us (16%)
  between operations  14.2 us (9%)
  matrix products  3.43 us (2%)
    ppermute x18, waiting for transfers between devices, along_x(): return lax.ppermute(value, 'enc', pairs)  38.5 us
    ppermute x18, waiting for transfers between devices, along_y(): return lax.ppermute(value, 'enc', pairs)  33.5 us
    ppermute x18, starting transfers between devices, along_x(): return lax.ppermute(value, 'enc', pairs)  25.5 us
    ppermute x18, starting transfers between devices, along_y(): return lax.ppermute(value, 'enc', pairs)  17.1 us
    pallas_call x1, Pallas kernels, attend(): pl.pallas_call(attention_kernel, grid_spec=pltpu.PrefetchScalarGridSpec(n...  13.6 us
    pallas_call x3, Pallas kernels, call(): pl.pallas_call(kernel, out_shape=[jax.ShapeDtypeStruct(*out) if kept is N...  5.49 us
    pallas_call x1, Pallas kernels, last_outputs(): pl.pallas_call(last_kernel, out_shape=[jax.ShapeDtypeStruct(shape, F32) f...  5.14 us
    dot_general x1, matrix products, body(): jnp.dot(queries_in, w_query, preferred_element_type=F32).astype(BF16)  3.43 us
  transfers between devices with their start and end apart: 38, of which 27 were waited for; matrix products, arithmetic and copies ran while one was open for 2% of the time, Pallas kernels for 2%

profile of v5, /device:TPU:0, one launch (start us, length us, event | category | flops | bytes accessed | tf_op | source)
XLA Modules:
  0.0 160.8 jit_solution(17141571016292348562)
XLA Ops:
  7.2 2.0 %gather.2 = (bf16[2,16,896]{2,1,0:T(8,128)(2,1)S(1)}, bf16[2,16,896]{2,1,0:T(8,128)(2,1)S(1)}, bf16[2,16,896]{2,1,0:T(8,128)(2,1)S(1)}, bf16[2,16,896]{2,1,0:T(8...) custom-call(s32[2,8]{1,0:T(2,128)} %bitcast.5, ...), custom_call_target="tpu_custom_call" | custom-call | tf_op jit(solution)/shard_map/gather/pallas_call | solution.py:322
  9.3 1.6 %collective-permute-start = (bf16[2,16,896]{2,1,0:T(8,128)(2,1)S(1)}, bf16[2,16,896]{2,1,0:T(8,128)(2,1)S(1)}, u32[]{:S(2)}, u32[]{:S(2)}) collective-permute-start(bf16[2,16,896]{2,1,0:T(8,128)(2,1)S(1)} %get-tuple-element.48), channel_id=1, source_target_pairs={{0,4},{1,5},{2,6},{3,7},{4,8},{5,9},{6,10},{7,11},{8,12},{9,13},{1... | collective-permute-start | bytes 172040 | tf_op jit(solution)/shard_map/gather/ppermute | solution.py:22
  10.9 2.7 %collective-permute-start.1 = (bf16[2,16,896]{2,1,0:T(8,128)(2,1)S(1)}, bf16[2,16,896]{2,1,0:T(8,128)(2,1)S(1)}, u32[]{:S(2)}, u32[]{:S(2)}) collective-permute-start(bf16[2,16,896]{2,1,0:T(8,128)(2,1)S(1)} %get-tuple-element.49), channel_id=1, source_target_pairs={{0,8},{1,9},{2,10},{3,11},{4,12},{5,13},{6,14},{7,15},{8,0},{9,1},... | collective-permute-start | bytes 172040 | tf_op jit(solution)/shard_map/gather/ppermute | solution.py:22
  15.1 1.6 collective-permute-start.6
  16.7 2.9 %collective-permute-start.7 = (bf16[2,16,896]{2,1,0:T(8,128)(2,1)S(1)}, bf16[2,16,896]{2,1,0:T(8,128)(2,1)S(1)}, u32[]{:S(2)}, u32[]{:S(2)}) collective-permute-start(bf16[2,16,896]{2,1,0:T(8,128)(2,1)S(1)} %get-tuple-element.53), channel_id=1, source_target_pairs={{0,2},{1,3},{2,0},{3,1},{4,6},{5,7},{6,4},{7,5},{8,10},{9,11},{10,... | collective-permute-start | bytes 172040 | tf_op jit(solution)/shard_map/gather/ppermute | solution.py:27
  22.3 2.8 %collective-permute-done.8 = bf16[2,16,896]{2,1,0:T(8,128)(2,1)S(1)} collective-permute-done((bf16[2,16,896]{2,1,0:T(8,128)(2,1)S(1)}, bf16[2,16,896]{2,1,0:T(8,128)(2,1)S(1)}, u32[]{:S(2)}, u32[]{:S(2)}) %collective-permute-start.8) | collective-permute-done | bytes 57376 | tf_op jit(solution)/shard_map/gather/ppermute | solution.py:27
  25.3 2.5 %collective-permute-start.10 = (bf16[8,16,896]{2,1,0:T(8,128)(2,1)S(1)}, bf16[8,16,896]{2,1,0:T(8,128)(2,1)S(1)}, u32[]{:S(2)}, u32[]{:S(2)}) collective-permute-start(bf16[8,16,896]{2,1,0:T(8,128)(2,1)S(1)} %constant_dynamic-update-slice_fusion.4.refs_4_), channel_id=1, source_target_pairs={{0,8},{1,9},{2,10},{3,11},{4,12},{5,13},{6,14},{7,15},{8,0},{9,1},... | collective-permute-start | bytes 688136 | tf_op jit(solution)/shard_map/gather/ppermute | solution.py:22
  28.0 2.6 %collective-permute-start.5 = (bf16[8,16,896]{2,1,0:T(8,128)(2,1)S(1)}, bf16[8,16,896]{2,1,0:T(8,128)(2,1)S(1)}, u32[]{:S(2)}, u32[]{:S(2)}) collective-permute-start(bf16[8,16,896]{2,1,0:T(8,128)(2,1)S(1)} %constant_dynamic-update-slice_fusion.refs_0_), channel_id=1, source_target_pairs={{0,3},{1,0},{2,1},{3,2},{4,7},{5,4},{6,5},{7,6},{8,11},{9,8},{10,9... | collective-permute-start | bytes 688136 | tf_op jit(solution)/shard_map/gather/ppermute | solution.py:27
  30.5 1.6 collective-permute-done.11.refs_7_
  32.2 1.6 %collective-permute-done.10.refs_6_ = bf16[8,16,896]{2,1,0:T(8,128)(2,1)S(1)} collective-permute-done((bf16[8,16,896]{2,1,0:T(8,128)(2,1)S(1)}, bf16[8,16,896]{2,1,0:T(8,128)(2,1)S(1)}, u32[]{:S(2)}, u32[]{:S(2)}) %collective-permute-start.10) | collective-permute-done | bytes 229408 | tf_op jit(solution)/shard_map/gather/ppermute | solution.py:22
  33.8 2.4 %collective-permute-done.9.refs_5_ = bf16[8,16,896]{2,1,0:T(8,128)(2,1)S(1)} collective-permute-done((bf16[8,16,896]{2,1,0:T(8,128)(2,1)S(1)}, bf16[8,16,896]{2,1,0:T(8,128)(2,1)S(1)}, u32[]{:S(2)}, u32[]{:S(2)}) %collective-permute-start.9) | collective-permute-done | bytes 229408 | tf_op jit(solution)/shard_map/gather/ppermute | solution.py:22
  38.4 2.4 %collective-permute-done.3.refs_1_ = bf16[8,16,896]{2,1,0:T(8,128)(2,1)S(1)} collective-permute-done((bf16[8,16,896]{2,1,0:T(8,128)(2,1)S(1)}, bf16[8,16,896]{2,1,0:T(8,128)(2,1)S(1)}, u32[]{:S(2)}, u32[]{:S(2)}) %collective-permute-start.3) | collective-permute-done | bytes 229408 | tf_op jit(solution)/shard_map/gather/ppermute | solution.py:27
  41.4 1.9 %gather.3 = (bf16[16,16,896]{2,1,0:T(8,128)(2,1)S(1)}, bf16[16,16,896]{2,1,0:T(8,128)(2,1)S(1)}) custom-call(s32[2,8]{1,0:T(2,128)S(1)} %bitcast.6, bf16[8,16,896]{2,1,0:T(8,128)(2,1)S(1)} %constant_dynamic-update-slice_fusion.refs_0_, bf16[8,16,896]{2,1,0:T(8,128)(2,1)S(1)} %collective-permute-done.3.refs_1_, ...), custom_call_target="tpu_custom_call" | custom-call | tf_op jit(solution)/shard_map/gather/pallas_call | solution.py:339
  43.3 3.1 %collective-permute-start.14 = (bf16[16,16,896]{2,1,0:T(8,128)(2,1)S(1)}, bf16[16,16,896]{2,1,0:T(8,128)(2,1)S(1)}, u32[]{:S(2)}, u32[]{:S(2)}) collective-permute-start(bf16[16,16,896]{2,1,0:T(8,128)(2,1)S(1)} %get-tuple-element.55.refs_0_), channel_id=1, source_target_pairs={{0,12},{1,13},{2,14},{3,15},{4,0},{5,1},{6,2},{7,3},{8,4},{9,5},{1... | collective-permute-start | bytes 1376264 | tf_op jit(solution)/shard_map/gather/ppermute | solution.py:22
  49.3 11.4 %collective-permute-done.14.refs_3_ = bf16[16,16,896]{2,1,0:T(8,128)(2,1)S(1)} collective-permute-done((bf16[16,16,896]{2,1,0:T(8,128)(2,1)S(1)}, bf16[16,16,896]{2,1,0:T(8,128)(2,1)S(1)}, u32[]{:S(2)}, u32[]{:S(2)}) %collective-permute-start.14) | collective-permute-done | bytes 458784 | tf_op jit(solution)/shard_map/gather/ppermute | solution.py:22
  60.7 3.4 %convolution_convert_fusion.refs_8_ = bf16[512,256]{1,0:T(8,128)(2,1)S(1)} fusion(bf16[512,4096]{1,0:T(8,128)(2,1)} %refs_11_.1, bf16[4096,256]{1,0:T(8,128)(2,1)S(1)} %copy-done), kind=kOutput, calls=%fused_computation | convolution fusion | flops 1073872896 | bytes 6553600 | tf_op jit(solution)/shard_map/dot_general | solution.py:417
  64.6 5.9 %collective-permute-done.15.refs_5_ = bf16[16,16,896]{2,1,0:T(8,128)(2,1)S(1)} collective-permute-done((bf16[16,16,896]{2,1,0:T(8,128)(2,1)S(1)}, bf16[16,16,896]{2,1,0:T(8,128)(2,1)S(1)}, u32[]{:S(2)}, u32[]{:S(2)}) %collective-permute-start.15) | collective-permute-done | bytes 458784 | tf_op jit(solution)/shard_map/gather/ppermute | solution.py:27
  70.4 13.6 %attend.1 = (bf16[512,256]{1,0:T(8,128)(2,1)}, bf16[16,16,896]{2,1,0:T(8,128)(2,1)}, bf16[16,16,896]{2,1,0:T(8,128)(2,1)}, bf16[16,16,896]{2,1,0:T(8,128)(2,1)},...) custom-call(s32[2,8]{1,0:T(2,128)S(1)} %bitcast.11, ...), custom_call_target="tpu_custom_call" | custom-call | tf_op jit(solution)/shard_map/attend/pallas_call | solution.py:359
  84.1 3.7 %collective-permute-start.18 = (bf16[16,16,896]{2,1,0:T(8,128)(2,1)}, bf16[16,16,896]{2,1,0:T(8,128)(2,1)S(1)}, u32[]{:S(2)}, u32[]{:S(2)}) collective-permute-start(bf16[16,16,896]{2,1,0:T(8,128)(2,1)} %get-tuple-element.59), channel_id=1, source_target_pairs={{0,12},{1,13},{2,14},{3,15},{4,0},{5,1},{6,2},{7,3},{8,4},{9,5},{1... | collective-permute-start | bytes 1376264 | tf_op jit(solution)/shard_map/scatter/ppermute | solution.py:22
  89.7 10.8 %collective-permute-done.18.refs_1_ = bf16[16,16,896]{2,1,0:T(8,128)(2,1)S(1)} collective-permute-done((bf16[16,16,896]{2,1,0:T(8,128)(2,1)}, bf16[16,16,896]{2,1,0:T(8,128)(2,1)S(1)}, u32[]{:S(2)}, u32[]{:S(2)}) %collective-permute-start.18) | collective-permute-done | bytes 458784 | tf_op jit(solution)/shard_map/scatter/ppermute | solution.py:22
  100.5 3.3 %collective-permute-done.20.refs_3_ = bf16[16,16,896]{2,1,0:T(8,128)(2,1)S(1)} collective-permute-done((bf16[16,16,896]{2,1,0:T(8,128)(2,1)}, bf16[16,16,896]{2,1,0:T(8,128)(2,1)S(1)}, u32[]{:S(2)}, u32[]{:S(2)}) %collective-permute-start.20) | collective-permute-done | bytes 458784 | tf_op jit(solution)/shard_map/scatter/ppermute | solution.py:22
  103.8 6.4 %collective-permute-done.23.refs_7_ = bf16[16,16,896]{2,1,0:T(8,128)(2,1)S(1)} collective-permute-done((bf16[16,16,896]{2,1,0:T(8,128)(2,1)S(1)}, bf16[16,16,896]{2,1,0:T(8,128)(2,1)S(1)}, u32[]{:S(2)}, u32[]{:S(2)}) %collective-permute-start.23) | collective-permute-done | bytes 458784 | tf_op jit(solution)/shard_map/scatter/ppermute | solution.py:27
  110.2 3.3 %scatter.3 = (bf16[8,16,896]{2,1,0:T(8,128)(2,1)S(1)}, bf16[8,16,896]{2,1,0:T(8,128)(2,1)}, bf16[8,16,896]{2,1,0:T(8,128)(2,1)}, bf16[8,16,896]{2,1,0:T(8,128)(2...) custom-call(s32[2,8]{1,0:T(2,128)S(1)} %bitcast.7, ...), custom_call_target="tpu_custom_call" | custom-call | tf_op jit(solution)/shard_map/scatter/pallas_call | solution.py:339
  113.8 5.9 %collective-permute-done.24.refs_1_ = bf16[8,16,896]{2,1,0:T(8,128)(2,1)S(1)} collective-permute-done((bf16[8,16,896]{2,1,0:T(8,128)(2,1)}, bf16[8,16,896]{2,1,0:T(8,128)(2,1)S(1)}, u32[]{:S(2)}, u32[]{:S(2)}) %collective-permute-start.24) | collective-permute-done | bytes 229408 | tf_op jit(solution)/shard_map/scatter/ppermute | solution.py:27
  120.7 2.9 %collective-permute-start.25 = (bf16[8,16,896]{2,1,0:T(8,128)(2,1)}, bf16[8,16,896]{2,1,0:T(8,128)(2,1)S(1)}, u32[]{:S(2)}, u32[]{:S(2)}) collective-permute-start(bf16[8,16,896]{2,1,0:T(8,128)(2,1)} %get-tuple-element.70), channel_id=1, source_target_pairs={{0,2},{1,3},{2,0},{3,1},{4,6},{5,7},{6,4},{7,5},{8,10},{9,11},{10,... | collective-permute-start | bytes 688136 | tf_op jit(solution)/shard_map/scatter/ppermute | solution.py:27
  124.2 2.7 %collective-permute-start.27 = (bf16[8,16,896]{2,1,0:T(8,128)(2,1)}, bf16[8,16,896]{2,1,0:T(8,128)(2,1)S(1)}, u32[]{:S(2)}, u32[]{:S(2)}) collective-permute-start(bf16[8,16,896]{2,1,0:T(8,128)(2,1)} %get-tuple-element.73), channel_id=1, source_target_pairs={{0,12},{1,13},{2,14},{3,15},{4,0},{5,1},{6,2},{7,3},{8,4},{9,5},{1... | collective-permute-start | bytes 688136 | tf_op jit(solution)/shard_map/scatter/ppermute | solution.py:22
  129.5 2.4 %collective-permute-done.26.refs_3_ = bf16[8,16,896]{2,1,0:T(8,128)(2,1)S(1)} collective-permute-done((bf16[8,16,896]{2,1,0:T(8,128)(2,1)}, bf16[8,16,896]{2,1,0:T(8,128)(2,1)S(1)}, u32[]{:S(2)}, u32[]{:S(2)}) %collective-permute-start.26) | collective-permute-done | bytes 229408 | tf_op jit(solution)/shard_map/scatter/ppermute | solution.py:27
  131.9 1.5 collective-permute-done.27.refs_5_
  134.8 2.5 %collective-permute-done.29.refs_7_ = bf16[8,16,896]{2,1,0:T(8,128)(2,1)S(1)} collective-permute-done((bf16[8,16,896]{2,1,0:T(8,128)(2,1)}, bf16[8,16,896]{2,1,0:T(8,128)(2,1)S(1)}, u32[]{:S(2)}, u32[]{:S(2)}) %collective-permute-start.29) | collective-permute-done | bytes 229408 | tf_op jit(solution)/shard_map/scatter/ppermute | solution.py:22
  140.4 2.1 %collective-permute-start.33 = (bf16[2,16,896]{2,1,0:T(8,128)(2,1)S(1)}, bf16[2,16,896]{2,1,0:T(8,128)(2,1)S(1)}, u32[]{:S(2)}, u32[]{:S(2)}) collective-permute-start(bf16[2,16,896]{2,1,0:T(8,128)(2,1)S(1)} %get-tuple-element.81), channel_id=1, source_target_pairs={{0,3},{1,0},{2,1},{3,2},{4,7},{5,4},{6,5},{7,6},{8,11},{9,8},{10,9... | collective-permute-start | bytes 172040 | tf_op jit(solution)/shard_map/scatter/ppermute | solution.py:27
  144.9 3.3 %collective-permute-done.34.refs_6_ = bf16[2,16,896]{2,1,0:T(8,128)(2,1)S(1)} collective-permute-done((bf16[2,16,896]{2,1,0:T(8,128)(2,1)S(1)}, bf16[2,16,896]{2,1,0:T(8,128)(2,1)S(1)}, u32[]{:S(2)}, u32[]{:S(2)}) %collective-permute-start.34) | collective-permute-done | bytes 57376 | tf_op jit(solution)/shard_map/scatter/ppermute | solution.py:27
  148.8 5.1 %scatter.5 = (f32[4096,256]{1,0:T(8,128)}, f32[896,256]{1,0:T(8,128)}, f32[896,256]{1,0:T(8,128)}, f32[4,128,896]{2,1,0:T(8,128)}) custom-call(s32[2,8]{1,0:T(2,128)S(1)} %bitcast.8, s32[2,8]{1,0:T(2,128)S(1)} %bitcast.10, bf16[2,16,896]{2,1,0:T(8,128)(2,1)S(1)} %get-tuple-element.76.refs_0_, bf16[2,16,896]{2,1,0:T(8,128)(2,1)S(1)} %collective-permute-done.30.refs_1_, ...), custom_call_target="tpu_custom_call" | custom-call | tf_op jit(solution)/shard_map/scatter/pallas_call | solution.py:301
  (84 shorter events, 24.5 us)
Async XLA Ops:
  7.2 113.5 %reduce-scatter.2.cloned.1.call-start = ((), (), s32[]{:S(2)}) async-start(), calls=%async_computation.1 | async-start | bytes 3391488 | tf_op jit(solution)/shard_map/weights/reduce_scatter | solution.py:427
  9.3 18.6 %collective-permute-start = (bf16[2,16,896]{2,1,0:T(8,128)(2,1)S(1)}, bf16[2,16,896]{2,1,0:T(8,128)(2,1)S(1)}, u32[]{:S(2)}, u32[]{:S(2)}) collective-permute-start(bf16[2,16,896]{2,1,0:T(8,128)(2,1)S(1)} %get-tuple-element.48), channel_id=1, source_target_pairs={{0,4},{1,5},{2,6},{3,7},{4,8},{5,9},{6,10},{7,11},{8,12},{9,13},{1... | collective-permute-start | bytes 172040 | tf_op jit(solution)/shard_map/gather/ppermute | solution.py:22
  10.9 17.0 %collective-permute-start.1 = (bf16[2,16,896]{2,1,0:T(8,128)(2,1)S(1)}, bf16[2,16,896]{2,1,0:T(8,128)(2,1)S(1)}, u32[]{:S(2)}, u32[]{:S(2)}) collective-permute-start(bf16[2,16,896]{2,1,0:T(8,128)(2,1)S(1)} %get-tuple-element.49), channel_id=1, source_target_pairs={{0,8},{1,9},{2,10},{3,11},{4,12},{5,13},{6,14},{7,15},{8,0},{9,1},... | collective-permute-start | bytes 172040 | tf_op jit(solution)/shard_map/gather/ppermute | solution.py:22
  13.6 14.3 %collective-permute-start.2 = (bf16[2,16,896]{2,1,0:T(8,128)(2,1)S(1)}, bf16[2,16,896]{2,1,0:T(8,128)(2,1)S(1)}, u32[]{:S(2)}, u32[]{:S(2)}) collective-permute-start(bf16[2,16,896]{2,1,0:T(8,128)(2,1)S(1)} %get-tuple-element.50), channel_id=1, source_target_pairs={{0,12},{1,13},{2,14},{3,15},{4,0},{5,1},{6,2},{7,3},{8,4},{9,5},{1... | collective-permute-start | bytes 172040 | tf_op jit(solution)/shard_map/gather/ppermute | solution.py:22
  15.1 5.9 %collective-permute-start.6 = (bf16[2,16,896]{2,1,0:T(8,128)(2,1)S(1)}, bf16[2,16,896]{2,1,0:T(8,128)(2,1)S(1)}, u32[]{:S(2)}, u32[]{:S(2)}) collective-permute-start(bf16[2,16,896]{2,1,0:T(8,128)(2,1)S(1)} %get-tuple-element.52), channel_id=1, source_target_pairs={{0,1},{1,2},{2,3},{3,0},{4,5},{5,6},{6,7},{7,4},{8,9},{9,10},{10,1... | collective-permute-start | bytes 172040 | tf_op jit(solution)/shard_map/gather/ppermute | solution.py:27
  25.2 7.0 %collective-permute-start.11 = (bf16[8,16,896]{2,1,0:T(8,128)(2,1)S(1)}, bf16[8,16,896]{2,1,0:T(8,128)(2,1)S(1)}, u32[]{:S(2)}, u32[]{:S(2)}) collective-permute-start(bf16[8,16,896]{2,1,0:T(8,128)(2,1)S(1)} %constant_dynamic-update-slice_fusion.4.refs_4_), channel_id=1, source_target_pairs={{0,12},{1,13},{2,14},{3,15},{4,0},{5,1},{6,2},{7,3},{8,4},{9,5},{1... | collective-permute-start | bytes 688136 | tf_op jit(solution)/shard_map/gather/ppermute | solution.py:22
  25.3 8.5 %collective-permute-start.10 = (bf16[8,16,896]{2,1,0:T(8,128)(2,1)S(1)}, bf16[8,16,896]{2,1,0:T(8,128)(2,1)S(1)}, u32[]{:S(2)}, u32[]{:S(2)}) collective-permute-start(bf16[8,16,896]{2,1,0:T(8,128)(2,1)S(1)} %constant_dynamic-update-slice_fusion.4.refs_4_), channel_id=1, source_target_pairs={{0,8},{1,9},{2,10},{3,11},{4,12},{5,13},{6,14},{7,15},{8,0},{9,1},... | collective-permute-start | bytes 688136 | tf_op jit(solution)/shard_map/gather/ppermute | solution.py:22
  27.9 8.3 %collective-permute-start.9 = (bf16[8,16,896]{2,1,0:T(8,128)(2,1)S(1)}, bf16[8,16,896]{2,1,0:T(8,128)(2,1)S(1)}, u32[]{:S(2)}, u32[]{:S(2)}) collective-permute-start(bf16[8,16,896]{2,1,0:T(8,128)(2,1)S(1)} %constant_dynamic-update-slice_fusion.4.refs_4_), channel_id=1, source_target_pairs={{0,4},{1,5},{2,6},{3,7},{4,8},{5,9},{6,10},{7,11},{8,12},{9,13},{1... | collective-permute-start | bytes 688136 | tf_op jit(solution)/shard_map/gather/ppermute | solution.py:22
  28.0 9.1 %collective-permute-start.5 = (bf16[8,16,896]{2,1,0:T(8,128)(2,1)S(1)}, bf16[8,16,896]{2,1,0:T(8,128)(2,1)S(1)}, u32[]{:S(2)}, u32[]{:S(2)}) collective-permute-start(bf16[8,16,896]{2,1,0:T(8,128)(2,1)S(1)} %constant_dynamic-update-slice_fusion.refs_0_), channel_id=1, source_target_pairs={{0,3},{1,0},{2,1},{3,2},{4,7},{5,4},{6,5},{7,6},{8,11},{9,8},{10,9... | collective-permute-start | bytes 688136 | tf_op jit(solution)/shard_map/gather/ppermute | solution.py:27
  30.5 7.8 %collective-permute-start.4 = (bf16[8,16,896]{2,1,0:T(8,128)(2,1)S(1)}, bf16[8,16,896]{2,1,0:T(8,128)(2,1)S(1)}, u32[]{:S(2)}, u32[]{:S(2)}) collective-permute-start(bf16[8,16,896]{2,1,0:T(8,128)(2,1)S(1)} %constant_dynamic-update-slice_fusion.refs_0_), channel_id=1, source_target_pairs={{0,2},{1,3},{2,0},{3,1},{4,6},{5,7},{6,4},{7,5},{8,10},{9,11},{10,... | collective-permute-start | bytes 688136 | tf_op jit(solution)/shard_map/gather/ppermute | solution.py:27
  32.1 8.6 %collective-permute-start.3 = (bf16[8,16,896]{2,1,0:T(8,128)(2,1)S(1)}, bf16[8,16,896]{2,1,0:T(8,128)(2,1)S(1)}, u32[]{:S(2)}, u32[]{:S(2)}) collective-permute-start(bf16[8,16,896]{2,1,0:T(8,128)(2,1)S(1)} %constant_dynamic-update-slice_fusion.refs_0_), channel_id=1, source_target_pairs={{0,1},{1,2},{2,3},{3,0},{4,5},{5,6},{6,7},{7,4},{8,9},{9,10},{10,1... | collective-permute-start | bytes 688136 | tf_op jit(solution)/shard_map/gather/ppermute | solution.py:27
  43.3 17.4 %collective-permute-start.14 = (bf16[16,16,896]{2,1,0:T(8,128)(2,1)S(1)}, bf16[16,16,896]{2,1,0:T(8,128)(2,1)S(1)}, u32[]{:S(2)}, u32[]{:S(2)}) collective-permute-start(bf16[16,16,896]{2,1,0:T(8,128)(2,1)S(1)} %get-tuple-element.55.refs_0_), channel_id=1, source_target_pairs={{0,12},{1,13},{2,14},{3,15},{4,0},{5,1},{6,2},{7,3},{8,4},{9,5},{1... | collective-permute-start | bytes 1376264 | tf_op jit(solution)/shard_map/gather/ppermute | solution.py:22
  46.5 17.7 %collective-permute-start.13 = (bf16[16,16,896]{2,1,0:T(8,128)(2,1)S(1)}, bf16[16,16,896]{2,1,0:T(8,128)(2,1)S(1)}, u32[]{:S(2)}, u32[]{:S(2)}) collective-permute-start(bf16[16,16,896]{2,1,0:T(8,128)(2,1)S(1)} %get-tuple-element.55.refs_0_), channel_id=1, source_target_pairs={{0,8},{1,9},{2,10},{3,11},{4,12},{5,13},{6,14},{7,15},{8,0},{9,1},... | collective-permute-start | bytes 1376264 | tf_op jit(solution)/shard_map/gather/ppermute | solution.py:22
  47.8 16.7 %collective-permute-start.12 = (bf16[16,16,896]{2,1,0:T(8,128)(2,1)S(1)}, bf16[16,16,896]{2,1,0:T(8,128)(2,1)S(1)}, u32[]{:S(2)}, u32[]{:S(2)}) collective-permute-start(bf16[16,16,896]{2,1,0:T(8,128)(2,1)S(1)} %get-tuple-element.55.refs_0_), channel_id=1, source_target_pairs={{0,4},{1,5},{2,6},{3,7},{4,8},{5,9},{6,10},{7,11},{8,12},{9,13},{1... | collective-permute-start | bytes 1376264 | tf_op jit(solution)/shard_map/gather/ppermute | solution.py:22
  48.3 16.3 %collective-permute-start.17 = (bf16[16,16,896]{2,1,0:T(8,128)(2,1)S(1)}, bf16[16,16,896]{2,1,0:T(8,128)(2,1)S(1)}, u32[]{:S(2)}, u32[]{:S(2)}) collective-permute-start(bf16[16,16,896]{2,1,0:T(8,128)(2,1)S(1)} %get-tuple-element.56.refs_4_), channel_id=1, source_target_pairs={{0,3},{1,0},{2,1},{3,2},{4,7},{5,4},{6,5},{7,6},{8,11},{9,8},{10,9... | collective-permute-start | bytes 1376264 | tf_op jit(solution)/shard_map/gather/ppermute | solution.py:27
  49.3 15.2 %collective-permute-start.16 = (bf16[16,16,896]{2,1,0:T(8,128)(2,1)S(1)}, bf16[16,16,896]{2,1,0:T(8,128)(2,1)S(1)}, u32[]{:S(2)}, u32[]{:S(2)}) collective-permute-start(bf16[16,16,896]{2,1,0:T(8,128)(2,1)S(1)} %get-tuple-element.56.refs_4_), channel_id=1, source_target_pairs={{0,2},{1,3},{2,0},{3,1},{4,6},{5,7},{6,4},{7,5},{8,10},{9,11},{10,... | collective-permute-start | bytes 1376264 | tf_op jit(solution)/shard_map/gather/ppermute | solution.py:27
  60.7 9.7 %collective-permute-start.15 = (bf16[16,16,896]{2,1,0:T(8,128)(2,1)S(1)}, bf16[16,16,896]{2,1,0:T(8,128)(2,1)S(1)}, u32[]{:S(2)}, u32[]{:S(2)}) collective-permute-start(bf16[16,16,896]{2,1,0:T(8,128)(2,1)S(1)} %get-tuple-element.56.refs_4_), channel_id=1, source_target_pairs={{0,1},{1,2},{2,3},{3,0},{4,5},{5,6},{6,7},{7,4},{8,9},{9,10},{10,1... | collective-permute-start | bytes 1376264 | tf_op jit(solution)/shard_map/gather/ppermute | solution.py:27
  84.1 64.7 %all-gather.2.cloned.1.call-start = ((), (), s32[]{:S(2)}) async-start(), calls=%async_computation.2 | async-start | bytes 3391488 | tf_op jit(solution)/shard_map/weights/all_gather | solution.py:435
  84.1 16.4 %collective-permute-start.18 = (bf16[16,16,896]{2,1,0:T(8,128)(2,1)}, bf16[16,16,896]{2,1,0:T(8,128)(2,1)S(1)}, u32[]{:S(2)}, u32[]{:S(2)}) collective-permute-start(bf16[16,16,896]{2,1,0:T(8,128)(2,1)} %get-tuple-element.59), channel_id=1, source_target_pairs={{0,12},{1,13},{2,14},{3,15},{4,0},{5,1},{6,2},{7,3},{8,4},{9,5},{1... | collective-permute-start | bytes 1376264 | tf_op jit(solution)/shard_map/scatter/ppermute | solution.py:22
  87.8 12.7 %collective-permute-start.19 = (bf16[16,16,896]{2,1,0:T(8,128)(2,1)}, bf16[16,16,896]{2,1,0:T(8,128)(2,1)S(1)}, u32[]{:S(2)}, u32[]{:S(2)}) collective-permute-start(bf16[16,16,896]{2,1,0:T(8,128)(2,1)} %get-tuple-element.60), channel_id=1, source_target_pairs={{0,8},{1,9},{2,10},{3,11},{4,12},{5,13},{6,14},{7,15},{8,0},{9,1},... | collective-permute-start | bytes 1376264 | tf_op jit(solution)/shard_map/scatter/ppermute | solution.py:22
  87.8 15.9 %collective-permute-start.20 = (bf16[16,16,896]{2,1,0:T(8,128)(2,1)}, bf16[16,16,896]{2,1,0:T(8,128)(2,1)S(1)}, u32[]{:S(2)}, u32[]{:S(2)}) collective-permute-start(bf16[16,16,896]{2,1,0:T(8,128)(2,1)} %get-tuple-element.61), channel_id=1, source_target_pairs={{0,4},{1,5},{2,6},{3,7},{4,8},{5,9},{6,10},{7,11},{8,12},{9,13},{1... | collective-permute-start | bytes 1376264 | tf_op jit(solution)/shard_map/scatter/ppermute | solution.py:22
  88.8 15.0 %collective-permute-start.21 = (bf16[16,16,896]{2,1,0:T(8,128)(2,1)}, bf16[16,16,896]{2,1,0:T(8,128)(2,1)S(1)}, u32[]{:S(2)}, u32[]{:S(2)}) collective-permute-start(bf16[16,16,896]{2,1,0:T(8,128)(2,1)} %get-tuple-element.63), channel_id=1, source_target_pairs={{0,3},{1,0},{2,1},{3,2},{4,7},{5,4},{6,5},{7,6},{8,11},{9,8},{10,9... | collective-permute-start | bytes 1376264 | tf_op jit(solution)/shard_map/scatter/ppermute | solution.py:27
  88.8 15.0 %collective-permute-start.22 = (bf16[16,16,896]{2,1,0:T(8,128)(2,1)}, bf16[16,16,896]{2,1,0:T(8,128)(2,1)S(1)}, u32[]{:S(2)}, u32[]{:S(2)}) collective-permute-start(bf16[16,16,896]{2,1,0:T(8,128)(2,1)} %get-tuple-element.64), channel_id=1, source_target_pairs={{0,2},{1,3},{2,0},{3,1},{4,6},{5,7},{6,4},{7,5},{8,10},{9,11},{10,... | collective-permute-start | bytes 1376264 | tf_op jit(solution)/shard_map/scatter/ppermute | solution.py:27
  100.5 9.7 %collective-permute-start.23 = (bf16[16,16,896]{2,1,0:T(8,128)(2,1)S(1)}, bf16[16,16,896]{2,1,0:T(8,128)(2,1)S(1)}, u32[]{:S(2)}, u32[]{:S(2)}) collective-permute-start(bf16[16,16,896]{2,1,0:T(8,128)(2,1)S(1)} %copy-done.10), channel_id=1, source_target_pairs={{0,1},{1,2},{2,3},{3,0},{4,5},{5,6},{6,7},{7,4},{8,9},{9,10},{10,1... | collective-permute-start | bytes 1376264 | tf_op jit(solution)/shard_map/scatter/ppermute | solution.py:27
  113.6 6.2 %collective-permute-start.24 = (bf16[8,16,896]{2,1,0:T(8,128)(2,1)}, bf16[8,16,896]{2,1,0:T(8,128)(2,1)S(1)}, u32[]{:S(2)}, u32[]{:S(2)}) collective-permute-start(bf16[8,16,896]{2,1,0:T(8,128)(2,1)} %get-tuple-element.68), channel_id=1, source_target_pairs={{0,3},{1,0},{2,1},{3,2},{4,7},{5,4},{6,5},{7,6},{8,11},{9,8},{10,9... | collective-permute-start | bytes 688136 | tf_op jit(solution)/shard_map/scatter/ppermute | solution.py:27
  120.7 8.7 %collective-permute-start.25 = (bf16[8,16,896]{2,1,0:T(8,128)(2,1)}, bf16[8,16,896]{2,1,0:T(8,128)(2,1)S(1)}, u32[]{:S(2)}, u32[]{:S(2)}) collective-permute-start(bf16[8,16,896]{2,1,0:T(8,128)(2,1)} %get-tuple-element.70), channel_id=1, source_target_pairs={{0,2},{1,3},{2,0},{3,1},{4,6},{5,7},{6,4},{7,5},{8,10},{9,11},{10,... | collective-permute-start | bytes 688136 | tf_op jit(solution)/shard_map/scatter/ppermute | solution.py:27
  123.7 8.2 %collective-permute-start.26 = (bf16[8,16,896]{2,1,0:T(8,128)(2,1)}, bf16[8,16,896]{2,1,0:T(8,128)(2,1)S(1)}, u32[]{:S(2)}, u32[]{:S(2)}) collective-permute-start(bf16[8,16,896]{2,1,0:T(8,128)(2,1)} %get-tuple-element.71), channel_id=1, source_target_pairs={{0,1},{1,2},{2,3},{3,0},{4,5},{5,6},{6,7},{7,4},{8,9},{9,10},{10,1... | collective-permute-start | bytes 688136 | tf_op jit(solution)/shard_map/scatter/ppermute | solution.py:27
  124.2 9.2 %collective-permute-start.27 = (bf16[8,16,896]{2,1,0:T(8,128)(2,1)}, bf16[8,16,896]{2,1,0:T(8,128)(2,1)S(1)}, u32[]{:S(2)}, u32[]{:S(2)}) collective-permute-start(bf16[8,16,896]{2,1,0:T(8,128)(2,1)} %get-tuple-element.73), channel_id=1, source_target_pairs={{0,12},{1,13},{2,14},{3,15},{4,0},{5,1},{6,2},{7,3},{8,4},{9,5},{1... | collective-permute-start | bytes 688136 | tf_op jit(solution)/shard_map/scatter/ppermute | solution.py:22
  127.0 7.8 %collective-permute-start.28 = (bf16[8,16,896]{2,1,0:T(8,128)(2,1)}, bf16[8,16,896]{2,1,0:T(8,128)(2,1)S(1)}, u32[]{:S(2)}, u32[]{:S(2)}) collective-permute-start(bf16[8,16,896]{2,1,0:T(8,128)(2,1)} %get-tuple-element.74), channel_id=1, source_target_pairs={{0,8},{1,9},{2,10},{3,11},{4,12},{5,13},{6,14},{7,15},{8,0},{9,1},... | collective-permute-start | bytes 688136 | tf_op jit(solution)/shard_map/scatter/ppermute | solution.py:22
  128.0 9.3 %collective-permute-start.29 = (bf16[8,16,896]{2,1,0:T(8,128)(2,1)}, bf16[8,16,896]{2,1,0:T(8,128)(2,1)S(1)}, u32[]{:S(2)}, u32[]{:S(2)}) collective-permute-start(bf16[8,16,896]{2,1,0:T(8,128)(2,1)} %get-tuple-element.75), channel_id=1, source_target_pairs={{0,4},{1,5},{2,6},{3,7},{4,8},{5,9},{6,10},{7,11},{8,12},{9,13},{1... | collective-permute-start | bytes 688136 | tf_op jit(solution)/shard_map/scatter/ppermute | solution.py:22
  142.4 5.8 %collective-permute-start.34 = (bf16[2,16,896]{2,1,0:T(8,128)(2,1)S(1)}, bf16[2,16,896]{2,1,0:T(8,128)(2,1)S(1)}, u32[]{:S(2)}, u32[]{:S(2)}) collective-permute-start(bf16[2,16,896]{2,1,0:T(8,128)(2,1)S(1)} %get-tuple-element.82), channel_id=1, source_target_pairs={{0,2},{1,3},{2,0},{3,1},{4,6},{5,7},{6,4},{7,5},{8,10},{9,11},{10,... | collective-permute-start | bytes 172040 | tf_op jit(solution)/shard_map/scatter/ppermute | solution.py:27
  142.4 6.0 %collective-permute-start.35 = (bf16[2,16,896]{2,1,0:T(8,128)(2,1)S(1)}, bf16[2,16,896]{2,1,0:T(8,128)(2,1)S(1)}, u32[]{:S(2)}, u32[]{:S(2)}) collective-permute-start(bf16[2,16,896]{2,1,0:T(8,128)(2,1)S(1)} %get-tuple-element.83), channel_id=1, source_target_pairs={{0,1},{1,2},{2,3},{3,0},{4,5},{5,6},{6,7},{7,4},{8,9},{9,10},{10,1... | collective-permute-start | bytes 172040 | tf_op jit(solution)/shard_map/scatter/ppermute | solution.py:27
  (17 other events, 340.9 us)
Sparse Core Ops, SparseCore 0:
  84.2 36.4 reduce-scatter.1
  122.5 26.2 all-gather.1
